TPU v7x, 256 devices: a whole 4x4x8 slice. The times are simulated.
256 devices in a mesh: ka: 16 (over y_hi, x, core), fft: 16 (over y_lo, z).
Axes of the slice: x: 4, y: 4 (y_hi: 2, y_lo: 2; y = y_hi * 2 + y_lo), z: 8, core: 2. Of those that a mesh axis runs over, the one named last changes fastest.
Arguments:
- psi_val: bfloat16 [16, 2, 4, 442368], P('ka', None, None, 'fft'), may hold values from -6 to 6
- psi_cond: bfloat16 [16, 48, 9216, 128], P('ka', 'fft'), may hold values from -6 to 6
- e_val: float32 [16, 2], replicated, may hold values from -6 to -1
- e_cond: float32 [16, 32], replicated, may hold values from 1 to 8
- occ_val: int32 [16, 2], replicated, may hold values from 1 to 2
- occ_cond: int32 [16, 32], replicated, may hold values from 0 to 1
- umklapp: int32 [16], replicated, may hold values from -2 to 2
- sphere: int32 [4096], replicated, may hold values from 0 to 13823, as said below
Outputs:
- chi0: float32 [4096, 2, 4096], P('ka', None, 'fft')
Inputs may be any that keep to these rules, and one draw needn't show every extreme that they name: `sphere`: 4096 distinct indices of the box of 13824 frequencies.
All inputs are finite; a program needn't handle non-finite values.
Results may differ from a plain program's by a relative error of at most 0.02.
Values may be sent and summed in bfloat16 or wider, within the bound.
No kernel may reach another device: no remote copies, remote signals or barrier semaphores. Data moves between devices by JAX's collectives and lax.ppermute only.
A program may use at most 128 MiB of HBM per device.

v0:
```python
import math

import jax
import jax.numpy as jnp
from jax import lax
from jax.sharding import PartitionSpec as P

GRID = 96
BOX = 24
NG = 4096


def shifted(block, axis, distance):
    devices = range(lax.axis_size(axis))
    route = [((i - distance) % len(devices), i) for i in devices]
    return lax.ppermute(block, axis, route)


def phase_tables():
    kx_freq = jnp.arange(BOX, dtype=jnp.int32) - BOX // 2
    x_place = jnp.arange(GRID, dtype=jnp.int32)
    phase_turns = jnp.mod(kx_freq[:, None] * x_place[None, :], GRID).astype(jnp.float32)
    phase_angle = phase_turns * (2.0 * math.pi / GRID)
    return (jnp.cos(phase_angle).astype(jnp.bfloat16), jnp.sin(phase_angle).astype(jnp.bfloat16))


def complex_section(einsum_form, field_in, cosine, sine_table):
    with_cos = jnp.einsum(einsum_form, field_in, cosine, preferred_element_type=jnp.float32)
    with_sin = jnp.einsum(einsum_form, field_in, sine_table, preferred_element_type=jnp.float32)
    dims_out = with_cos.shape
    lane_count = dims_out[-1] // 4
    cos_split = with_cos.reshape(dims_out[:-1] + (2, 2, lane_count))
    sin_split = with_sin.reshape(dims_out[:-1] + (2, 2, lane_count))
    real_part = cos_split[..., 0, :] + sin_split[..., 1, :]
    imag_part = cos_split[..., 1, :] - sin_split[..., 0, :]
    return jnp.stack([real_part, imag_part], axis=-2).reshape(dims_out).astype(jnp.bfloat16)


def band_fields(val_band, conduction, cosine, sine_table):
    half_planes, points, lane_count = conduction.shape
    cond_parts = conduction.reshape(half_planes, points, 2, 2, lane_count // 4).astype(jnp.float32)
    val_parts = jnp.moveaxis(val_band.reshape(2, 2, half_planes, points), (0, 1), (2, 3)).astype(
        jnp.float32
    )
    val_real = val_parts[..., 0][..., None]
    val_imag = val_parts[..., 1][..., None]
    cond_real = cond_parts[..., 0, :]
    cond_imag = cond_parts[..., 1, :]
    pair_real = (val_real * cond_real + val_imag * cond_imag).astype(jnp.bfloat16)
    pair_imag = (val_real * cond_imag - val_imag * cond_real).astype(jnp.bfloat16)
    pair_field = jnp.stack([pair_real, pair_imag], axis=-2).reshape(
        half_planes, GRID, GRID, lane_count
    )
    z_field = complex_section("ayzl,fz->ayfl", pair_field, cosine, sine_table)
    return complex_section("ayfl,gy->agfl", z_field, cosine, sine_table)


def dot_last(left_side, right_side):
    return lax.dot_general(
        left_side, right_side, (((1,), (1,)), ((), ())), preferred_element_type=jnp.float32
    )


def turned(rho_block, groups):
    halves = rho_block.reshape(rho_block.shape[0], groups, 2, -1)
    return jnp.stack([-halves[:, :, 1], halves[:, :, 0]], axis=2).reshape(rho_block.shape)


def shards(psi_val, psi_cond, e_val, e_cond, occ_val, occ_cond, umklapp, sphere):
    count_k = lax.axis_size("ka")
    step_q = count_k // 4
    k_index = lax.axis_index("ka")
    x_block = lax.axis_index("fft")
    valence = psi_val[0]
    conduction = shifted(psi_cond, "ka", count_k - step_q)[0]
    k_pair = jnp.mod(k_index, count_k)
    cosine, sine_table = phase_tables()

    def one_band(val_band):
        return band_fields(val_band, conduction, cosine, sine_table)

    fields = lax.map(one_band, valence)
    band_count, half_planes = (fields.shape[0], fields.shape[1])
    lane_count = fields.shape[-1]
    cond_count = lane_count // 4
    columns = fields.reshape(band_count, half_planes, BOX * BOX, lane_count)
    offset = lax.dynamic_index_in_dim(umklapp, k_pair, keepdims=False)
    norm_scale = 1.0 / (GRID * math.sqrt(GRID))
    x_place = (
        2 * (x_block * half_planes + jnp.arange(half_planes, dtype=jnp.int32))[:, None]
        + jnp.arange(2, dtype=jnp.int32)[None, :]
    )
    kx_freq = sphere // (BOX * BOX) - BOX // 2 - offset
    column = sphere % (BOX * BOX)
    phase_turns = jnp.mod(kx_freq[:, None, None] * x_place[None], GRID).astype(jnp.float32)
    phase_angle = phase_turns * (2.0 * math.pi / GRID)
    cos_x = jnp.cos(phase_angle).astype(jnp.bfloat16)
    sin_x = jnp.sin(phase_angle).astype(jnp.bfloat16)
    picked = jnp.take(columns, column, axis=2).reshape(
        band_count,
        half_planes,
        lax.axis_size("fft") * (NG // lax.axis_size("fft")),
        2,
        2,
        cond_count,
    )
    picked_real = picked[..., 0, :]
    picked_imag = picked[..., 1, :]
    real_part = jnp.einsum(
        "gap,vagpc->gvc", cos_x, picked_real, preferred_element_type=jnp.float32
    ) + jnp.einsum("gap,vagpc->gvc", sin_x, picked_imag, preferred_element_type=jnp.float32)
    imag_part = jnp.einsum(
        "gap,vagpc->gvc", cos_x, picked_imag, preferred_element_type=jnp.float32
    ) - jnp.einsum("gap,vagpc->gvc", sin_x, picked_real, preferred_element_type=jnp.float32)
    rho_here = lax.psum_scatter(
        (jnp.stack([real_part, imag_part], axis=2) * norm_scale).reshape(
            lax.axis_size("fft") * (NG // lax.axis_size("fft")), band_count * 2 * cond_count
        ),
        "fft",
        scatter_dimension=0,
        tiled=True,
    ).astype(jnp.bfloat16)
    rho_all = lax.all_gather(rho_here, "fft", axis=0, tiled=True)
    k_cond = jnp.mod(k_pair + step_q, count_k)
    val_energy = lax.dynamic_index_in_dim(e_val, k_pair, keepdims=False)
    cond_energy = lax.dynamic_index_in_dim(e_cond, k_cond, keepdims=False)
    val_occ = lax.dynamic_index_in_dim(occ_val, k_pair, keepdims=False)
    cond_occ = lax.dynamic_index_in_dim(occ_cond, k_cond, keepdims=False)
    weight = (val_occ[:, None] - cond_occ[None, :]).astype(jnp.float32) / (
        (val_energy[:, None] - cond_energy[None, :]) * (count_k * val_energy.shape[0])
    )
    own_weight = jnp.broadcast_to(
        weight[:, None, :], (weight.shape[0], 2, weight.shape[1])
    ).reshape(-1)
    swapped = turned(rho_here, band_count)
    weighted = (rho_all.astype(jnp.float32) * own_weight).astype(jnp.bfloat16)
    real_part = dot_last(weighted, rho_here)
    imag_part = dot_last(weighted, swapped)
    return lax.psum_scatter(
        jnp.stack([real_part, imag_part], axis=1).astype(jnp.bfloat16),
        "ka",
        scatter_dimension=0,
        tiled=True,
    ).astype(jnp.float32)


def solution(mesh):
    placed = (P("ka", None, None, "fft"), P("ka", "fft", None, None), P(), P(), P(), P(), P(), P())
    return jax.shard_map(
        shards, mesh=mesh, in_specs=placed, out_specs=P("ka", None, "fft"), check_vma=False
    )
```

profile of v0, /device:TPU:62, one launch (start us, length us, event | category | flops | bytes accessed | tf_op | source)
XLA Modules:
  0.0 634.5 jit_solution(9968031530903670301)
XLA Ops:
  6.5 9.7 %copy.32 = bf16[1,3,9216,128]{2,3,1,0:T(8,128)(2,1)} copy(bf16[1,3,9216,128]{3,2,1,0:T(8,128)(2,1)} %param.11) | data formatting | bytes 14155776 | tf_op args[1]
  22.7 151.9 %collective-permute-done = bf16[1,3,9216,128]{2,3,1,0:T(8,128)(2,1)} collective-permute-done((bf16[1,3,9216,128]{2,3,1,0:T(8,128)(2,1)}, bf16[1,3,9216,128]{2,3,1,0:T(8,128)(2,1)}, u32[]{:S(2)}, u32[]{:S(2)}) %collective-permute-start) | collective-permute-done | bytes 7077920 | tf_op jit(solution)/shard_map/ppermute | solution.py:16
  174.6 154.0 %while.13 = (s32[]{:T(128)}, bf16[2,3,24,24,128]{4,3,2,1,0:T(8,128)(2,1)}, bf16[2,4,27648]{2,1,0:T(4,128)(2,1)}, bf16[1,3,9216,128]{2,3,1,0:T(8,128)(2,1)}, s32[24]{0:T(128)S(1)}, /*index=5*/s32[]{:T(128)}) while((s32[]{:T(128)}, bf16[2,3,24,24,128]{4,3,2,1,0:T(8,128)(2,1)}, bf16[2,4,27648]{2,1,0:T(4,128)(2,1)}, ...), condition=%wide.region_1.2_spmd.clone.clone.clone, body=%wide.region_0.1_spmd.clone.clone.clone.sunk | while | flops 450091008 | bytes 174957184 | solution.py:82
  176.5 4.7 convert.76
  185.3 6.6 %pad_maximum_fusion.8 = bf16[3,9216,2,2,32]{1,4,3,2,0:T(8,128)(2,1)} fusion(bf16[3,9216,2,1,32]{1,4,3,2,0:T(8,128)(2,1)} %get-tuple-element.168, bf16[3,9216,2,1,32]{1,4,3,2,0:T(8,128)(2,1)} %get-tuple-element.169), kind=kLoop, calls=%fused_computation.3.clone.1 | loop fusion | flops 3538944 | bytes 14155776 | tf_op jit(solution)/shard_map/while/body/eval_jaxpr/stack | solution.py:51
  192.0 14.4 %reshape.195 = bf16[3,96,96,128]{2,1,3,0:T(8,128)(2,1)} reshape(bf16[3,9216,2,2,32]{1,4,3,2,0:T(8,128)(2,1)} %pad_maximum_fusion.8) | data formatting | bytes 14155776 | tf_op jit(solution)/shard_map/while/body/eval_jaxpr/reshape | solution.py:51
  206.4 8.6 %convolution_bitcast_fusion.8 = f32[3,96,24,128]{1,2,3,0:T(8,128)S(1)} fusion(bf16[3,96,96,128]{2,1,3,0:T(8,128)(2,1)} %reshape.195, s32[24]{0:T(128)S(1)} %get-tuple-element.190), kind=kOutput, calls=%fused_computation.11.clone.1 | convolution fusion | flops 169892352 | bytes 10616928 | tf_op jit(solution)/shard_map/while/body/eval_jaxpr/ayzl,fz->ayfl/dot_general | solution.py:29
  216.2 5.9 convolution_bitcast_fusion.9
  232.3 5.5 reshape.197
  237.8 7.1 %fusion.71 = (bf16[3,24,24,2,1,32]{5,4,3,1,2,0:T(2,128)(2,1)S(1)}, bf16[3,24,24,2,1,32]{5,4,3,1,2,0:T(2,128)(2,1)S(1)}) fusion(f32[3,24,24,2,2,32]{5,4,3,1,2,0:T(2,128)S(1)} %copy-done.1, f32[3,24,24,2,2,32]{5,4,3,1,2,0:T(2,128)} %reshape.197), kind=kLoop, calls=%fused_computation.16.clone.1 | loop fusion | flops 442368 | bytes 2211840 | tf_op jit(solution)/shard_map/convert.3
  245.0 4.6 pad_maximum_fusion.10
  253.5 4.7 convert.76
  262.3 6.6 %pad_maximum_fusion.8 = bf16[3,9216,2,2,32]{1,4,3,2,0:T(8,128)(2,1)} fusion(bf16[3,9216,2,1,32]{1,4,3,2,0:T(8,128)(2,1)} %get-tuple-element.168, bf16[3,9216,2,1,32]{1,4,3,2,0:T(8,128)(2,1)} %get-tuple-element.169), kind=kLoop, calls=%fused_computation.3.clone.1 | loop fusion | flops 3538944 | bytes 14155776 | tf_op jit(solution)/shard_map/while/body/eval_jaxpr/stack | solution.py:51
  269.0 14.4 %reshape.195 = bf16[3,96,96,128]{2,1,3,0:T(8,128)(2,1)} reshape(bf16[3,9216,2,2,32]{1,4,3,2,0:T(8,128)(2,1)} %pad_maximum_fusion.8) | data formatting | bytes 14155776 | tf_op jit(solution)/shard_map/while/body/eval_jaxpr/reshape | solution.py:51
  283.4 8.6 %convolution_bitcast_fusion.8 = f32[3,96,24,128]{1,2,3,0:T(8,128)S(1)} fusion(bf16[3,96,96,128]{2,1,3,0:T(8,128)(2,1)} %reshape.195, s32[24]{0:T(128)S(1)} %get-tuple-element.190), kind=kOutput, calls=%fused_computation.11.clone.1 | convolution fusion | flops 169892352 | bytes 10616928 | tf_op jit(solution)/shard_map/while/body/eval_jaxpr/ayzl,fz->ayfl/dot_general | solution.py:29
  293.2 5.9 convolution_bitcast_fusion.9
  309.3 5.5 reshape.197
  314.8 7.1 %fusion.71 = (bf16[3,24,24,2,1,32]{5,4,3,1,2,0:T(2,128)(2,1)S(1)}, bf16[3,24,24,2,1,32]{5,4,3,1,2,0:T(2,128)(2,1)S(1)}) fusion(f32[3,24,24,2,2,32]{5,4,3,1,2,0:T(2,128)S(1)} %copy-done.1, f32[3,24,24,2,2,32]{5,4,3,1,2,0:T(2,128)} %reshape.197), kind=kLoop, calls=%fused_computation.16.clone.1 | loop fusion | flops 442368 | bytes 2211840 | tf_op jit(solution)/shard_map/convert.3
  322.0 4.6 pad_maximum_fusion.10
  330.7 40.1 %gather_fusion = bf16[4096,2,3,128]{3,1,2,0:T(2,128)(2,1)} fusion(bf16[2,3,576,128]{3,0,2,1:T(2,128)(2,1)S(1)} %copy.34, s32[4096]{0:T(1024)} %get-tuple-element.123), kind=kCustom, calls=%fused_computation | custom fusion | bytes 12599296 | tf_op jit(solution)/shard_map/jit(_take)/gather | solution.py:99
  370.8 16.2 %copy.35 = bf16[2,3,4096,128]{2,3,1,0:T(8,128)(2,1)} copy(bf16[2,3,4096,128]{3,0,1,2:T(2,128)(2,1)} %bitcast.133) | data formatting | bytes 12582912 | tf_op jit(solution)/shard_map/jit(_take)/gather | solution.py:99
  395.2 73.6 %reduce-scatter.3.cloned.1.call-done = f32[256,128]{0,1:T(8,128)} async-done(((f32[4096,128]{0,1:T(8,128)}), f32[256,128]{0,1:T(8,128)}) %reduce-scatter.3.cloned.1.call-update) | async-done | bytes 131088 | tf_op jit(solution)/shard_map/reduce_scatter | solution.py:115
  472.5 61.9 %all-gather.2.cloned.1.call-done = bf16[4096,128]{0,1:T(8,128)(2,1)} async-done(((bf16[256,128]{0,1:T(8,128)(2,1)}), bf16[4096,128]{0,1:T(8,128)(2,1)}) %all-gather.2.cloned.1.call-update) | async-done | bytes 1048592 | tf_op jit(solution)/shard_map/all_gather | solution.py:123
  539.8 86.2 %reduce-scatter.5.cloned.1.call-done = bf16[256,2,256]{2,0,1:T(8,128)(2,1)} async-done(((bf16[4096,2,256]{2,0,1:T(8,128)(2,1)}), bf16[256,2,256]{2,0,1:T(8,128)(2,1)}) %reduce-scatter.5.cloned.1.call-update) | async-done | bytes 262160 | tf_op jit(solution)/shard_map/reduce_scatter | solution.py:139
  (108 shorter events, 66.1 us)
Async XLA Ops:
  6.5 464.3 %copy-start = (f32[16,32]{1,0:T(8,128)S(1)}, f32[16,32]{1,0:T(8,128)}, u32[]{:S(2)}) copy-start(f32[16,32]{1,0:T(8,128)} %param.13) | copy-start | bytes 6148
  6.5 11.2 %copy-start.11 = (s32[16]{0:T(128)S(1)}, s32[16]{0:T(128)}, u32[]{:S(2)}) copy-start(s32[16]{0:T(128)} %param.16) | copy-start | bytes 196
  6.5 11.8 %copy-start.7 = (s32[4096]{0:T(1024)S(1)}, s32[4096]{0:T(1024)}, u32[]{:S(2)}) copy-start(s32[4096]{0:T(1024)} %param.17) | copy-start | bytes 49156
  6.5 462.3 %reduce-scatter.3.cloned.1.call-start = ((), (), s32[]{:S(2)}) async-start(), calls=%async_computation.2 | async-start | bytes 2228224 | tf_op jit(solution)/shard_map/reduce_scatter | solution.py:115
  16.3 158.3 %collective-permute-start = (bf16[1,3,9216,128]{2,3,1,0:T(8,128)(2,1)}, bf16[1,3,9216,128]{2,3,1,0:T(8,128)(2,1)}, u32[]{:S(2)}, u32[]{:S(2)}) collective-permute-start(bf16[1,3,9216,128]{2,3,1,0:T(8,128)(2,1)} %copy.32), channel_id=1, source_target_pairs={{64,0},{80,16},{96,32},{112,48},{128,64},{144,80},{160,96},{176,11... | collective-permute-start | bytes 21233672 | tf_op jit(solution)/shard_map/ppermute | solution.py:16
  206.4 9.4 %slice-start = ((s8[9437184]{0:T(1024)(128)(4,1)}), s8[4194304]{0:T(1024)(128)(4,1)S(1)}, s32[]{:S(2)}) async-start(s8[9437184]{0:T(1024)(128)(4,1)} %bitcast.126), calls=%async_computation.5 | async-start | bytes 8388608 | tf_op jit(solution)/shard_map/while
  206.4 9.4 %slice-start.1 = ((s8[9437184]{0:T(1024)(128)(4,1)}), s8[4194304]{0:T(1024)(128)(4,1)S(1)}, s32[]{:S(2)}) async-start(s8[9437184]{0:T(1024)(128)(4,1)} %bitcast.126), calls=%async_computation.6 | async-start | bytes 8388608 | tf_op jit(solution)/shard_map/while
  215.0 1.2 slice-start.2
  232.3 5.5 copy-start.1
  245.0 5.6 copy-start.3
  283.4 9.4 %slice-start = ((s8[9437184]{0:T(1024)(128)(4,1)}), s8[4194304]{0:T(1024)(128)(4,1)S(1)}, s32[]{:S(2)}) async-start(s8[9437184]{0:T(1024)(128)(4,1)} %bitcast.126), calls=%async_computation.5 | async-start | bytes 8388608 | tf_op jit(solution)/shard_map/while
  283.4 9.4 %slice-start.1 = ((s8[9437184]{0:T(1024)(128)(4,1)}), s8[4194304]{0:T(1024)(128)(4,1)S(1)}, s32[]{:S(2)}) async-start(s8[9437184]{0:T(1024)(128)(4,1)} %bitcast.126), calls=%async_computation.6 | async-start | bytes 8388608 | tf_op jit(solution)/shard_map/while
  291.9 1.2 slice-start.2
  309.3 5.5 copy-start.1
  321.9 5.6 copy-start.3
  327.7 0.9 copy-start.4
  370.8 16.2 %copy-start.8 = (pred[4096]{0:T(1024)(128)(4,1)S(1)}, pred[4096]{0:T(1024)(128)(4,1)}, u32[]{:S(2)}) copy-start(pred[4096]{0:T(1024)(128)(4,1)} %compare_and_fusion) | copy-start | bytes 12292
  387.0 3.5 copy-start.5
  387.0 3.5 copy-start.6
  393.6 76.8 %copy-start.9 = (f32[16,2]{0,1:T(2,128)S(1)}, f32[16,2]{0,1:T(2,128)}, u32[]{:S(2)}) copy-start(f32[16,2]{0,1:T(2,128)} %param.12) | copy-start | bytes 388
  393.6 77.0 %copy-start.10 = (s32[16,2]{0,1:T(2,128)S(1)}, s32[16,2]{0,1:T(2,128)}, u32[]{:S(2)}) copy-start(s32[16,2]{0,1:T(2,128)} %param.14) | copy-start | bytes 388
  395.2 139.3 %all-gather.2.cloned.1.call-start = ((), (), s32[]{:S(2)}) async-start(), calls=%async_computation.3 | async-start | bytes 1114112 | tf_op jit(solution)/shard_map/all_gather | solution.py:123
  470.4 155.6 %reduce-scatter.5.cloned.1.call-start = ((), (), s32[]{:S(2)}) async-start(), calls=%async_computation.4 | async-start | bytes 4456448 | tf_op jit(solution)/shard_map/reduce_scatter | solution.py:139
  534.5 2.1 copy-start.2
  (1 other events, 0.9 us)
Sparse Core Ops, SparseCore 0:
  395.3 73.4 reduce-scatter.2
  470.5 63.8 all-gather.1
  539.9 86.0 reduce-scatter.4
where the time goes:
time: 639 us; the launch traced here: 635 us
  waiting for transfers between devices  374 us (59%)
  local copies, waits for them, and re-layouts  129 us (20%)
  other arithmetic  77 us (12%)
  matrix products  39.3 us (6%)
  between operations  13.3 us (2%)
    ppermute x1, waiting for transfers between devices, shifted(): return lax.ppermute(block, axis, route)  152 us
    reduce_scatter x1, waiting for transfers between devices, shards(): lax.psum_scatter(jnp.stack([real_part, imag_part], axis=1).astype(jnp.bfl...  86.2 us
    reduce_scatter x1, waiting for transfers between devices, shards(): lax.psum_scatter((jnp.stack([real_part, imag_part], axis=2) * norm_scale)...  73.6 us
    all_gather x1, waiting for transfers between devices, shards(): rho_all = lax.all_gather(rho_here, 'fft', axis=0, tiled=True)  61.9 us
    gather x2, local copies, waits for them, and re-layouts, shards(): jnp.take(columns, column, axis=2)  56.4 us
    reshape x2, local copies, waits for them, and re-layouts, band_fields(): jnp.stack([pair_real, pair_imag], axis=-2)  28.8 us
    dot_general x4, matrix products, complex_section(): jnp.einsum(einsum_form, field_in, sine_table, preferred_element_type=jnp....  19.9 us
    another operation x4, other arithmetic  16.6 us
  transfers between devices with their start and end apart: 4, of which 4 were waited for; matrix products, arithmetic and copies ran while one was open for 1% of the time, Pallas kernels for 0%

commit v1 on v0

v1 whole, which is shorter than its diff:
```python
import math

import jax
import jax.numpy as jnp
import ml_dtypes
import numpy as np
from jax import lax
from jax.experimental import pallas as pl
from jax.experimental.pallas import tpu as pltpu
from jax.sharding import PartitionSpec as P

GRID = 96
BOX = 24
NG = 4096
NV = 2
NC = 32
COLS = 768
ROWS = 256
YCHUNK = 4
PICK = 512


def dft_tables():
    turns = np.mod((np.arange(BOX) - BOX // 2)[:, None] * np.arange(GRID)[None, :], GRID)
    angle = turns.astype(np.float32) * np.float32(2.0 * math.pi / GRID)
    return np.cos(angle), np.sin(angle)


def z_table():
    cosine, sine = dft_tables()
    out = np.zeros((BOX, 2, 2, GRID), np.float32)
    out[:, 0, 0], out[:, 0, 1] = cosine, sine
    out[:, 1, 0], out[:, 1, 1] = -sine, cosine
    return out.reshape(2 * BOX, 2 * GRID).astype(ml_dtypes.bfloat16)


def y_table():
    cosine, sine = dft_tables()
    out = np.zeros((2, 32, 2, GRID), np.float32)
    out[0, :BOX, 0], out[0, :BOX, 1] = cosine, sine
    out[1, :BOX, 0], out[1, :BOX, 1] = -sine, cosine
    return out.reshape(64, 2 * GRID).astype(ml_dtypes.bfloat16)


def val_spread():
    out = np.zeros((NV, 2, 2, 2, 2, NV, NC), np.float32)
    for v in range(NV):
        for p in range(2):
            for i in range(2):
                out[v, p, i, i, p, v, :] = 1.0
    return out.reshape(8, 256).astype(ml_dtypes.bfloat16)


def cond_spread():
    out = np.zeros((2, 2, NC, 2, 2, NV, NC), np.float32)
    for p in range(2):
        for i in range(2):
            for c in range(NC):
                out[p, i, c, i, p, :, c] = 1.0
    return out.reshape(128, 256).astype(ml_dtypes.bfloat16)


def dot(left, right):
    return jnp.dot(left, right, preferred_element_type=jnp.float32)


def field_kernel(val_ref, cond_ref, vs_ref, cs_ref, tz_ref, ty_ref, out_ref, zs_ref):
    points = YCHUNK * GRID

    def z_step(step, carry):
        at = pl.multiple_of(step * points, points)
        val = jnp.concatenate(
            [val_ref[v, :, pl.ds(at, points)].astype(jnp.float32) for v in range(NV)], axis=0
        ).astype(jnp.bfloat16)
        spread = lax.dot_general(
            val, vs_ref[...], (((0,), (0,)), ((), ())), preferred_element_type=jnp.float32
        )
        cond = dot(cond_ref[0, 0, pl.ds(at, points), :], cs_ref[...])
        val_re, val_im = spread[:, :128], spread[:, 128:]
        cond_re, cond_im = cond[:, :128], cond[:, 128:]
        pair_re = (val_re * cond_re + val_im * cond_im).astype(jnp.bfloat16)
        pair_im = (val_re * cond_im - val_im * cond_re).astype(jnp.bfloat16)
        for y in range(0, YCHUNK, 2):
            rhs = jnp.concatenate(
                [
                    jnp.concatenate(
                        [pair_re[(y + u) * GRID : (y + u + 1) * GRID] for u in range(2)], axis=1
                    ),
                    jnp.concatenate(
                        [pair_im[(y + u) * GRID : (y + u + 1) * GRID] for u in range(2)], axis=1
                    ),
                ],
                axis=0,
            )
            z_out = dot(tz_ref[...], rhs)
            for u in range(2):
                zs_ref[pl.ds(step * YCHUNK + y + u, 2 * BOX, stride=GRID), :] = z_out[
                    :, u * 128 : (u + 1) * 128
                ]
        return carry

    lax.fori_loop(0, GRID // YCHUNK, z_step, 0)
    for fz in range(0, BOX, 2):
        rhs = jnp.concatenate(
            [
                zs_ref[(fz + u) * 2 * GRID : (fz + u + 1) * 2 * GRID, :].astype(jnp.bfloat16)
                for u in range(2)
            ],
            axis=1,
        )
        y_out = dot(ty_ref[...], rhs).astype(jnp.bfloat16)
        for u in range(2):
            for i in range(2):
                out_ref[0, (fz + u) * 32 : (fz + u + 1) * 32, i * 128 : (i + 1) * 128] = y_out[
                    i * 32 : (i + 1) * 32, u * 128 : (u + 1) * 128
                ]


def fields(val, cond):
    planes = cond.shape[1]
    return pl.pallas_call(
        field_kernel,
        grid=(planes,),
        in_specs=[
            pl.BlockSpec((NV, 4, GRID * GRID), lambda a: (0, 0, a)),
            pl.BlockSpec((1, 1, GRID * GRID, 128), lambda a: (0, a, 0, 0)),
            pl.BlockSpec((8, 256), lambda a: (0, 0)),
            pl.BlockSpec((128, 256), lambda a: (0, 0)),
            pl.BlockSpec((2 * BOX, 2 * GRID), lambda a: (0, 0)),
            pl.BlockSpec((64, 2 * GRID), lambda a: (0, 0)),
        ],
        out_specs=pl.BlockSpec((1, COLS, 256), lambda a: (a, 0, 0)),
        out_shape=jax.ShapeDtypeStruct((planes, COLS, 256), jnp.bfloat16),
        scratch_shapes=[pltpu.VMEM((2 * BOX * GRID, 128), jnp.float32)],
        compiler_params=pltpu.CompilerParams(vmem_limit_bytes=40 * 2**20),
        cost_estimate=pl.CostEstimate(
            flops=4_000_000_000, bytes_accessed=9_000_000, transcendentals=0
        ),
    )(val, cond, val_spread(), cond_spread(), z_table(), y_table())


def pick_kernel(col_ref, fx_ref, y_ref, xt_ref, out_ref):
    lane = lax.broadcasted_iota(jnp.int32, (PICK, 128), 1)
    column = col_ref[...]
    chosen = jnp.concatenate(
        [
            jnp.where(column == lane + 128 * t, 1.0, 0.0).astype(jnp.bfloat16)
            for t in range(COLS // 128)
        ],
        axis=1,
    )
    freq = jnp.where(fx_ref[...] == lane, 1.0, 0.0).astype(jnp.bfloat16)
    real = jnp.zeros((PICK, 128), jnp.float32)
    imag = jnp.zeros((PICK, 128), jnp.float32)
    for a in range(y_ref.shape[0]):
        got = dot(chosen, y_ref[a])
        phase = dot(freq, xt_ref[:, a * 256 : (a + 1) * 256])
        cosine, sine = phase[:, :128], phase[:, 128:]
        got_re, got_im = got[:, :128], got[:, 128:]
        real = real + cosine * got_re + sine * got_im
        imag = imag + cosine * got_im - sine * got_re
    real = real + pltpu.roll(real, 64, 1)
    imag = imag + pltpu.roll(imag, 64, 1)
    scale = 1.0 / (GRID * math.sqrt(GRID))
    out_ref[...] = (jnp.where(lane < 64, real, imag) * scale).astype(jnp.bfloat16)


def pick(column, freq, field, x_table):
    planes = field.shape[0]
    return pl.pallas_call(
        pick_kernel,
        grid=(NG // PICK,),
        in_specs=[
            pl.BlockSpec((PICK, 128), lambda g: (g, 0)),
            pl.BlockSpec((PICK, 128), lambda g: (g, 0)),
            pl.BlockSpec((planes, COLS, 256), lambda g: (0, 0, 0)),
            pl.BlockSpec((128, planes * 256), lambda g: (0, 0)),
        ],
        out_specs=pl.BlockSpec((PICK, 128), lambda g: (g, 0)),
        out_shape=jax.ShapeDtypeStruct((NG, 128), jnp.bfloat16),
        compiler_params=pltpu.CompilerParams(vmem_limit_bytes=40 * 2**20),
        cost_estimate=pl.CostEstimate(
            flops=8_000_000_000, bytes_accessed=6_000_000, transcendentals=0
        ),
    )(column, freq, field, x_table)


def chi_kernel(row_a_ref, row_b_ref, *refs):
    a_refs, b_refs = refs[:10], refs[10:12]
    weight_ref, out_ref, wa_ref = refs[12:]
    lane = lax.broadcasted_iota(jnp.int32, (ROWS, 128), 1)
    sign = jnp.where(lane < 64, 1.0, -1.0)
    place = 0
    for ref in a_refs:
        for part in range(ref.shape[0] // ROWS):
            row = row_a_ref[place]
            piece = ref[part * ROWS : (part + 1) * ROWS, :].astype(jnp.float32)
            weighted = (piece * weight_ref[pl.ds(row, 1), :]).astype(jnp.bfloat16).astype(jnp.float32)
            wa_ref[row, :ROWS, :] = weighted.astype(jnp.bfloat16)
            wa_ref[row, ROWS:, :] = (pltpu.roll(weighted, 64, 1) * sign).astype(jnp.bfloat16)
            place += 1
    total = jnp.zeros((2 * ROWS, ROWS), jnp.float32)
    place = 0
    for ref in b_refs:
        for part in range(0, ref.shape[0] // ROWS, 2):
            left = jnp.concatenate(
                [wa_ref[row_b_ref[place]], wa_ref[row_b_ref[place + 1]]], axis=1
            )
            right = jnp.concatenate(
                [ref[(part + u) * ROWS : (part + u + 1) * ROWS, :] for u in range(2)], axis=1
            )
            total = total + lax.dot_general(
                left, right, (((1,), (1,)), ((), ())), preferred_element_type=jnp.float32
            )
            place += 2
    out_ref[:, 0, :] = total[:ROWS]
    out_ref[:, 1, :] = total[ROWS:]


def contract(row_a, row_b, a_parts, b_parts, weight):
    smem = pl.BlockSpec(memory_space=pltpu.SMEM)
    vmem = pl.BlockSpec(memory_space=pltpu.VMEM)
    return pl.pallas_call(
        chi_kernel,
        in_specs=[smem, smem] + [vmem] * (len(a_parts) + len(b_parts) + 1),
        out_specs=vmem,
        out_shape=jax.ShapeDtypeStruct((ROWS, 2, ROWS), jnp.float32),
        scratch_shapes=[pltpu.VMEM((16, 2 * ROWS, 128), jnp.bfloat16)],
        compiler_params=pltpu.CompilerParams(vmem_limit_bytes=40 * 2**20),
        cost_estimate=pl.CostEstimate(
            flops=600_000_000, bytes_accessed=4_000_000, transcendentals=0
        ),
    )(row_a, row_b, *a_parts, *b_parts, weight)


def ka_route(move):
    route = []
    for i in range(16):
        y, x, c = move(i // 8, (i // 2) % 4, i % 2)
        route.append((i, (y % 2) * 8 + (x % 4) * 2 + c % 2))
    return route


def fft_route(move):
    route = []
    for i in range(16):
        y, z = move(i // 8, i % 8)
        route.append((i, (y % 2) * 8 + z % 8))
    return route


def gather_columns(rho):
    across = lax.ppermute(rho, "ka", ka_route(lambda y, x, c: (y + 1, x, c)))
    block = jnp.concatenate([rho, across])
    ring = [
        lax.ppermute(block, "ka", ka_route(lambda y, x, c, s=s: (y, x + s, c))) for s in (1, 2, 3)
    ]
    block = jnp.concatenate([block] + ring)
    other = lax.ppermute(block, "ka", ka_route(lambda y, x, c: (y, x, c + 1)))
    row = lax.axis_index("ka")
    y, x, c = row // 8, (row // 2) % 4, row % 2
    places = [
        ((y + dy) % 2) * 8 + ((x - s) % 4) * 2 + (c + dc) % 2
        for dc in range(2)
        for s in range(4)
        for dy in range(2)
    ]
    return [block, other], jnp.stack(places).astype(jnp.int32)


def gather_rows(rho):
    own = lax.ppermute(
        rho, ("ka", "fft"), [(i * 16 + j, j * 16 + i) for i in range(16) for j in range(16)]
    )
    across = lax.ppermute(own, "fft", fft_route(lambda y, z: (y + 1, z)))
    block = jnp.concatenate([own, across])
    spot = lax.axis_index("fft")
    y, z = spot // 8, spot % 8
    parts, places = [own, across], [(y, z), (y + 1, z)]
    up = down = block
    for t in range(1, 4):
        up = lax.ppermute(up, "fft", fft_route(lambda y, z: (y, z + 1)))
        down = lax.ppermute(down, "fft", fft_route(lambda y, z: (y, z - 1)))
        parts += [up, down]
        places += [(y, z - t), (y + 1, z - t), (y, z + t), (y + 1, z + t)]
    parts.append(lax.ppermute(up[:ROWS], "fft", fft_route(lambda y, z: (y, z + 1))))
    parts.append(lax.ppermute(down[ROWS:], "fft", fft_route(lambda y, z: (y, z - 1))))
    places += [(y, z + 4), (y + 1, z + 4)]
    return parts, jnp.stack([(a % 2) * 8 + b % 8 for a, b in places]).astype(jnp.int32)


def shards(psi_val, psi_cond, e_val, e_cond, occ_val, occ_cond, umklapp, sphere):
    count_k = 16
    step_q = 4
    row = lax.axis_index("ka")
    x_block = lax.axis_index("fft")
    planes = psi_cond.shape[1]
    val = lax.ppermute(
        psi_val, "ka", [(i, (i + step_q) % count_k) for i in range(count_k)]
    )[0]
    k_here = jnp.mod(row - step_q, count_k)

    offset = lax.dynamic_index_in_dim(umklapp, k_here, keepdims=False)
    x_place = 2 * planes * x_block + jnp.arange(2 * planes, dtype=jnp.int32)
    x_freq = jnp.arange(128, dtype=jnp.int32) - BOX // 2 - offset
    turns = jnp.mod(x_freq[:, None] * x_place[None, :], GRID).astype(jnp.float32)
    angle = turns * (2.0 * math.pi / GRID)
    both = jnp.stack(
        [jnp.cos(angle).reshape(128, planes, 2), jnp.sin(angle).reshape(128, planes, 2)], axis=2
    )
    x_table = jnp.broadcast_to(both[..., None], (128, planes, 2, 2, 64)).reshape(128, planes * 256)
    x_table = x_table.astype(jnp.bfloat16)
    plane = sphere % (BOX * BOX)
    column = (plane % BOX) * 32 + plane // BOX
    column = jnp.broadcast_to(column[:, None], (NG, 128))
    freq = jnp.broadcast_to((sphere // (BOX * BOX))[:, None], (NG, 128))

    weight = (occ_val[:, :, None] - jnp.roll(occ_cond, -step_q, 0)[:, None, :]).astype(
        jnp.float32
    ) / ((e_val[:, :, None] - jnp.roll(e_cond, -step_q, 0)[:, None, :]) * (count_k * NV))
    weight = jnp.roll(weight.reshape(count_k, NV * NC), step_q, 0)
    weight = jnp.concatenate([weight, weight], axis=1)

    field = fields(val, psi_cond)
    share = pick(column, freq, field, x_table)
    spread = lax.all_to_all(share.reshape(16, ROWS, 128), "fft", 0, 0)
    rho = spread.astype(jnp.float32).sum(0).astype(jnp.bfloat16)
    b_parts, row_b = gather_columns(rho)
    a_parts, row_a = gather_rows(rho)
    return contract(row_a, row_b, a_parts, b_parts, weight)


def solution(mesh):
    placed = (P("ka", None, None, "fft"), P("ka", "fft", None, None), P(), P(), P(), P(), P(), P())
    return jax.shard_map(
        shards, mesh=mesh, in_specs=placed, out_specs=P("ka", None, "fft"), check_vma=False
    )
```

time: 639 us -> 149 us (0.23)
  the two profiles are of different devices: /device:TPU:62 before, /device:TPU:10 now
where the time goes in v1:
time: 149 us
  waiting for transfers between devices  52 us (35%)
  Pallas kernels  44.9 us (30%)
  starting transfers between devices  40.1 us (27%)
  local copies, waits for them, and re-layouts  9.3 us (6%)
  other arithmetic  1.91 us (1%)
    pallas_call x1, Pallas kernels, fields(): pl.pallas_call(field_kernel, grid=(planes,), in_specs=[pl.BlockSpec((NV,...  33.2 us
    all_to_all x1, waiting for transfers between devices, shards(): spread = lax.all_to_all(share.reshape(16, ROWS, 128), 'fft', 0, 0)  24.5 us
    ppermute x3, starting transfers between devices, gather_rows(): down = lax.ppermute(down, 'fft', fft_route(lambda y, z: (y, z - 1)))  11.6 us
    ppermute x1, waiting for transfers between devices, shards(): lax.ppermute(psi_val, 'ka', [(i, (i + step_q) % count_k) for i in range(c...  10.9 us
    all_to_all x1, starting transfers between devices, shards(): spread = lax.all_to_all(share.reshape(16, ROWS, 128), 'fft', 0, 0)  10.1 us
    pallas_call x1, Pallas kernels, pick(): pl.pallas_call(pick_kernel, grid=(NG // PICK,), in_specs=[pl.BlockSpec((P...  9.24 us
    ppermute x3, waiting for transfers between devices, gather_rows(): down = lax.ppermute(down, 'fft', fft_route(lambda y, z: (y, z - 1)))  6.96 us
    unnamed x25, local copies, waits for them, and re-layouts  6.28 us
  transfers between devices with their start and end apart: 17, of which 10 were waited for; matrix products, arithmetic and copies ran while one was open for 3% of the time, Pallas kernels for 0%

profile of v1, /device:TPU:10, one launch (start us, length us, event | category | flops | bytes accessed | tf_op | source)
XLA Modules:
  0.0 148.8 jit_solution(190643826782703425)
XLA Ops:
  0.0 2.1 %collective-permute-start = (bf16[1,2,4,27648]{3,2,1,0:T(4,128)(2,1)}, bf16[1,2,4,27648]{3,2,1,0:T(4,128)(2,1)S(1)}, u32[]{:S(2)}, u32[]{:S(2)}) collective-permute-start(bf16[1,2,4,27648]{3,2,1,0:T(4,128)(2,1)} %param.12), channel_id=1, source_target_pairs={{0,64},{16,80},{32,96},{48,112},{64,128},{80,144},{96,160},{112,17... | collective-permute-start | bytes 1327112 | tf_op jit(solution)/shard_map/ppermute | solution.py:298
  2.1 1.2 dynamic_slice.4
  5.1 10.9 %collective-permute-done = bf16[1,2,4,27648]{3,2,1,0:T(4,128)(2,1)S(1)} collective-permute-done((bf16[1,2,4,27648]{3,2,1,0:T(4,128)(2,1)}, bf16[1,2,4,27648]{3,2,1,0:T(4,128)(2,1)S(1)}, u32[]{:S(2)}, u32[]{:S(2)}) %collective-permute-start) | collective-permute-done | bytes 442400 | tf_op jit(solution)/shard_map/ppermute | solution.py:298
  16.0 3.0 %copy-done = bf16[1,3,9216,128]{3,2,1,0:T(8,128)(2,1)S(1)} copy-done((bf16[1,3,9216,128]{3,2,1,0:T(8,128)(2,1)S(1)}, bf16[1,3,9216,128]{3,2,1,0:T(8,128)(2,1)}, u32[]{:S(2)}) %copy-start) | copy-done | bytes 7077912
  22.1 33.2 %shard_map.118.y_ref = bf16[3,768,256]{2,1,0:T(8,128)(2,1)S(1)} custom-call(bf16[2,4,27648]{2,1,0:T(4,128)(2,1)S(1)} %bitcast.36, bf16[1,3,9216,128]{3,2,1,0:T(8,128)(2,1)S(1)} %copy-done, bf16[8,256]{1,0:T(8,128)(2,1)S(1)} %copy-done.4, bf16[128,256]{1,0:T(8,128)(2,1)S(1)} %copy-done.1, bf16[48,192]{1,0:T(8,128)(2,1)S(1)} %copy-done.3, ...), custom_call_target="tpu_custom_call" | custom-call | flops 4000000000 | bytes 9000000 | tf_op jit(solution)/shard_map/pallas_call | solution.py:121
  56.4 9.2 %shard_map.119 = bf16[4096,128]{1,0:T(8,128)(2,1)} custom-call(s32[4096,128]{1,0:T(8,128)S(1)} %broadcast_in_dim.6.col_ref, s32[4096,128]{1,0:T(8,128)S(1)} %broadcast_in_dim.7.fx_ref, bf16[3,768,256]{2,1,0:T(8,128)(2,1)S(1)} %shard_map.118.y_ref, bf16[128,768]{1,0:T(8,128)(2,1)S(1)} %copy.15.xt_ref), custom_call_target="tpu_custom_call" | custom-call | flops 8000000000 | bytes 6000000 | tf_op jit(solution)/shard_map/pallas_call | solution.py:170
  65.7 10.1 %all-to-all-start = ((bf16[16,256,128]{2,1,0:T(8,128)(2,1)}), bf16[16,256,128]{2,1,0:T(8,128)(2,1)S(1)}, u32[]{:S(2)}, u32[]{:S(2)}) async-start(bf16[16,256,128]{2,1,0:T(8,128)(2,1)} %bitcast.35), calls=%async_computation | async-start | bytes 2097152 | tf_op jit(solution)/shard_map/all_to_all | solution.py:326
  75.8 24.5 %all-to-all-done = bf16[16,256,128]{2,1,0:T(8,128)(2,1)S(1)} async-done(((bf16[16,256,128]{2,1,0:T(8,128)(2,1)}), bf16[16,256,128]{2,1,0:T(8,128)(2,1)S(1)}, u32[]{:S(2)}, u32[]{:S(2)}) %all-to-all-start) | async-done | bytes 1048608 | tf_op jit(solution)/shard_map/all_to_all | solution.py:326
  100.4 2.4 %collective-permute-start.11 = (bf16[256,128]{1,0:T(8,128)(2,1)S(1)}, bf16[256,128]{1,0:T(8,128)(2,1)S(1)}, u32[]{:S(2)}, u32[]{:S(2)}) collective-permute-start(bf16[256,128]{1,0:T(8,128)(2,1)S(1)} %reduce_sum.12), channel_id=1, source_target_pairs={{0,128},{16,144},{32,160},{48,176},{64,192},{80,208},{96,224},{112... | collective-permute-start | bytes 196616 | tf_op jit(solution)/shard_map/ppermute | solution.py:253
  102.8 3.1 %collective-permute-start.1 = (bf16[256,128]{1,0:T(8,128)(2,1)S(1)}, bf16[256,128]{1,0:T(8,128)(2,1)S(1)}, u32[]{:S(2)}, u32[]{:S(2)}) collective-permute-start(bf16[256,128]{1,0:T(8,128)(2,1)S(1)} %reduce_sum.12), channel_id=1, source_target_pairs={{0,0},{1,16},{2,32},{3,48},{4,64},{5,80},{6,96},{7,112},{8,128},{9... | collective-permute-start | bytes 196616 | tf_op jit(solution)/shard_map/ppermute | solution.py:272
  106.3 2.5 %collective-permute-start.12 = (bf16[512,128]{1,0:T(8,128)(2,1)S(1)}, bf16[512,128]{1,0:T(8,128)(2,1)S(1)}, u32[]{:S(2)}, u32[]{:S(2)}) collective-permute-start(bf16[512,128]{1,0:T(8,128)(2,1)S(1)} %pad_maximum_fusion), channel_id=1, source_target_pairs={{0,32},{16,48},{32,64},{48,80},{64,96},{80,112},{96,0},{112,16},{1... | collective-permute-start | bytes 393224 | tf_op jit(solution)/shard_map/ppermute | solution.py:256
  109.5 2.5 %collective-permute-start.14 = (bf16[512,128]{1,0:T(8,128)(2,1)S(1)}, bf16[512,128]{1,0:T(8,128)(2,1)S(1)}, u32[]{:S(2)}, u32[]{:S(2)}) collective-permute-start(bf16[512,128]{1,0:T(8,128)(2,1)S(1)} %pad_maximum_fusion), channel_id=1, source_target_pairs={{0,96},{16,112},{32,0},{48,16},{64,32},{80,48},{96,64},{112,80},{1... | collective-permute-start | bytes 393224 | tf_op jit(solution)/shard_map/ppermute | solution.py:256
  112.9 1.2 collective-permute-start.2
  114.1 3.0 %collective-permute-done.2.refs_1_ = bf16[256,128]{1,0:T(8,128)(2,1)S(1)} collective-permute-done((bf16[256,128]{1,0:T(8,128)(2,1)S(1)}, bf16[256,128]{1,0:T(8,128)(2,1)S(1)}, u32[]{:S(2)}, u32[]{:S(2)}) %collective-permute-start.2) | collective-permute-done | bytes 65568 | tf_op jit(solution)/shard_map/ppermute | solution.py:275
  117.1 4.3 %collective-permute-start.4 = (bf16[512,128]{1,0:T(8,128)(2,1)S(1)}, bf16[512,128]{1,0:T(8,128)(2,1)S(1)}, u32[]{:S(2)}, u32[]{:S(2)}) collective-permute-start(bf16[512,128]{1,0:T(8,128)(2,1)S(1)} %constant_dynamic-update-slice_fusion), channel_id=1, source_target_pairs={{0,7},{1,0},{2,1},{3,2},{4,3},{5,4},{6,5},{7,6},{8,15},{9,8},{10,9... | collective-permute-start | bytes 393224 | tf_op jit(solution)/shard_map/ppermute | solution.py:283
  121.7 2.3 %collective-permute-done.4.refs_3_ = bf16[512,128]{1,0:T(8,128)(2,1)S(1)} collective-permute-done((bf16[512,128]{1,0:T(8,128)(2,1)S(1)}, bf16[512,128]{1,0:T(8,128)(2,1)S(1)}, u32[]{:S(2)}, u32[]{:S(2)}) %collective-permute-start.4) | collective-permute-done | bytes 131104 | tf_op jit(solution)/shard_map/ppermute | solution.py:283
  124.0 3.7 %collective-permute-start.6 = (bf16[512,128]{1,0:T(8,128)(2,1)S(1)}, bf16[512,128]{1,0:T(8,128)(2,1)S(1)}, u32[]{:S(2)}, u32[]{:S(2)}) collective-permute-start(bf16[512,128]{1,0:T(8,128)(2,1)S(1)} %collective-permute-done.4.refs_3_), channel_id=1, source_target_pairs={{0,7},{1,0},{2,1},{3,2},{4,3},{5,4},{6,5},{7,6},{8,15},{9,8},{10,9... | collective-permute-start | bytes 393224 | tf_op jit(solution)/shard_map/ppermute | solution.py:283
  128.2 1.9 %collective-permute-done.6.refs_5_ = bf16[512,128]{1,0:T(8,128)(2,1)S(1)} collective-permute-done((bf16[512,128]{1,0:T(8,128)(2,1)S(1)}, bf16[512,128]{1,0:T(8,128)(2,1)S(1)}, u32[]{:S(2)}, u32[]{:S(2)}) %collective-permute-start.6) | collective-permute-done | bytes 131104 | tf_op jit(solution)/shard_map/ppermute | solution.py:283
  130.2 3.7 %collective-permute-start.8 = (bf16[512,128]{1,0:T(8,128)(2,1)S(1)}, bf16[512,128]{1,0:T(8,128)(2,1)S(1)}, u32[]{:S(2)}, u32[]{:S(2)}) collective-permute-start(bf16[512,128]{1,0:T(8,128)(2,1)S(1)} %collective-permute-done.6.refs_5_), channel_id=1, source_target_pairs={{0,7},{1,0},{2,1},{3,2},{4,3},{5,4},{6,5},{7,6},{8,15},{9,8},{10,9... | collective-permute-start | bytes 393224 | tf_op jit(solution)/shard_map/ppermute | solution.py:283
  134.3 2.7 %collective-permute-done.8.refs_7_ = bf16[512,128]{1,0:T(8,128)(2,1)S(1)} collective-permute-done((bf16[512,128]{1,0:T(8,128)(2,1)S(1)}, bf16[512,128]{1,0:T(8,128)(2,1)S(1)}, u32[]{:S(2)}, u32[]{:S(2)}) %collective-permute-start.8) | collective-permute-done | bytes 131104 | tf_op jit(solution)/shard_map/ppermute | solution.py:283
  137.0 3.7 %collective-permute-start.10 = (bf16[256,128]{1,0:T(8,128)(2,1)S(1)}, bf16[256,128]{1,0:T(8,128)(2,1)S(1)}, u32[]{:S(2)}, u32[]{:S(2)}) collective-permute-start(bf16[256,128]{1,0:T(8,128)(2,1)S(1)} %slice.47), channel_id=1, source_target_pairs={{0,7},{1,0},{2,1},{3,2},{4,3},{5,4},{6,5},{7,6},{8,15},{9,8},{10,9... | collective-permute-start | bytes 196616 | tf_op jit(solution)/shard_map/ppermute | solution.py:287
  140.9 1.7 %collective-permute-done.10.refs_9_ = bf16[256,128]{1,0:T(8,128)(2,1)S(1)} collective-permute-done((bf16[256,128]{1,0:T(8,128)(2,1)S(1)}, bf16[256,128]{1,0:T(8,128)(2,1)S(1)}, u32[]{:S(2)}, u32[]{:S(2)}) %collective-permute-start.10) | collective-permute-done | bytes 65568 | tf_op jit(solution)/shard_map/ppermute | solution.py:287
  142.6 3.7 %collective-permute-done.9.refs_8_ = bf16[256,128]{1,0:T(8,128)(2,1)S(1)} collective-permute-done((bf16[256,128]{1,0:T(8,128)(2,1)S(1)}, bf16[256,128]{1,0:T(8,128)(2,1)S(1)}, u32[]{:S(2)}, u32[]{:S(2)}) %collective-permute-start.9) | collective-permute-done | bytes 65568 | tf_op jit(solution)/shard_map/ppermute | solution.py:286
  146.3 2.5 %shard_map.120 = f32[256,2,256]{2,1,0:T(2,128)} custom-call(s32[16]{0:T(128)S(1)} %stack.122.row_a_ref, s32[16]{0:T(128)S(1)} %stack.139.row_b_ref, bf16[256,128]{1,0:T(8,128)(2,1)S(1)} %collective-permute-done.1.refs_0_, bf16[256,128]{1,0:T(8,128)(2,1)S(1)} %collective-permute-done.2.refs_1_, bf16[512,128]{1,0:T(8,128)(2,1)S(1)} %collective-permute-done.3.refs_2_, ...), custom_call_target="tpu_custom_call" | custom-call | flops 600000000 | bytes 4000000 | tf_op jit(solution)/shard_map/pallas_call | solution.py:223
  (70 shorter events, 9.1 us)
Async XLA Ops:
  0.0 16.0 %collective-permute-start = (bf16[1,2,4,27648]{3,2,1,0:T(4,128)(2,1)}, bf16[1,2,4,27648]{3,2,1,0:T(4,128)(2,1)S(1)}, u32[]{:S(2)}, u32[]{:S(2)}) collective-permute-start(bf16[1,2,4,27648]{3,2,1,0:T(4,128)(2,1)} %param.12), channel_id=1, source_target_pairs={{0,64},{16,80},{32,96},{48,112},{64,128},{80,144},{96,160},{112,17... | collective-permute-start | bytes 1327112 | tf_op jit(solution)/shard_map/ppermute | solution.py:298
  16.0 3.0 %copy-start = (bf16[1,3,9216,128]{3,2,1,0:T(8,128)(2,1)S(1)}, bf16[1,3,9216,128]{3,2,1,0:T(8,128)(2,1)}, u32[]{:S(2)}) copy-start(bf16[1,3,9216,128]{3,2,1,0:T(8,128)(2,1)} %cond_ref.1) | copy-start | bytes 21233668
  65.7 10.1 %copy-start.5 = (s32[16,32]{1,0:T(8,128)S(1)}, s32[16,32]{1,0:T(8,128)}, u32[]{:S(2)}) copy-start(s32[16,32]{1,0:T(8,128)} %param.17) | copy-start | bytes 6148
  65.7 62.0 %slice-start = ((s32[16,32]{1,0:T(8,128)}), s32[4,32]{1,0:T(4,128)S(1)}, s32[]{:S(2)}) async-start(s32[16,32]{1,0:T(8,128)} %param.17), calls=%async_computation.1 | async-start | bytes 4096 | tf_op jit(solution)/shard_map/jit(_roll_static)/slice | solution.py:318
  65.7 34.6 %all-to-all-start = ((bf16[16,256,128]{2,1,0:T(8,128)(2,1)}), bf16[16,256,128]{2,1,0:T(8,128)(2,1)S(1)}, u32[]{:S(2)}, u32[]{:S(2)}) async-start(bf16[16,256,128]{2,1,0:T(8,128)(2,1)} %bitcast.35), calls=%async_computation | async-start | bytes 2097152 | tf_op jit(solution)/shard_map/all_to_all | solution.py:326
  75.7 52.3 %copy-start.6 = (f32[16,32]{1,0:T(8,128)S(1)}, f32[16,32]{1,0:T(8,128)}, u32[]{:S(2)}) copy-start(f32[16,32]{1,0:T(8,128)} %param.15) | copy-start | bytes 6148
  75.8 52.3 %copy-start.7 = (s32[16,2]{0,1:T(2,128)S(1)}, s32[16,2]{0,1:T(2,128)}, u32[]{:S(2)}) copy-start(s32[16,2]{0,1:T(2,128)} %param.16) | copy-start | bytes 388
  75.8 52.3 %copy-start.8 = (f32[16,2]{0,1:T(2,128)S(1)}, f32[16,2]{0,1:T(2,128)}, u32[]{:S(2)}) copy-start(f32[16,2]{0,1:T(2,128)} %param.14) | copy-start | bytes 388
  75.8 52.4 %slice-start.1 = ((f32[16,32]{1,0:T(8,128)}), f32[4,32]{1,0:T(4,128)S(1)}, s32[]{:S(2)}) async-start(f32[16,32]{1,0:T(8,128)} %param.15), calls=%async_computation.2 | async-start | bytes 4096 | tf_op jit(solution)/shard_map/jit(_roll_static)/slice | solution.py:320
  100.4 5.9 %collective-permute-start.11 = (bf16[256,128]{1,0:T(8,128)(2,1)S(1)}, bf16[256,128]{1,0:T(8,128)(2,1)S(1)}, u32[]{:S(2)}, u32[]{:S(2)}) collective-permute-start(bf16[256,128]{1,0:T(8,128)(2,1)S(1)} %reduce_sum.12), channel_id=1, source_target_pairs={{0,128},{16,144},{32,160},{48,176},{64,192},{80,208},{96,224},{112... | collective-permute-start | bytes 196616 | tf_op jit(solution)/shard_map/ppermute | solution.py:253
  102.8 10.1 %collective-permute-start.1 = (bf16[256,128]{1,0:T(8,128)(2,1)S(1)}, bf16[256,128]{1,0:T(8,128)(2,1)S(1)}, u32[]{:S(2)}, u32[]{:S(2)}) collective-permute-start(bf16[256,128]{1,0:T(8,128)(2,1)S(1)} %reduce_sum.12), channel_id=1, source_target_pairs={{0,0},{1,16},{2,32},{3,48},{4,64},{5,80},{6,96},{7,112},{8,128},{9... | collective-permute-start | bytes 196616 | tf_op jit(solution)/shard_map/ppermute | solution.py:272
  106.3 15.2 %collective-permute-start.12 = (bf16[512,128]{1,0:T(8,128)(2,1)S(1)}, bf16[512,128]{1,0:T(8,128)(2,1)S(1)}, u32[]{:S(2)}, u32[]{:S(2)}) collective-permute-start(bf16[512,128]{1,0:T(8,128)(2,1)S(1)} %pad_maximum_fusion), channel_id=1, source_target_pairs={{0,32},{16,48},{32,64},{48,80},{64,96},{80,112},{96,0},{112,16},{1... | collective-permute-start | bytes 393224 | tf_op jit(solution)/shard_map/ppermute | solution.py:256
  108.8 12.7 %collective-permute-start.13 = (bf16[512,128]{1,0:T(8,128)(2,1)S(1)}, bf16[512,128]{1,0:T(8,128)(2,1)S(1)}, u32[]{:S(2)}, u32[]{:S(2)}) collective-permute-start(bf16[512,128]{1,0:T(8,128)(2,1)S(1)} %pad_maximum_fusion), channel_id=1, source_target_pairs={{0,64},{16,80},{32,96},{48,112},{64,0},{80,16},{96,32},{112,48},{1... | collective-permute-start | bytes 393224 | tf_op jit(solution)/shard_map/ppermute | solution.py:256
  109.5 12.1 %collective-permute-start.14 = (bf16[512,128]{1,0:T(8,128)(2,1)S(1)}, bf16[512,128]{1,0:T(8,128)(2,1)S(1)}, u32[]{:S(2)}, u32[]{:S(2)}) collective-permute-start(bf16[512,128]{1,0:T(8,128)(2,1)S(1)} %pad_maximum_fusion), channel_id=1, source_target_pairs={{0,96},{16,112},{32,0},{48,16},{64,32},{80,48},{96,64},{112,80},{1... | collective-permute-start | bytes 393224 | tf_op jit(solution)/shard_map/ppermute | solution.py:256
  112.9 4.3 %collective-permute-start.2 = (bf16[256,128]{1,0:T(8,128)(2,1)S(1)}, bf16[256,128]{1,0:T(8,128)(2,1)S(1)}, u32[]{:S(2)}, u32[]{:S(2)}) collective-permute-start(bf16[256,128]{1,0:T(8,128)(2,1)S(1)} %collective-permute-done.1.refs_0_), channel_id=1, source_target_pairs={{0,8},{1,9},{2,10},{3,11},{4,12},{5,13},{6,14},{7,15},{8,0},{9,1},... | collective-permute-start | bytes 196616 | tf_op jit(solution)/shard_map/ppermute | solution.py:275
  117.1 6.8 %collective-permute-start.4 = (bf16[512,128]{1,0:T(8,128)(2,1)S(1)}, bf16[512,128]{1,0:T(8,128)(2,1)S(1)}, u32[]{:S(2)}, u32[]{:S(2)}) collective-permute-start(bf16[512,128]{1,0:T(8,128)(2,1)S(1)} %constant_dynamic-update-slice_fusion), channel_id=1, source_target_pairs={{0,7},{1,0},{2,1},{3,2},{4,3},{5,4},{6,5},{7,6},{8,15},{9,8},{10,9... | collective-permute-start | bytes 393224 | tf_op jit(solution)/shard_map/ppermute | solution.py:283
  121.5 6.2 %collective-permute-start.3 = (bf16[512,128]{1,0:T(8,128)(2,1)S(1)}, bf16[512,128]{1,0:T(8,128)(2,1)S(1)}, u32[]{:S(2)}, u32[]{:S(2)}) collective-permute-start(bf16[512,128]{1,0:T(8,128)(2,1)S(1)} %constant_dynamic-update-slice_fusion), channel_id=1, source_target_pairs={{0,1},{1,2},{2,3},{3,4},{4,5},{5,6},{6,7},{7,0},{8,9},{9,10},{10,1... | collective-permute-start | bytes 393224 | tf_op jit(solution)/shard_map/ppermute | solution.py:282
  121.6 24.7 %collective-permute-start.15 = (bf16[2048,128]{1,0:T(8,128)(2,1)S(1)}, bf16[2048,128]{1,0:T(8,128)(2,1)S(1)}, u32[]{:S(2)}, u32[]{:S(2)}) collective-permute-start(bf16[2048,128]{1,0:T(8,128)(2,1)S(1)} %constant_dynamic-update-slice_fusion.2.refs_10_), channel_id=1, source_target_pairs={{0,16},{16,0},{32,48},{48,32},{64,80},{80,64},{96,112},{112,96},{1... | collective-permute-start | bytes 1572872 | tf_op jit(solution)/shard_map/ppermute | solution.py:259
  124.0 6.2 %collective-permute-start.6 = (bf16[512,128]{1,0:T(8,128)(2,1)S(1)}, bf16[512,128]{1,0:T(8,128)(2,1)S(1)}, u32[]{:S(2)}, u32[]{:S(2)}) collective-permute-start(bf16[512,128]{1,0:T(8,128)(2,1)S(1)} %collective-permute-done.4.refs_3_), channel_id=1, source_target_pairs={{0,7},{1,0},{2,1},{3,2},{4,3},{5,4},{6,5},{7,6},{8,15},{9,8},{10,9... | collective-permute-start | bytes 393224 | tf_op jit(solution)/shard_map/ppermute | solution.py:283
  127.6 6.2 %collective-permute-start.5 = (bf16[512,128]{1,0:T(8,128)(2,1)S(1)}, bf16[512,128]{1,0:T(8,128)(2,1)S(1)}, u32[]{:S(2)}, u32[]{:S(2)}) collective-permute-start(bf16[512,128]{1,0:T(8,128)(2,1)S(1)} %collective-permute-done.3.refs_2_), channel_id=1, source_target_pairs={{0,1},{1,2},{2,3},{3,4},{4,5},{5,6},{6,7},{7,0},{8,9},{9,10},{10,1... | collective-permute-start | bytes 393224 | tf_op jit(solution)/shard_map/ppermute | solution.py:282
  130.2 6.9 %collective-permute-start.8 = (bf16[512,128]{1,0:T(8,128)(2,1)S(1)}, bf16[512,128]{1,0:T(8,128)(2,1)S(1)}, u32[]{:S(2)}, u32[]{:S(2)}) collective-permute-start(bf16[512,128]{1,0:T(8,128)(2,1)S(1)} %collective-permute-done.6.refs_5_), channel_id=1, source_target_pairs={{0,7},{1,0},{2,1},{3,2},{4,3},{5,4},{6,5},{7,6},{8,15},{9,8},{10,9... | collective-permute-start | bytes 393224 | tf_op jit(solution)/shard_map/ppermute | solution.py:283
  133.8 6.9 %collective-permute-start.7 = (bf16[512,128]{1,0:T(8,128)(2,1)S(1)}, bf16[512,128]{1,0:T(8,128)(2,1)S(1)}, u32[]{:S(2)}, u32[]{:S(2)}) collective-permute-start(bf16[512,128]{1,0:T(8,128)(2,1)S(1)} %collective-permute-done.5.refs_4_), channel_id=1, source_target_pairs={{0,1},{1,2},{2,3},{3,4},{4,5},{5,6},{6,7},{7,0},{8,9},{9,10},{10,1... | collective-permute-start | bytes 393224 | tf_op jit(solution)/shard_map/ppermute | solution.py:282
  137.0 5.6 %collective-permute-start.10 = (bf16[256,128]{1,0:T(8,128)(2,1)S(1)}, bf16[256,128]{1,0:T(8,128)(2,1)S(1)}, u32[]{:S(2)}, u32[]{:S(2)}) collective-permute-start(bf16[256,128]{1,0:T(8,128)(2,1)S(1)} %slice.47), channel_id=1, source_target_pairs={{0,7},{1,0},{2,1},{3,2},{4,3},{5,4},{6,5},{7,6},{8,15},{9,8},{10,9... | collective-permute-start | bytes 196616 | tf_op jit(solution)/shard_map/ppermute | solution.py:287
  140.7 5.6 %collective-permute-start.9 = (bf16[256,128]{1,0:T(8,128)(2,1)S(1)}, bf16[256,128]{1,0:T(8,128)(2,1)S(1)}, u32[]{:S(2)}, u32[]{:S(2)}) collective-permute-start(bf16[256,128]{1,0:T(8,128)(2,1)S(1)} %slice.46), channel_id=1, source_target_pairs={{0,1},{1,2},{2,3},{3,4},{4,5},{5,6},{6,7},{7,0},{8,9},{9,10},{10,1... | collective-permute-start | bytes 196616 | tf_op jit(solution)/shard_map/ppermute | solution.py:286
  (4 other events, 3.0 us)

commit v2 on v1

--- a/solution.py
+++ b/solution.py
@@ -16,7 +16,9 @@
 NC = 32
 COLS = 768
 ROWS = 256
-YCHUNK = 4
+HALF = 128
+YCHUNK = 32
+ZROW = 104
 PICK = 512
 
 
@@ -64,10 +66,11 @@
     return jnp.dot(left, right, preferred_element_type=jnp.float32)
 
 
-def field_kernel(val_ref, cond_ref, vs_ref, cs_ref, tz_ref, ty_ref, out_ref, zs_ref):
+def field_kernel(val_ref, cond_ref, vs_ref, cs_ref, tz_ref, ty_ref, out_ref, zs_ref, pair_ref):
     points = YCHUNK * GRID
-
-    def z_step(step, carry):
+    steps = GRID // YCHUNK
+
+    def pairs(step, slot):
         at = pl.multiple_of(step * points, points)
         val = jnp.concatenate(
             [val_ref[v, :, pl.ds(at, points)].astype(jnp.float32) for v in range(NV)], axis=0
@@ -78,32 +81,45 @@
         cond = dot(cond_ref[0, 0, pl.ds(at, points), :], cs_ref[...])
         val_re, val_im = spread[:, :128], spread[:, 128:]
         cond_re, cond_im = cond[:, :128], cond[:, 128:]
-        pair_re = (val_re * cond_re + val_im * cond_im).astype(jnp.bfloat16)
-        pair_im = (val_re * cond_im - val_im * cond_re).astype(jnp.bfloat16)
+        pair_ref[slot, 0] = (val_re * cond_re + val_im * cond_im).astype(jnp.bfloat16)
+        pair_ref[slot, 1] = (val_re * cond_im - val_im * cond_re).astype(jnp.bfloat16)
+
+    def z_pass(step, slot):
         for y in range(0, YCHUNK, 2):
             rhs = jnp.concatenate(
                 [
                     jnp.concatenate(
-                        [pair_re[(y + u) * GRID : (y + u + 1) * GRID] for u in range(2)], axis=1
-                    ),
-                    jnp.concatenate(
-                        [pair_im[(y + u) * GRID : (y + u + 1) * GRID] for u in range(2)], axis=1
-                    ),
+                        [pair_ref[slot, i, (y + u) * GRID : (y + u + 1) * GRID] for u in range(2)],
+                        axis=1,
+                    )
+                    for i in range(2)
                 ],
                 axis=0,
             )
             z_out = dot(tz_ref[...], rhs)
             for u in range(2):
-                zs_ref[pl.ds(step * YCHUNK + y + u, 2 * BOX, stride=GRID), :] = z_out[
+                zs_ref[pl.ds(step * YCHUNK + y + u, 2 * BOX, stride=ZROW), :] = z_out[
                     :, u * 128 : (u + 1) * 128
                 ]
+
+    def body(step, carry):
+        z_pass(step - 1, (step - 1) % 2)
+        pairs(step, step % 2)
         return carry
 
-    lax.fori_loop(0, GRID // YCHUNK, z_step, 0)
+    pairs(0, 0)
+    lax.fori_loop(1, steps, body, 0)
+    z_pass(steps - 1, (steps - 1) % 2)
     for fz in range(0, BOX, 2):
         rhs = jnp.concatenate(
             [
-                zs_ref[(fz + u) * 2 * GRID : (fz + u + 1) * 2 * GRID, :].astype(jnp.bfloat16)
+                jnp.concatenate(
+                    [
+                        zs_ref[pl.ds(((fz + u) * 2 + i) * ZROW, GRID), :].astype(jnp.bfloat16)
+                        for i in range(2)
+                    ],
+                    axis=0,
+                )
                 for u in range(2)
             ],
             axis=1,
@@ -131,8 +147,11 @@
         ],
         out_specs=pl.BlockSpec((1, COLS, 256), lambda a: (a, 0, 0)),
         out_shape=jax.ShapeDtypeStruct((planes, COLS, 256), jnp.bfloat16),
-        scratch_shapes=[pltpu.VMEM((2 * BOX * GRID, 128), jnp.float32)],
-        compiler_params=pltpu.CompilerParams(vmem_limit_bytes=40 * 2**20),
+        scratch_shapes=[
+            pltpu.VMEM((2 * BOX * ZROW, 128), jnp.float32),
+            pltpu.VMEM((2, 2, YCHUNK * GRID, 128), jnp.bfloat16),
+        ],
+        compiler_params=pltpu.CompilerParams(vmem_limit_bytes=60 * 2**20),
         cost_estimate=pl.CostEstimate(
             flops=4_000_000_000, bytes_accessed=9_000_000, transcendentals=0
         ),
@@ -166,10 +185,10 @@
 
 
 def pick(column, freq, field, x_table):
-    planes = field.shape[0]
+    planes, count = field.shape[0], column.shape[0]
     return pl.pallas_call(
         pick_kernel,
-        grid=(NG // PICK,),
+        grid=(count // PICK,),
         in_specs=[
             pl.BlockSpec((PICK, 128), lambda g: (g, 0)),
             pl.BlockSpec((PICK, 128), lambda g: (g, 0)),
@@ -177,35 +196,30 @@
             pl.BlockSpec((128, planes * 256), lambda g: (0, 0)),
         ],
         out_specs=pl.BlockSpec((PICK, 128), lambda g: (g, 0)),
-        out_shape=jax.ShapeDtypeStruct((NG, 128), jnp.bfloat16),
-        compiler_params=pltpu.CompilerParams(vmem_limit_bytes=40 * 2**20),
+        out_shape=jax.ShapeDtypeStruct((count, 128), jnp.bfloat16),
+        compiler_params=pltpu.CompilerParams(vmem_limit_bytes=60 * 2**20),
         cost_estimate=pl.CostEstimate(
             flops=8_000_000_000, bytes_accessed=6_000_000, transcendentals=0
         ),
     )(column, freq, field, x_table)
 
 
-def chi_kernel(row_a_ref, row_b_ref, *refs):
-    a_refs, b_refs = refs[:10], refs[10:12]
-    weight_ref, out_ref, wa_ref = refs[12:]
-    lane = lax.broadcasted_iota(jnp.int32, (ROWS, 128), 1)
+def chi_kernel(half_ref, row_ref, own_ref, other_ref, near_ref, far_ref, weight_ref, out_ref, wa_ref):
+    lane = lax.broadcasted_iota(jnp.int32, (HALF, 128), 1)
     sign = jnp.where(lane < 64, 1.0, -1.0)
+    for h, ref in enumerate((own_ref, other_ref)):
+        for row in range(ref.shape[0]):
+            weighted = ref[row].astype(jnp.float32) * weight_ref[row : row + 1, :]
+            weighted = weighted.astype(jnp.bfloat16).astype(jnp.float32)
+            wa_ref[row, (2 * h) * HALF : (2 * h + 1) * HALF] = weighted.astype(jnp.bfloat16)
+            wa_ref[row, (2 * h + 1) * HALF : (2 * h + 2) * HALF] = (
+                pltpu.roll(weighted, 64, 1) * sign
+            ).astype(jnp.bfloat16)
+    total = jnp.zeros((4 * HALF, ROWS), jnp.float32)
     place = 0
-    for ref in a_refs:
-        for part in range(ref.shape[0] // ROWS):
-            row = row_a_ref[place]
-            piece = ref[part * ROWS : (part + 1) * ROWS, :].astype(jnp.float32)
-            weighted = (piece * weight_ref[pl.ds(row, 1), :]).astype(jnp.bfloat16).astype(jnp.float32)
-            wa_ref[row, :ROWS, :] = weighted.astype(jnp.bfloat16)
-            wa_ref[row, ROWS:, :] = (pltpu.roll(weighted, 64, 1) * sign).astype(jnp.bfloat16)
-            place += 1
-    total = jnp.zeros((2 * ROWS, ROWS), jnp.float32)
-    place = 0
-    for ref in b_refs:
+    for ref in (near_ref, far_ref):
         for part in range(0, ref.shape[0] // ROWS, 2):
-            left = jnp.concatenate(
-                [wa_ref[row_b_ref[place]], wa_ref[row_b_ref[place + 1]]], axis=1
-            )
+            left = jnp.concatenate([wa_ref[row_ref[place]], wa_ref[row_ref[place + 1]]], axis=1)
             right = jnp.concatenate(
                 [ref[(part + u) * ROWS : (part + u + 1) * ROWS, :] for u in range(2)], axis=1
             )
@@ -213,24 +227,26 @@
                 left, right, (((1,), (1,)), ((), ())), preferred_element_type=jnp.float32
             )
             place += 2
-    out_ref[:, 0, :] = total[:ROWS]
-    out_ref[:, 1, :] = total[ROWS:]
-
-
-def contract(row_a, row_b, a_parts, b_parts, weight):
+    for h in range(2):
+        at = pl.multiple_of((half_ref[0] + h) % 2 * HALF, HALF)
+        for i in range(2):
+            out_ref[pl.ds(at, HALF), i, :] = total[(2 * h + i) * HALF : (2 * h + i + 1) * HALF]
+
+
+def contract(half, row, own, other, near, far, weight):
     smem = pl.BlockSpec(memory_space=pltpu.SMEM)
     vmem = pl.BlockSpec(memory_space=pltpu.VMEM)
     return pl.pallas_call(
         chi_kernel,
-        in_specs=[smem, smem] + [vmem] * (len(a_parts) + len(b_parts) + 1),
+        in_specs=[smem, smem] + [vmem] * 5,
         out_specs=vmem,
         out_shape=jax.ShapeDtypeStruct((ROWS, 2, ROWS), jnp.float32),
-        scratch_shapes=[pltpu.VMEM((16, 2 * ROWS, 128), jnp.bfloat16)],
+        scratch_shapes=[pltpu.VMEM((16, 4 * HALF, 128), jnp.bfloat16)],
         compiler_params=pltpu.CompilerParams(vmem_limit_bytes=40 * 2**20),
         cost_estimate=pl.CostEstimate(
             flops=600_000_000, bytes_accessed=4_000_000, transcendentals=0
         ),
-    )(row_a, row_b, *a_parts, *b_parts, weight)
+    )(half, row, own, other, near, far, weight)
 
 
 def ka_route(move):
@@ -268,25 +284,12 @@
     return [block, other], jnp.stack(places).astype(jnp.int32)
 
 
-def gather_rows(rho):
-    own = lax.ppermute(
-        rho, ("ka", "fft"), [(i * 16 + j, j * 16 + i) for i in range(16) for j in range(16)]
-    )
-    across = lax.ppermute(own, "fft", fft_route(lambda y, z: (y + 1, z)))
-    block = jnp.concatenate([own, across])
-    spot = lax.axis_index("fft")
-    y, z = spot // 8, spot % 8
-    parts, places = [own, across], [(y, z), (y + 1, z)]
-    up = down = block
-    for t in range(1, 4):
-        up = lax.ppermute(up, "fft", fft_route(lambda y, z: (y, z + 1)))
-        down = lax.ppermute(down, "fft", fft_route(lambda y, z: (y, z - 1)))
-        parts += [up, down]
-        places += [(y, z - t), (y + 1, z - t), (y, z + t), (y + 1, z + t)]
-    parts.append(lax.ppermute(up[:ROWS], "fft", fft_route(lambda y, z: (y, z + 1))))
-    parts.append(lax.ppermute(down[ROWS:], "fft", fft_route(lambda y, z: (y, z - 1))))
-    places += [(y, z + 4), (y + 1, z + 4)]
-    return parts, jnp.stack([(a % 2) * 8 + b % 8 for a, b in places]).astype(jnp.int32)
+def gather_rows(own):
+    halves = own.reshape(2, 1, HALF, 128)
+    copies = jnp.broadcast_to(halves, (2, 8, HALF, 128)).reshape(16, HALF, 128)
+    mine = lax.all_to_all(copies, "fft", 0, 0)
+    other = lax.ppermute(mine, "fft", fft_route(lambda y, z: (y + 1, z)))
+    return mine, other
 
 
 def shards(psi_val, psi_cond, e_val, e_cond, occ_val, occ_cond, umklapp, sphere):
@@ -310,10 +313,17 @@
     )
     x_table = jnp.broadcast_to(both[..., None], (128, planes, 2, 2, 64)).reshape(128, planes * 256)
     x_table = x_table.astype(jnp.bfloat16)
-    plane = sphere % (BOX * BOX)
-    column = (plane % BOX) * 32 + plane // BOX
-    column = jnp.broadcast_to(column[:, None], (NG, 128))
-    freq = jnp.broadcast_to((sphere // (BOX * BOX))[:, None], (NG, 128))
+    half = x_block // 8
+    blocks = sphere.reshape(16, 2, HALF)
+
+    def places(part):
+        index = lax.dynamic_index_in_dim(blocks, part, 1, keepdims=False).reshape(NG // 2)
+        plane = index % (BOX * BOX)
+        column = (plane % BOX) * 32 + plane // BOX
+        freq = index // (BOX * BOX)
+        return [jnp.broadcast_to(a[:, None], (NG // 2, 128)) for a in (column, freq)]
+
+    away, home = places(1 - half), places(half)
 
     weight = (occ_val[:, :, None] - jnp.roll(occ_cond, -step_q, 0)[:, None, :]).astype(
         jnp.float32
@@ -321,13 +331,23 @@
     weight = jnp.roll(weight.reshape(count_k, NV * NC), step_q, 0)
     weight = jnp.concatenate([weight, weight], axis=1)
 
+    val, away, home, x_table, weight = lax.optimization_barrier(
+        (val, away, home, x_table, weight)
+    )
     field = fields(val, psi_cond)
-    share = pick(column, freq, field, x_table)
-    spread = lax.all_to_all(share.reshape(16, ROWS, 128), "fft", 0, 0)
-    rho = spread.astype(jnp.float32).sum(0).astype(jnp.bfloat16)
-    b_parts, row_b = gather_columns(rho)
-    a_parts, row_a = gather_rows(rho)
-    return contract(row_a, row_b, a_parts, b_parts, weight)
+    sent = pick(away[0], away[1], field, x_table)
+    came = lax.ppermute(sent, "fft", fft_route(lambda y, z: (y + 1, z)))
+    kept = pick(home[0], home[1], field, x_table)
+    share = (kept.astype(jnp.float32) + came.astype(jnp.float32)).astype(jnp.bfloat16)
+    spread = lax.all_to_all(share.reshape(16, HALF, 128), "fft", 0, 0)
+    rho = spread.reshape(2, 8, HALF, 128).astype(jnp.float32).sum(1).astype(jnp.bfloat16)
+    rho = rho.reshape(ROWS, 128)
+    turned = lax.ppermute(
+        rho, ("ka", "fft"), [(i * 16 + j, j * 16 + i) for i in range(16) for j in range(16)]
+    )
+    (near, far), row_b = gather_columns(rho)
+    mine, other = gather_rows(turned)
+    return contract(half[None].astype(jnp.int32), row_b, mine, other, near, far, weight)
 
 
 def solution(mesh):

time: 149 us -> 135 us (0.906)
  the two profiles are of different devices: /device:TPU:10 before, /device:TPU:1 now
where the time goes in v2:
time: 135 us
  starting transfers between devices  35.2 us (26%)
  Pallas kernels  30.6 us (23%)
  waiting for transfers between devices  29.8 us (22%)
  blocking collectives  21.8 us (16%)
  local copies, waits for them, and re-layouts  12.9 us (10%)
  other arithmetic  4.06 us (3%)
    all_to_all x1, blocking collectives, shards(): spread = lax.all_to_all(share.reshape(16, HALF, 128), 'fft', 0, 0)  21.8 us
    pallas_call x1, Pallas kernels, fields(): pl.pallas_call(field_kernel, grid=(planes,), in_specs=[pl.BlockSpec((NV,...  15.2 us
    pallas_call x2, Pallas kernels, pick(): pl.pallas_call(pick_kernel, grid=(count // PICK,), in_specs=[pl.BlockSpec...  12.9 us
    ppermute x1, waiting for transfers between devices, gather_rows(): other = lax.ppermute(mine, 'fft', fft_route(lambda y, z: (y + 1, z)))  12 us
    all_to_all x1, starting transfers between devices, gather_rows(): mine = lax.all_to_all(copies, 'fft', 0, 0)  9.09 us
    ppermute x1, starting transfers between devices, shards(): lax.ppermute(rho, ('ka', 'fft'), [(i * 16 + j, j * 16 + i) for i in range...  7.08 us
    ppermute x3, waiting for transfers between devices, gather_columns(): lax.ppermute(block, 'ka', ka_route(lambda y, x, c, s=s: (y, x + s, c)))  6.78 us
    ppermute x1, starting transfers between devices, gather_columns(): other = lax.ppermute(block, 'ka', ka_route(lambda y, x, c: (y, x, c + 1)))  6.58 us
  transfers between devices with their start and end apart: 10, of which 8 were waited for; matrix products, arithmetic and copies ran while one was open for 6% of the time, Pallas kernels for 5%

profile of v2, /device:TPU:1, one launch (start us, length us, event | category | flops | bytes accessed | tf_op | source)
XLA Modules:
  0.0 134.7 jit_solution(5516273980639230308)
XLA Ops:
  0.0 3.6 %collective-permute-start = (bf16[1,2,4,27648]{3,2,1,0:T(4,128)(2,1)}, bf16[1,2,4,27648]{3,2,1,0:T(4,128)(2,1)S(1)}, u32[]{:S(2)}, u32[]{:S(2)}) collective-permute-start(bf16[1,2,4,27648]{3,2,1,0:T(4,128)(2,1)} %param.12), channel_id=1, source_target_pairs={{0,64},{16,80},{32,96},{48,112},{64,128},{80,144},{96,160},{112,17... | collective-permute-start | bytes 1327112 | tf_op jit(solution)/shard_map/ppermute | solution.py:301
  8.0 1.2 dynamic_slice.13
  12.1 2.1 %collective-permute-done = bf16[1,2,4,27648]{3,2,1,0:T(4,128)(2,1)S(1)} collective-permute-done((bf16[1,2,4,27648]{3,2,1,0:T(4,128)(2,1)}, bf16[1,2,4,27648]{3,2,1,0:T(4,128)(2,1)S(1)}, u32[]{:S(2)}, u32[]{:S(2)}) %collective-permute-start) | collective-permute-done | bytes 442400 | tf_op jit(solution)/shard_map/ppermute | solution.py:301
  14.2 1.3 broadcast_in_dim.20.fx_ref
  15.5 1.3 broadcast_in_dim.19.col_ref
  16.9 1.3 broadcast_in_dim.17.col_ref
  18.2 1.3 broadcast_in_dim.18.fx_ref
  20.4 15.2 %shard_map.118.y_ref = bf16[3,768,256]{2,1,0:T(8,128)(2,1)} custom-call(bf16[2,4,27648]{2,1,0:T(4,128)(2,1)} %bitcast.52, bf16[1,3,9216,128]{3,2,1,0:T(8,128)(2,1)} %cond_ref.1, bf16[8,256]{1,0:T(8,128)(2,1)} %constant.276.clone.vs_ref, bf16[128,256]{1,0:T(8,128)(2,1)} %constant.277.clone.cs_ref, bf16[48,192]{1,0:T(8,128)(2,1)} %constant.278.clone.tz_ref, ...), custom_call_target="tpu_custom_call" | custom-call | flops 4000000000 | bytes 9000000 | tf_op jit(solution)/shard_map/pallas_call | solution.py:137
  35.6 6.5 %shard_map.120 = bf16[2048,128]{1,0:T(8,128)(2,1)} custom-call(s32[2048,128]{1,0:T(8,128)} %broadcast_in_dim.17.col_ref, s32[2048,128]{1,0:T(8,128)} %broadcast_in_dim.18.fx_ref, bf16[3,768,256]{2,1,0:T(8,128)(2,1)} %shard_map.118.y_ref, bf16[128,768]{1,0:T(8,128)(2,1)} %copy.21.xt_ref), custom_call_target="tpu_custom_call" | custom-call | flops 8000000000 | bytes 6000000 | tf_op jit(solution)/shard_map/pallas_call | solution.py:189
  42.1 3.1 %collective-permute-start.1 = (bf16[2048,128]{1,0:T(8,128)(2,1)}, bf16[2048,128]{1,0:T(8,128)(2,1)S(1)}, u32[]{:S(2)}, u32[]{:S(2)}) collective-permute-start(bf16[2048,128]{1,0:T(8,128)(2,1)} %shard_map.120), channel_id=1, source_target_pairs={{0,8},{1,9},{2,10},{3,11},{4,12},{5,13},{6,14},{7,15},{8,0},{9,1},... | collective-permute-start | bytes 1572872 | tf_op jit(solution)/shard_map/ppermute | solution.py:339
  45.2 6.4 %shard_map.119 = bf16[2048,128]{1,0:T(8,128)(2,1)} custom-call(s32[2048,128]{1,0:T(8,128)} %broadcast_in_dim.19.col_ref, s32[2048,128]{1,0:T(8,128)} %broadcast_in_dim.20.fx_ref, bf16[3,768,256]{2,1,0:T(8,128)(2,1)} %shard_map.118.y_ref, bf16[128,768]{1,0:T(8,128)(2,1)} %copy.21.xt_ref), custom_call_target="tpu_custom_call" | custom-call | flops 8000000000 | bytes 6000000 | tf_op jit(solution)/shard_map/pallas_call | solution.py:189
  51.6 4.0 %collective-permute-done.1 = bf16[2048,128]{1,0:T(8,128)(2,1)S(1)} collective-permute-done((bf16[2048,128]{1,0:T(8,128)(2,1)}, bf16[2048,128]{1,0:T(8,128)(2,1)S(1)}, u32[]{:S(2)}, u32[]{:S(2)}) %collective-permute-start.1) | collective-permute-done | bytes 524320 | tf_op jit(solution)/shard_map/ppermute | solution.py:339
  56.8 21.8 %all_to_all.10 = bf16[16,128,128]{2,1,0:T(8,128)(2,1)S(1)} all-to-all(bf16[16,128,128]{2,1,0:T(8,128)(2,1)S(1)} %bitcast.39), channel_id=1, replica_groups=mesh['ka'=16,'fft'=16] {'fft'}, dimensions={0} | all-to-all | bytes 1048576 | tf_op jit(solution)/shard_map/all_to_all | solution.py:342
  78.7 7.1 %collective-permute-start.2 = (bf16[256,128]{1,0:T(8,128)(2,1)S(1)}, bf16[256,128]{1,0:T(8,128)(2,1)S(1)}, u32[]{:S(2)}, u32[]{:S(2)}) collective-permute-start(bf16[256,128]{1,0:T(8,128)(2,1)S(1)} %bitcast.41), channel_id=1, source_target_pairs={{0,0},{1,16},{2,32},{3,48},{4,64},{5,80},{6,96},{7,112},{8,128},{9... | collective-permute-start | bytes 196616 | tf_op jit(solution)/shard_map/ppermute | solution.py:345
  85.8 1.9 %collective-permute-done.2 = bf16[256,128]{1,0:T(8,128)(2,1)S(1)} collective-permute-done((bf16[256,128]{1,0:T(8,128)(2,1)S(1)}, bf16[256,128]{1,0:T(8,128)(2,1)S(1)}, u32[]{:S(2)}, u32[]{:S(2)}) %collective-permute-start.2) | collective-permute-done | bytes 65568 | tf_op jit(solution)/shard_map/ppermute | solution.py:345
  88.6 9.1 %all-to-all-start.1 = ((bf16[16,128,128]{2,1,0:T(8,128)(2,1)}), bf16[16,128,128]{2,1,0:T(8,128)(2,1)S(1)}, u32[]{:S(2)}, u32[]{:S(2)}) async-start(bf16[16,128,128]{2,1,0:T(8,128)(2,1)} %bitcast.29), calls=%async_computation.1 | async-start | bytes 1048576 | tf_op jit(solution)/shard_map/all_to_all | solution.py:290
  97.7 2.5 %collective-permute-start.4 = (bf16[256,128]{1,0:T(8,128)(2,1)S(1)}, bf16[256,128]{1,0:T(8,128)(2,1)S(1)}, u32[]{:S(2)}, u32[]{:S(2)}) collective-permute-start(bf16[256,128]{1,0:T(8,128)(2,1)S(1)} %bitcast.42), channel_id=1, source_target_pairs={{0,128},{16,144},{32,160},{48,176},{64,192},{80,208},{96,224},{112... | collective-permute-start | bytes 196616 | tf_op jit(solution)/shard_map/ppermute | solution.py:269
  100.3 2.2 %collective-permute-done.4 = bf16[256,128]{1,0:T(8,128)(2,1)S(1)} collective-permute-done((bf16[256,128]{1,0:T(8,128)(2,1)S(1)}, bf16[256,128]{1,0:T(8,128)(2,1)S(1)}, u32[]{:S(2)}, u32[]{:S(2)}) %collective-permute-start.4) | collective-permute-done | bytes 65568 | tf_op jit(solution)/shard_map/ppermute | solution.py:269
  102.6 2.7 %collective-permute-start.7 = (bf16[512,128]{1,0:T(8,128)(2,1)S(1)}, bf16[512,128]{1,0:T(8,128)(2,1)S(1)}, u32[]{:S(2)}, u32[]{:S(2)}) collective-permute-start(bf16[512,128]{1,0:T(8,128)(2,1)S(1)} %pad_maximum_fusion), channel_id=1, source_target_pairs={{0,96},{16,112},{32,0},{48,16},{64,32},{80,48},{96,64},{112,80},{1... | collective-permute-start | bytes 393224 | tf_op jit(solution)/shard_map/ppermute | solution.py:272
  105.2 2.6 %collective-permute-done.5 = bf16[512,128]{1,0:T(8,128)(2,1)S(1)} collective-permute-done((bf16[512,128]{1,0:T(8,128)(2,1)S(1)}, bf16[512,128]{1,0:T(8,128)(2,1)S(1)}, u32[]{:S(2)}, u32[]{:S(2)}) %collective-permute-start.5) | collective-permute-done | bytes 131104 | tf_op jit(solution)/shard_map/ppermute | solution.py:272
  107.9 4.2 %collective-permute-done.6 = bf16[512,128]{1,0:T(8,128)(2,1)S(1)} collective-permute-done((bf16[512,128]{1,0:T(8,128)(2,1)S(1)}, bf16[512,128]{1,0:T(8,128)(2,1)S(1)}, u32[]{:S(2)}, u32[]{:S(2)}) %collective-permute-start.6) | collective-permute-done | bytes 131104 | tf_op jit(solution)/shard_map/ppermute | solution.py:272
  112.1 6.6 %collective-permute-start.8 = (bf16[2048,128]{1,0:T(8,128)(2,1)S(1)}, bf16[2048,128]{1,0:T(8,128)(2,1)S(1)}, u32[]{:S(2)}, u32[]{:S(2)}) collective-permute-start(bf16[2048,128]{1,0:T(8,128)(2,1)S(1)} %constant_dynamic-update-slice_fusion.near_ref), channel_id=1, source_target_pairs={{0,16},{16,0},{32,48},{48,32},{64,80},{80,64},{96,112},{112,96},{1... | collective-permute-start | bytes 1572872 | tf_op jit(solution)/shard_map/ppermute | solution.py:275
  120.2 12.0 %collective-permute-done.3.other_ref = bf16[16,128,128]{2,1,0:T(8,128)(2,1)S(1)} collective-permute-done((bf16[16,128,128]{2,1,0:T(8,128)(2,1)S(1)}, bf16[16,128,128]{2,1,0:T(8,128)(2,1)S(1)}, u32[]{:S(2)}, u32[]{:S(2)}) %collective-permute-start.3) | collective-permute-done | bytes 524320 | tf_op jit(solution)/shard_map/ppermute | solution.py:291
  132.2 2.5 %shard_map.121 = f32[256,2,256]{2,1,0:T(2,128)} custom-call(s32[1]{0:T(128)} %bitcast.half_ref, s32[16]{0:T(128)S(1)} %stack.71.row_ref, bf16[16,128,128]{2,1,0:T(8,128)(2,1)S(1)} %all-to-all-done.1.own_ref, bf16[16,128,128]{2,1,0:T(8,128)(2,1)S(1)} %collective-permute-done.3.other_ref, bf16[2048,128]{1,0:T(8,128)(2,1)S(1)} %constant_dynamic-update-slice_fusion.near_ref, ...), custom_call_target="tpu_custom_call" | custom-call | flops 600000000 | bytes 4000000 | tf_op jit(solution)/shard_map/pallas_call | solution.py:239
  (41 shorter events, 12.0 us)
Async XLA Ops:
  0.0 14.2 %collective-permute-start = (bf16[1,2,4,27648]{3,2,1,0:T(4,128)(2,1)}, bf16[1,2,4,27648]{3,2,1,0:T(4,128)(2,1)S(1)}, u32[]{:S(2)}, u32[]{:S(2)}) collective-permute-start(bf16[1,2,4,27648]{3,2,1,0:T(4,128)(2,1)} %param.12), channel_id=1, source_target_pairs={{0,64},{16,80},{32,96},{48,112},{64,128},{80,144},{96,160},{112,17... | collective-permute-start | bytes 1327112 | tf_op jit(solution)/shard_map/ppermute | solution.py:301
  14.2 6.1 %copy-start = (bf16[1,2,4,27648]{3,2,1,0:T(4,128)(2,1)}, bf16[1,2,4,27648]{3,2,1,0:T(4,128)(2,1)S(1)}, u32[]{:S(2)}) copy-start(bf16[1,2,4,27648]{3,2,1,0:T(4,128)(2,1)S(1)} %collective-permute-done) | copy-start | bytes 1327108
  42.1 13.5 %collective-permute-start.1 = (bf16[2048,128]{1,0:T(8,128)(2,1)}, bf16[2048,128]{1,0:T(8,128)(2,1)S(1)}, u32[]{:S(2)}, u32[]{:S(2)}) collective-permute-start(bf16[2048,128]{1,0:T(8,128)(2,1)} %shard_map.120), channel_id=1, source_target_pairs={{0,8},{1,9},{2,10},{3,11},{4,12},{5,13},{6,14},{7,15},{8,0},{9,1},... | collective-permute-start | bytes 1572872 | tf_op jit(solution)/shard_map/ppermute | solution.py:339
  78.7 9.0 %collective-permute-start.2 = (bf16[256,128]{1,0:T(8,128)(2,1)S(1)}, bf16[256,128]{1,0:T(8,128)(2,1)S(1)}, u32[]{:S(2)}, u32[]{:S(2)}) collective-permute-start(bf16[256,128]{1,0:T(8,128)(2,1)S(1)} %bitcast.41), channel_id=1, source_target_pairs={{0,0},{1,16},{2,32},{3,48},{4,64},{5,80},{6,96},{7,112},{8,128},{9... | collective-permute-start | bytes 196616 | tf_op jit(solution)/shard_map/ppermute | solution.py:345
  88.6 30.0 %all-to-all-start.1 = ((bf16[16,128,128]{2,1,0:T(8,128)(2,1)}), bf16[16,128,128]{2,1,0:T(8,128)(2,1)S(1)}, u32[]{:S(2)}, u32[]{:S(2)}) async-start(bf16[16,128,128]{2,1,0:T(8,128)(2,1)} %bitcast.29), calls=%async_computation.1 | async-start | bytes 1048576 | tf_op jit(solution)/shard_map/all_to_all | solution.py:290
  97.7 4.7 %collective-permute-start.4 = (bf16[256,128]{1,0:T(8,128)(2,1)S(1)}, bf16[256,128]{1,0:T(8,128)(2,1)S(1)}, u32[]{:S(2)}, u32[]{:S(2)}) collective-permute-start(bf16[256,128]{1,0:T(8,128)(2,1)S(1)} %bitcast.42), channel_id=1, source_target_pairs={{0,128},{16,144},{32,160},{48,176},{64,192},{80,208},{96,224},{112... | collective-permute-start | bytes 196616 | tf_op jit(solution)/shard_map/ppermute | solution.py:269
  102.5 5.4 %collective-permute-start.5 = (bf16[512,128]{1,0:T(8,128)(2,1)S(1)}, bf16[512,128]{1,0:T(8,128)(2,1)S(1)}, u32[]{:S(2)}, u32[]{:S(2)}) collective-permute-start(bf16[512,128]{1,0:T(8,128)(2,1)S(1)} %pad_maximum_fusion), channel_id=1, source_target_pairs={{0,32},{16,48},{32,64},{48,80},{64,96},{80,112},{96,0},{112,16},{1... | collective-permute-start | bytes 393224 | tf_op jit(solution)/shard_map/ppermute | solution.py:272
  102.6 9.5 %collective-permute-start.7 = (bf16[512,128]{1,0:T(8,128)(2,1)S(1)}, bf16[512,128]{1,0:T(8,128)(2,1)S(1)}, u32[]{:S(2)}, u32[]{:S(2)}) collective-permute-start(bf16[512,128]{1,0:T(8,128)(2,1)S(1)} %pad_maximum_fusion), channel_id=1, source_target_pairs={{0,96},{16,112},{32,0},{48,16},{64,32},{80,48},{96,64},{112,80},{1... | collective-permute-start | bytes 393224 | tf_op jit(solution)/shard_map/ppermute | solution.py:272
  105.2 6.8 %collective-permute-start.6 = (bf16[512,128]{1,0:T(8,128)(2,1)S(1)}, bf16[512,128]{1,0:T(8,128)(2,1)S(1)}, u32[]{:S(2)}, u32[]{:S(2)}) collective-permute-start(bf16[512,128]{1,0:T(8,128)(2,1)S(1)} %pad_maximum_fusion), channel_id=1, source_target_pairs={{0,64},{16,80},{32,96},{48,112},{64,0},{80,16},{96,32},{112,48},{1... | collective-permute-start | bytes 393224 | tf_op jit(solution)/shard_map/ppermute | solution.py:272
  112.1 8.1 %collective-permute-start.8 = (bf16[2048,128]{1,0:T(8,128)(2,1)S(1)}, bf16[2048,128]{1,0:T(8,128)(2,1)S(1)}, u32[]{:S(2)}, u32[]{:S(2)}) collective-permute-start(bf16[2048,128]{1,0:T(8,128)(2,1)S(1)} %constant_dynamic-update-slice_fusion.near_ref), channel_id=1, source_target_pairs={{0,16},{16,0},{32,48},{48,32},{64,80},{80,64},{96,112},{112,96},{1... | collective-permute-start | bytes 1572872 | tf_op jit(solution)/shard_map/ppermute | solution.py:275
  118.7 13.5 %collective-permute-start.3 = (bf16[16,128,128]{2,1,0:T(8,128)(2,1)S(1)}, bf16[16,128,128]{2,1,0:T(8,128)(2,1)S(1)}, u32[]{:S(2)}, u32[]{:S(2)}) collective-permute-start(bf16[16,128,128]{2,1,0:T(8,128)(2,1)S(1)} %all-to-all-done.1.own_ref), channel_id=1, source_target_pairs={{0,8},{1,9},{2,10},{3,11},{4,12},{5,13},{6,14},{7,15},{8,0},{9,1},... | collective-permute-start | bytes 1572872 | tf_op jit(solution)/shard_map/ppermute | solution.py:291

commit v3 on v2

--- a/solution.py
+++ b/solution.py
@@ -19,7 +19,7 @@
 HALF = 128
 YCHUNK = 32
 ZROW = 104
-PICK = 512
+PICK = 256
 
 
 def dft_tables():
@@ -66,7 +66,9 @@
     return jnp.dot(left, right, preferred_element_type=jnp.float32)
 
 
-def field_kernel(val_ref, cond_ref, vs_ref, cs_ref, tz_ref, ty_ref, out_ref, zs_ref, pair_ref):
+def field_kernel(
+    val_ref, cond_ref, vs_ref, cs_ref, tz_ref, ty_ref, out_ref, zs_ref, pair_ref, y_ref
+):
     points = YCHUNK * GRID
     steps = GRID // YCHUNK
 
@@ -127,9 +129,10 @@
         y_out = dot(ty_ref[...], rhs).astype(jnp.bfloat16)
         for u in range(2):
             for i in range(2):
-                out_ref[0, (fz + u) * 32 : (fz + u + 1) * 32, i * 128 : (i + 1) * 128] = y_out[
+                y_ref[(fz + u) * 32 : (fz + u + 1) * 32, i * 128 : (i + 1) * 128] = y_out[
                     i * 32 : (i + 1) * 32, u * 128 : (u + 1) * 128
                 ]
+    out_ref[0] = y_ref[...].T
 
 
 def fields(val, cond):
@@ -145,11 +148,12 @@
             pl.BlockSpec((2 * BOX, 2 * GRID), lambda a: (0, 0)),
             pl.BlockSpec((64, 2 * GRID), lambda a: (0, 0)),
         ],
-        out_specs=pl.BlockSpec((1, COLS, 256), lambda a: (a, 0, 0)),
-        out_shape=jax.ShapeDtypeStruct((planes, COLS, 256), jnp.bfloat16),
+        out_specs=pl.BlockSpec((1, 256, COLS), lambda a: (a, 0, 0)),
+        out_shape=jax.ShapeDtypeStruct((planes, 256, COLS), jnp.bfloat16),
         scratch_shapes=[
             pltpu.VMEM((2 * BOX * ZROW, 128), jnp.float32),
             pltpu.VMEM((2, 2, YCHUNK * GRID, 128), jnp.bfloat16),
+            pltpu.VMEM((COLS, 256), jnp.bfloat16),
         ],
         compiler_params=pltpu.CompilerParams(vmem_limit_bytes=60 * 2**20),
         cost_estimate=pl.CostEstimate(
@@ -159,60 +163,58 @@
 
 
 def pick_kernel(col_ref, fx_ref, y_ref, xt_ref, out_ref):
-    lane = lax.broadcasted_iota(jnp.int32, (PICK, 128), 1)
-    column = col_ref[...]
-    chosen = jnp.concatenate(
-        [
-            jnp.where(column == lane + 128 * t, 1.0, 0.0).astype(jnp.bfloat16)
-            for t in range(COLS // 128)
-        ],
-        axis=1,
-    )
-    freq = jnp.where(fx_ref[...] == lane, 1.0, 0.0).astype(jnp.bfloat16)
-    real = jnp.zeros((PICK, 128), jnp.float32)
-    imag = jnp.zeros((PICK, 128), jnp.float32)
-    for a in range(y_ref.shape[0]):
-        got = dot(chosen, y_ref[a])
-        phase = dot(freq, xt_ref[:, a * 256 : (a + 1) * 256])
-        cosine, sine = phase[:, :128], phase[:, 128:]
-        got_re, got_im = got[:, :128], got[:, 128:]
-        real = real + cosine * got_re + sine * got_im
-        imag = imag + cosine * got_im - sine * got_re
-    real = real + pltpu.roll(real, 64, 1)
-    imag = imag + pltpu.roll(imag, 64, 1)
-    scale = 1.0 / (GRID * math.sqrt(GRID))
-    out_ref[...] = (jnp.where(lane < 64, real, imag) * scale).astype(jnp.bfloat16)
+    planes = y_ref.shape[0] // 256
+
+    def tile(step, carry):
+        at = pl.multiple_of(step * PICK, PICK)
+        spot = lax.broadcasted_iota(jnp.int32, (COLS, PICK), 0)
+        chosen = jnp.where(col_ref[:, pl.ds(at, PICK)] == spot, 1.0, 0.0).astype(jnp.bfloat16)
+        freq = jnp.where(fx_ref[:, pl.ds(at, PICK)] == spot[:32], 1.0, 0.0).astype(jnp.bfloat16)
+        phase = dot(xt_ref[...], freq)
+        got = dot(y_ref[...], chosen)
+        real = jnp.zeros((64, PICK), jnp.float32)
+        imag = jnp.zeros((64, PICK), jnp.float32)
+        for a in range(planes):
+            for p in range(2):
+                cosine = phase[a * 2 + p : a * 2 + p + 1]
+                sine = phase[8 + a * 2 + p : 9 + a * 2 + p]
+                got_re = got[a * 256 + p * 64 : a * 256 + (p + 1) * 64]
+                got_im = got[a * 256 + 128 + p * 64 : a * 256 + 128 + (p + 1) * 64]
+                real = real + cosine * got_re + sine * got_im
+                imag = imag + cosine * got_im - sine * got_re
+        scale = 1.0 / (GRID * math.sqrt(GRID))
+        both = (jnp.concatenate([real, imag], axis=0) * scale).astype(jnp.bfloat16)
+        out_ref[pl.ds(at, PICK), :] = both.T
+        return carry
+
+    lax.fori_loop(0, out_ref.shape[0] // PICK, tile, 0)
 
 
 def pick(column, freq, field, x_table):
-    planes, count = field.shape[0], column.shape[0]
+    count = column.shape[1]
+    vmem = pl.BlockSpec(memory_space=pltpu.VMEM)
     return pl.pallas_call(
         pick_kernel,
-        grid=(count // PICK,),
-        in_specs=[
-            pl.BlockSpec((PICK, 128), lambda g: (g, 0)),
-            pl.BlockSpec((PICK, 128), lambda g: (g, 0)),
-            pl.BlockSpec((planes, COLS, 256), lambda g: (0, 0, 0)),
-            pl.BlockSpec((128, planes * 256), lambda g: (0, 0)),
-        ],
-        out_specs=pl.BlockSpec((PICK, 128), lambda g: (g, 0)),
+        in_specs=[vmem] * 4,
+        out_specs=vmem,
         out_shape=jax.ShapeDtypeStruct((count, 128), jnp.bfloat16),
-        compiler_params=pltpu.CompilerParams(vmem_limit_bytes=60 * 2**20),
+        compiler_params=pltpu.CompilerParams(vmem_limit_bytes=40 * 2**20),
         cost_estimate=pl.CostEstimate(
-            flops=8_000_000_000, bytes_accessed=6_000_000, transcendentals=0
+            flops=3_000_000_000, bytes_accessed=2_000_000, transcendentals=0
         ),
     )(column, freq, field, x_table)
 
 
-def chi_kernel(half_ref, row_ref, own_ref, other_ref, near_ref, far_ref, weight_ref, out_ref, wa_ref):
+def chi_kernel(half_ref, row_a_ref, row_ref, own_ref, other_ref, near_ref, far_ref, weight_ref, out_ref, wa_ref):
     lane = lax.broadcasted_iota(jnp.int32, (HALF, 128), 1)
     sign = jnp.where(lane < 64, 1.0, -1.0)
     for h, ref in enumerate((own_ref, other_ref)):
         for row in range(ref.shape[0]):
-            weighted = ref[row].astype(jnp.float32) * weight_ref[row : row + 1, :]
+            k_row = row_a_ref[row]
+            weighted = ref[row].astype(jnp.float32) * weight_ref[pl.ds(k_row, 1), :]
             weighted = weighted.astype(jnp.bfloat16).astype(jnp.float32)
-            wa_ref[row, (2 * h) * HALF : (2 * h + 1) * HALF] = weighted.astype(jnp.bfloat16)
-            wa_ref[row, (2 * h + 1) * HALF : (2 * h + 2) * HALF] = (
+            wa_ref[k_row, (2 * h) * HALF : (2 * h + 1) * HALF] = weighted.astype(jnp.bfloat16)
+            wa_ref[k_row, (2 * h + 1) * HALF : (2 * h + 2) * HALF] = (
                 pltpu.roll(weighted, 64, 1) * sign
             ).astype(jnp.bfloat16)
     total = jnp.zeros((4 * HALF, ROWS), jnp.float32)
@@ -233,12 +235,12 @@
             out_ref[pl.ds(at, HALF), i, :] = total[(2 * h + i) * HALF : (2 * h + i + 1) * HALF]
 
 
-def contract(half, row, own, other, near, far, weight):
+def contract(half, row_a, row, own, other, near, far, weight):
     smem = pl.BlockSpec(memory_space=pltpu.SMEM)
     vmem = pl.BlockSpec(memory_space=pltpu.VMEM)
     return pl.pallas_call(
         chi_kernel,
-        in_specs=[smem, smem] + [vmem] * 5,
+        in_specs=[smem] * 3 + [vmem] * 5,
         out_specs=vmem,
         out_shape=jax.ShapeDtypeStruct((ROWS, 2, ROWS), jnp.float32),
         scratch_shapes=[pltpu.VMEM((16, 4 * HALF, 128), jnp.bfloat16)],
@@ -246,7 +248,7 @@
         cost_estimate=pl.CostEstimate(
             flops=600_000_000, bytes_accessed=4_000_000, transcendentals=0
         ),
-    )(half, row, own, other, near, far, weight)
+    )(half, row_a, row, own, other, near, far, weight)
 
 
 def ka_route(move):
@@ -265,14 +267,16 @@
     return route
 
 
-def gather_columns(rho):
-    across = lax.ppermute(rho, "ka", ka_route(lambda y, x, c: (y + 1, x, c)))
-    block = jnp.concatenate([rho, across])
-    ring = [
-        lax.ppermute(block, "ka", ka_route(lambda y, x, c, s=s: (y, x + s, c))) for s in (1, 2, 3)
-    ]
-    block = jnp.concatenate([block] + ring)
-    other = lax.ppermute(block, "ka", ka_route(lambda y, x, c: (y, x, c + 1)))
+def mesh_route(move):
+    route = []
+    for k in range(16):
+        for f in range(16):
+            to_k, to_f = move(k, f)
+            route.append((k * 16 + f, to_k * 16 + to_f))
+    return route
+
+
+def column_places():
     row = lax.axis_index("ka")
     y, x, c = row // 8, (row // 2) % 4, row % 2
     places = [
@@ -281,15 +285,7 @@
         for s in range(4)
         for dy in range(2)
     ]
-    return [block, other], jnp.stack(places).astype(jnp.int32)
-
-
-def gather_rows(own):
-    halves = own.reshape(2, 1, HALF, 128)
-    copies = jnp.broadcast_to(halves, (2, 8, HALF, 128)).reshape(16, HALF, 128)
-    mine = lax.all_to_all(copies, "fft", 0, 0)
-    other = lax.ppermute(mine, "fft", fft_route(lambda y, z: (y + 1, z)))
-    return mine, other
+    return jnp.stack(places).astype(jnp.int32)
 
 
 def shards(psi_val, psi_cond, e_val, e_cond, occ_val, occ_cond, umklapp, sphere):
@@ -304,37 +300,34 @@
     k_here = jnp.mod(row - step_q, count_k)
 
     offset = lax.dynamic_index_in_dim(umklapp, k_here, keepdims=False)
-    x_place = 2 * planes * x_block + jnp.arange(2 * planes, dtype=jnp.int32)
-    x_freq = jnp.arange(128, dtype=jnp.int32) - BOX // 2 - offset
-    turns = jnp.mod(x_freq[:, None] * x_place[None, :], GRID).astype(jnp.float32)
+    x_place = 2 * planes * x_block + jnp.arange(8, dtype=jnp.int32)
+    x_freq = jnp.arange(32, dtype=jnp.int32) - BOX // 2 - offset
+    turns = jnp.mod(x_place[:, None] * x_freq[None, :], GRID).astype(jnp.float32)
     angle = turns * (2.0 * math.pi / GRID)
-    both = jnp.stack(
-        [jnp.cos(angle).reshape(128, planes, 2), jnp.sin(angle).reshape(128, planes, 2)], axis=2
+    x_table = jnp.concatenate([jnp.cos(angle), jnp.sin(angle)]).astype(jnp.bfloat16)
+    half = x_block // 8
+    others = jnp.arange(16, dtype=jnp.int32) ^ row
+    blocks = jnp.take(sphere.reshape(16, 2, HALF), others, axis=0)
+
+    def places(part):
+        index = lax.dynamic_index_in_dim(blocks, part, 1, keepdims=False).reshape(1, NG // 2)
+        plane = index % (BOX * BOX)
+        return (plane % BOX) * 32 + plane // BOX, index // (BOX * BOX)
+
+    away, home = places(1 - half), places(half)
+    val_occ = jnp.roll(occ_val, step_q, 0)[:, :, None]
+    val_energy = jnp.roll(e_val, step_q, 0)[:, :, None]
+    weight = (val_occ - occ_cond[:, None, :]).astype(jnp.float32) / (
+        (val_energy - e_cond[:, None, :]) * (count_k * NV)
     )
-    x_table = jnp.broadcast_to(both[..., None], (128, planes, 2, 2, 64)).reshape(128, planes * 256)
-    x_table = x_table.astype(jnp.bfloat16)
-    half = x_block // 8
-    blocks = sphere.reshape(16, 2, HALF)
-
-    def places(part):
-        index = lax.dynamic_index_in_dim(blocks, part, 1, keepdims=False).reshape(NG // 2)
-        plane = index % (BOX * BOX)
-        column = (plane % BOX) * 32 + plane // BOX
-        freq = index // (BOX * BOX)
-        return [jnp.broadcast_to(a[:, None], (NG // 2, 128)) for a in (column, freq)]
-
-    away, home = places(1 - half), places(half)
-
-    weight = (occ_val[:, :, None] - jnp.roll(occ_cond, -step_q, 0)[:, None, :]).astype(
-        jnp.float32
-    ) / ((e_val[:, :, None] - jnp.roll(e_cond, -step_q, 0)[:, None, :]) * (count_k * NV))
-    weight = jnp.roll(weight.reshape(count_k, NV * NC), step_q, 0)
+    weight = weight.reshape(count_k, NV * NC)
     weight = jnp.concatenate([weight, weight], axis=1)
-
-    val, away, home, x_table, weight = lax.optimization_barrier(
-        (val, away, home, x_table, weight)
+    row_b = column_places()
+
+    val, away, home, x_table, weight, others, row_b = lax.optimization_barrier(
+        (val, away, home, x_table, weight, others, row_b)
     )
-    field = fields(val, psi_cond)
+    field = fields(val, psi_cond).reshape(planes * 256, COLS)
     sent = pick(away[0], away[1], field, x_table)
     came = lax.ppermute(sent, "fft", fft_route(lambda y, z: (y + 1, z)))
     kept = pick(home[0], home[1], field, x_table)
@@ -342,12 +335,22 @@
     spread = lax.all_to_all(share.reshape(16, HALF, 128), "fft", 0, 0)
     rho = spread.reshape(2, 8, HALF, 128).astype(jnp.float32).sum(1).astype(jnp.bfloat16)
     rho = rho.reshape(ROWS, 128)
-    turned = lax.ppermute(
-        rho, ("ka", "fft"), [(i * 16 + j, j * 16 + i) for i in range(16) for j in range(16)]
+    by_row = lax.ppermute(rho, ("ka", "fft"), mesh_route(lambda k, f: (k ^ f, f)))
+    by_column = lax.ppermute(rho, ("ka", "fft"), mesh_route(lambda k, f: (k, f ^ k)))
+    copies = jnp.broadcast_to(by_row.reshape(2, 1, HALF, 128), (2, 8, HALF, 128))
+    mine = lax.all_to_all(copies.reshape(16, HALF, 128), "fft", 0, 0)
+    across = lax.ppermute(by_column, "ka", ka_route(lambda y, x, c: (y + 1, x, c)))
+    block = jnp.concatenate([by_column, across])
+    ring = [
+        lax.ppermute(block, "ka", ka_route(lambda y, x, c, s=s: (y, x + s, c))) for s in (1, 2, 3)
+    ]
+    near = jnp.concatenate([block] + ring)
+    near, mine = lax.optimization_barrier((near, mine))
+    other = lax.ppermute(mine, "fft", fft_route(lambda y, z: (y + 1, z)))
+    far = lax.ppermute(near, "ka", ka_route(lambda y, x, c: (y, x, c + 1)))
+    return contract(
+        half[None].astype(jnp.int32), others, row_b, mine, other, near, far, weight
     )
-    (near, far), row_b = gather_columns(rho)
-    mine, other = gather_rows(turned)
-    return contract(half[None].astype(jnp.int32), row_b, mine, other, near, far, weight)
 
 
 def solution(mesh):

time: 135 us -> 137 us (1.015)
  the two profiles are of different devices: /device:TPU:1 before, /device:TPU:62 now
where the time goes in v3:
time: 137 us; the launch traced here: 135 us
  waiting for transfers between devices  47.8 us (35%)
  Pallas kernels  27.7 us (20%)
  starting transfers between devices  25.4 us (19%)
  blocking collectives  22.9 us (17%)
  local copies, waits for them, and re-layouts  6.78 us (5%)
  other arithmetic  3.81 us (3%)
    all_to_all x1, blocking collectives, shards(): spread = lax.all_to_all(share.reshape(16, HALF, 128), 'fft', 0, 0)  22.9 us
    pallas_call x1, Pallas kernels, fields(): pl.pallas_call(field_kernel, grid=(planes,), in_specs=[pl.BlockSpec((NV,...  15.6 us
    ppermute x1, waiting for transfers between devices, shards(): other = lax.ppermute(mine, 'fft', fft_route(lambda y, z: (y + 1, z)))  11.2 us
    ppermute x1, waiting for transfers between devices, shards(): lax.ppermute(rho, ('ka', 'fft'), mesh_route(lambda k, f: (k, f ^ k)))  10.9 us
    pallas_call x2, Pallas kernels, pick(): pl.pallas_call(pick_kernel, in_specs=[vmem] * 4, out_specs=vmem, out_shap...  9.59 us
    all_to_all x1, starting transfers between devices, shards(): mine = lax.all_to_all(copies.reshape(16, HALF, 128), 'fft', 0, 0)  7.85 us
    ppermute x1, waiting for transfers between devices, shards(): came = lax.ppermute(sent, 'fft', fft_route(lambda y, z: (y + 1, z)))  7.24 us
    ppermute x3, waiting for transfers between devices, shards(): lax.ppermute(block, 'ka', ka_route(lambda y, x, c, s=s: (y, x + s, c)))  6.35 us
  transfers between devices with their start and end apart: 11, of which 9 were waited for; matrix products, arithmetic and copies ran while one was open for 6% of the time, Pallas kernels for 4%

profile of v3, /device:TPU:62, one launch (start us, length us, event | category | flops | bytes accessed | tf_op | source)
XLA Modules:
  0.0 134.6 jit_solution(18196008175541985015)
XLA Ops:
  0.0 2.1 %collective-permute-start = (bf16[1,2,4,27648]{3,2,1,0:T(4,128)(2,1)}, bf16[1,2,4,27648]{3,2,1,0:T(4,128)(2,1)S(1)}, u32[]{:S(2)}, u32[]{:S(2)}) collective-permute-start(bf16[1,2,4,27648]{3,2,1,0:T(4,128)(2,1)} %param.12), channel_id=1, source_target_pairs={{0,64},{16,80},{32,96},{48,112},{64,128},{80,144},{96,160},{112,17... | collective-permute-start | bytes 1327112 | tf_op jit(solution)/shard_map/ppermute | solution.py:297
  2.1 1.3 dynamic_slice.13
  9.5 4.1 %collective-permute-done = bf16[1,2,4,27648]{3,2,1,0:T(4,128)(2,1)S(1)} collective-permute-done((bf16[1,2,4,27648]{3,2,1,0:T(4,128)(2,1)}, bf16[1,2,4,27648]{3,2,1,0:T(4,128)(2,1)S(1)}, u32[]{:S(2)}, u32[]{:S(2)}) %collective-permute-start) | collective-permute-done | bytes 442400 | tf_op jit(solution)/shard_map/ppermute | solution.py:297
  14.4 15.6 %shard_map.118 = bf16[3,256,768]{2,1,0:T(8,128)(2,1)} custom-call(bf16[2,4,27648]{2,1,0:T(4,128)(2,1)} %bitcast.62, bf16[1,3,9216,128]{3,2,1,0:T(8,128)(2,1)} %cond_ref.1, bf16[8,256]{1,0:T(8,128)(2,1)} %constant.288.clone.vs_ref, bf16[128,256]{1,0:T(8,128)(2,1)} %constant.289.clone.cs_ref, bf16[48,192]{1,0:T(8,128)(2,1)} %constant.290.clone.tz_ref, ...), custom_call_target="tpu_custom_call" | custom-call | flops 4000000000 | bytes 9000000 | tf_op jit(solution)/shard_map/pallas_call | solution.py:140
  30.0 1.3 copy-done.1
  31.3 4.8 %shard_map.120 = bf16[2048,128]{1,0:T(8,128)(2,1)S(1)} custom-call(s32[1,2048]{1,0:T(1,128)S(1)} %get-tuple-element.22.col_ref, s32[1,2048]{1,0:T(1,128)S(1)} %get-tuple-element.23.fx_ref, bf16[768,768]{1,0:T(8,128)(2,1)S(1)} %bitcast.54, bf16[16,32]{1,0:T(8,128)(2,1)S(1)} %pad_maximum_fusion.1.xt_ref), custom_call_target="tpu_custom_call" | custom-call | flops 3000000000 | bytes 2000000 | tf_op jit(solution)/shard_map/pallas_call | solution.py:196
  36.9 4.8 %shard_map.119 = bf16[2048,128]{1,0:T(8,128)(2,1)S(1)} custom-call(s32[1,2048]{1,0:T(1,128)S(1)} %get-tuple-element.18.col_ref, s32[1,2048]{1,0:T(1,128)S(1)} %get-tuple-element.19.fx_ref, bf16[768,768]{1,0:T(8,128)(2,1)S(1)} %bitcast.55, bf16[16,32]{1,0:T(8,128)(2,1)S(1)} %pad_maximum_fusion.1.xt_ref), custom_call_target="tpu_custom_call" | custom-call | flops 3000000000 | bytes 2000000 | tf_op jit(solution)/shard_map/pallas_call | solution.py:196
  41.7 7.2 %collective-permute-done.1 = bf16[2048,128]{1,0:T(8,128)(2,1)S(1)} collective-permute-done((bf16[2048,128]{1,0:T(8,128)(2,1)S(1)}, bf16[2048,128]{1,0:T(8,128)(2,1)S(1)}, u32[]{:S(2)}, u32[]{:S(2)}) %collective-permute-start.1) | collective-permute-done | bytes 524320 | tf_op jit(solution)/shard_map/ppermute | solution.py:332
  49.1 22.9 %all_to_all.10 = bf16[16,128,128]{2,1,0:T(8,128)(2,1)S(1)} all-to-all(bf16[16,128,128]{2,1,0:T(8,128)(2,1)S(1)} %bitcast.56), channel_id=1, replica_groups=mesh['ka'=16,'fft'=16] {'fft'}, dimensions={0} | all-to-all | bytes 1048576 | tf_op jit(solution)/shard_map/all_to_all | solution.py:335
  72.0 1.9 %collective-permute-start.7 = (bf16[256,128]{1,0:T(8,128)(2,1)S(1)}, bf16[256,128]{1,0:T(8,128)(2,1)S(1)}, u32[]{:S(2)}, u32[]{:S(2)}) collective-permute-start(bf16[256,128]{1,0:T(8,128)(2,1)S(1)} %bitcast.57), channel_id=1, source_target_pairs={{0,0},{1,17},{2,34},{3,51},{4,68},{5,85},{6,102},{7,119},{8,136},{... | collective-permute-start | bytes 196616 | tf_op jit(solution)/shard_map/ppermute | solution.py:338
  73.9 5.2 %collective-permute-done.7 = bf16[256,128]{1,0:T(8,128)(2,1)S(1)} collective-permute-done((bf16[256,128]{1,0:T(8,128)(2,1)S(1)}, bf16[256,128]{1,0:T(8,128)(2,1)S(1)}, u32[]{:S(2)}, u32[]{:S(2)}) %collective-permute-start.7) | collective-permute-done | bytes 65568 | tf_op jit(solution)/shard_map/ppermute | solution.py:338
  79.1 0.9 broadcast_in_dim.30
  80.0 7.9 %all-to-all-start.1 = ((bf16[16,128,128]{2,1,0:T(8,128)(2,1)}), bf16[16,128,128]{2,1,0:T(8,128)(2,1)S(1)}, u32[]{:S(2)}, u32[]{:S(2)}) async-start(bf16[16,128,128]{2,1,0:T(8,128)(2,1)} %bitcast.32), calls=%async_computation.1 | async-start | bytes 1048576 | tf_op jit(solution)/shard_map/all_to_all | solution.py:341
  87.8 4.6 %collective-permute-start.2 = (bf16[256,128]{1,0:T(8,128)(2,1)S(1)}, bf16[256,128]{1,0:T(8,128)(2,1)S(1)}, u32[]{:S(2)}, u32[]{:S(2)}) collective-permute-start(bf16[256,128]{1,0:T(8,128)(2,1)S(1)} %bitcast.58), channel_id=1, source_target_pairs={{0,0},{1,1},{2,2},{3,3},{4,4},{5,5},{6,6},{7,7},{8,8},{9,9},{10,10... | collective-permute-start | bytes 196616 | tf_op jit(solution)/shard_map/ppermute | solution.py:339
  92.4 10.9 %collective-permute-done.2 = bf16[256,128]{1,0:T(8,128)(2,1)S(1)} collective-permute-done((bf16[256,128]{1,0:T(8,128)(2,1)S(1)}, bf16[256,128]{1,0:T(8,128)(2,1)S(1)}, u32[]{:S(2)}, u32[]{:S(2)}) %collective-permute-start.2) | collective-permute-done | bytes 65568 | tf_op jit(solution)/shard_map/ppermute | solution.py:339
  103.3 2.9 %collective-permute-start.3 = (bf16[256,128]{1,0:T(8,128)(2,1)S(1)}, bf16[256,128]{1,0:T(8,128)(2,1)S(1)}, u32[]{:S(2)}, u32[]{:S(2)}) collective-permute-start(bf16[256,128]{1,0:T(8,128)(2,1)S(1)} %collective-permute-done.2), channel_id=1, source_target_pairs={{0,128},{16,144},{32,160},{48,176},{64,192},{80,208},{96,224},{112... | collective-permute-start | bytes 196616 | tf_op jit(solution)/shard_map/ppermute | solution.py:342
  106.2 2.9 %collective-permute-done.3 = bf16[256,128]{1,0:T(8,128)(2,1)S(1)} collective-permute-done((bf16[256,128]{1,0:T(8,128)(2,1)S(1)}, bf16[256,128]{1,0:T(8,128)(2,1)S(1)}, u32[]{:S(2)}, u32[]{:S(2)}) %collective-permute-start.3) | collective-permute-done | bytes 65568 | tf_op jit(solution)/shard_map/ppermute | solution.py:342
  109.2 3.7 %collective-permute-start.5 = (bf16[512,128]{1,0:T(8,128)(2,1)S(1)}, bf16[512,128]{1,0:T(8,128)(2,1)S(1)}, u32[]{:S(2)}, u32[]{:S(2)}) collective-permute-start(bf16[512,128]{1,0:T(8,128)(2,1)S(1)} %get-tuple-element.27), channel_id=1, source_target_pairs={{0,64},{16,80},{32,96},{48,112},{64,0},{80,16},{96,32},{112,48},{1... | collective-permute-start | bytes 393224 | tf_op jit(solution)/shard_map/ppermute | solution.py:345
  112.9 2.7 %collective-permute-done.4 = bf16[512,128]{1,0:T(8,128)(2,1)S(1)} collective-permute-done((bf16[512,128]{1,0:T(8,128)(2,1)S(1)}, bf16[512,128]{1,0:T(8,128)(2,1)S(1)}, u32[]{:S(2)}, u32[]{:S(2)}) %collective-permute-start.4) | collective-permute-done | bytes 131104 | tf_op jit(solution)/shard_map/ppermute | solution.py:345
  115.6 1.4 %collective-permute-done.5 = bf16[512,128]{1,0:T(8,128)(2,1)S(1)} collective-permute-done((bf16[512,128]{1,0:T(8,128)(2,1)S(1)}, bf16[512,128]{1,0:T(8,128)(2,1)S(1)}, u32[]{:S(2)}, u32[]{:S(2)}) %collective-permute-start.5) | collective-permute-done | bytes 131104 | tf_op jit(solution)/shard_map/ppermute | solution.py:345
  117.0 2.2 %collective-permute-done.6 = bf16[512,128]{1,0:T(8,128)(2,1)S(1)} collective-permute-done((bf16[512,128]{1,0:T(8,128)(2,1)S(1)}, bf16[512,128]{1,0:T(8,128)(2,1)S(1)}, u32[]{:S(2)}, u32[]{:S(2)}) %collective-permute-start.6) | collective-permute-done | bytes 131104 | tf_op jit(solution)/shard_map/ppermute | solution.py:345
  119.3 1.5 %collective-permute-start.8 = (bf16[16,128,128]{2,1,0:T(8,128)(2,1)S(1)}, bf16[16,128,128]{2,1,0:T(8,128)(2,1)S(1)}, u32[]{:S(2)}, u32[]{:S(2)}) collective-permute-start(bf16[16,128,128]{2,1,0:T(8,128)(2,1)S(1)} %all-to-all-done.1.own_ref), channel_id=1, source_target_pairs={{0,8},{1,9},{2,10},{3,11},{4,12},{5,13},{6,14},{7,15},{8,0},{9,1},... | collective-permute-start | bytes 1572872 | tf_op jit(solution)/shard_map/ppermute | solution.py:349
  120.8 11.2 %collective-permute-done.8.other_ref = bf16[16,128,128]{2,1,0:T(8,128)(2,1)S(1)} collective-permute-done((bf16[16,128,128]{2,1,0:T(8,128)(2,1)S(1)}, bf16[16,128,128]{2,1,0:T(8,128)(2,1)S(1)}, u32[]{:S(2)}, u32[]{:S(2)}) %collective-permute-start.8) | collective-permute-done | bytes 524320 | tf_op jit(solution)/shard_map/ppermute | solution.py:349
  132.1 2.5 %shard_map.121 = f32[256,2,256]{2,1,0:T(2,128)} custom-call(s32[1]{0:T(128)} %bitcast.half_ref, s32[16]{0:T(128)S(1)} %iota_xor_fusion.row_a_ref, s32[16]{0:T(128)S(1)} %stack.67.row_ref, bf16[16,128,128]{2,1,0:T(8,128)(2,1)S(1)} %all-to-all-done.1.own_ref, bf16[16,128,128]{2,1,0:T(8,128)(2,1)S(1)} %collective-permute-done.8.other_ref, ...), custom_call_target="tpu_custom_call" | custom-call | flops 600000000 | bytes 4000000 | tf_op jit(solution)/shard_map/pallas_call | solution.py:241
  (39 shorter events, 8.0 us)
Async XLA Ops:
  0.0 8.5 %copy-start = (s32[4096]{0:T(1024)S(1)}, s32[4096]{0:T(1024)}, u32[]{:S(2)}) copy-start(s32[4096]{0:T(1024)} %param.19) | copy-start | bytes 49156
  0.0 13.6 %collective-permute-start = (bf16[1,2,4,27648]{3,2,1,0:T(4,128)(2,1)}, bf16[1,2,4,27648]{3,2,1,0:T(4,128)(2,1)S(1)}, u32[]{:S(2)}, u32[]{:S(2)}) collective-permute-start(bf16[1,2,4,27648]{3,2,1,0:T(4,128)(2,1)} %param.12), channel_id=1, source_target_pairs={{0,64},{16,80},{32,96},{48,112},{64,128},{80,144},{96,160},{112,17... | collective-permute-start | bytes 1327112 | tf_op jit(solution)/shard_map/ppermute | solution.py:297
  13.6 0.8 copy-start.2
  30.0 1.3 copy-start.1
  36.1 12.9 %collective-permute-start.1 = (bf16[2048,128]{1,0:T(8,128)(2,1)S(1)}, bf16[2048,128]{1,0:T(8,128)(2,1)S(1)}, u32[]{:S(2)}, u32[]{:S(2)}) collective-permute-start(bf16[2048,128]{1,0:T(8,128)(2,1)S(1)} %shard_map.120), channel_id=1, source_target_pairs={{0,8},{1,9},{2,10},{3,11},{4,12},{5,13},{6,14},{7,15},{8,0},{9,1},... | collective-permute-start | bytes 1572872 | tf_op jit(solution)/shard_map/ppermute | solution.py:332
  72.0 7.1 %collective-permute-start.7 = (bf16[256,128]{1,0:T(8,128)(2,1)S(1)}, bf16[256,128]{1,0:T(8,128)(2,1)S(1)}, u32[]{:S(2)}, u32[]{:S(2)}) collective-permute-start(bf16[256,128]{1,0:T(8,128)(2,1)S(1)} %bitcast.57), channel_id=1, source_target_pairs={{0,0},{1,17},{2,34},{3,51},{4,68},{5,85},{6,102},{7,119},{8,136},{... | collective-permute-start | bytes 196616 | tf_op jit(solution)/shard_map/ppermute | solution.py:338
  80.0 39.3 %all-to-all-start.1 = ((bf16[16,128,128]{2,1,0:T(8,128)(2,1)}), bf16[16,128,128]{2,1,0:T(8,128)(2,1)S(1)}, u32[]{:S(2)}, u32[]{:S(2)}) async-start(bf16[16,128,128]{2,1,0:T(8,128)(2,1)} %bitcast.32), calls=%async_computation.1 | async-start | bytes 1048576 | tf_op jit(solution)/shard_map/all_to_all | solution.py:341
  87.8 15.4 %collective-permute-start.2 = (bf16[256,128]{1,0:T(8,128)(2,1)S(1)}, bf16[256,128]{1,0:T(8,128)(2,1)S(1)}, u32[]{:S(2)}, u32[]{:S(2)}) collective-permute-start(bf16[256,128]{1,0:T(8,128)(2,1)S(1)} %bitcast.58), channel_id=1, source_target_pairs={{0,0},{1,1},{2,2},{3,3},{4,4},{5,5},{6,6},{7,7},{8,8},{9,9},{10,10... | collective-permute-start | bytes 196616 | tf_op jit(solution)/shard_map/ppermute | solution.py:339
  103.3 5.8 %collective-permute-start.3 = (bf16[256,128]{1,0:T(8,128)(2,1)S(1)}, bf16[256,128]{1,0:T(8,128)(2,1)S(1)}, u32[]{:S(2)}, u32[]{:S(2)}) collective-permute-start(bf16[256,128]{1,0:T(8,128)(2,1)S(1)} %collective-permute-done.2), channel_id=1, source_target_pairs={{0,128},{16,144},{32,160},{48,176},{64,192},{80,208},{96,224},{112... | collective-permute-start | bytes 196616 | tf_op jit(solution)/shard_map/ppermute | solution.py:342
  109.1 6.5 %collective-permute-start.4 = (bf16[512,128]{1,0:T(8,128)(2,1)S(1)}, bf16[512,128]{1,0:T(8,128)(2,1)S(1)}, u32[]{:S(2)}, u32[]{:S(2)}) collective-permute-start(bf16[512,128]{1,0:T(8,128)(2,1)S(1)} %get-tuple-element.27), channel_id=1, source_target_pairs={{0,32},{16,48},{32,64},{48,80},{64,96},{80,112},{96,0},{112,16},{1... | collective-permute-start | bytes 393224 | tf_op jit(solution)/shard_map/ppermute | solution.py:345
  109.2 7.8 %collective-permute-start.5 = (bf16[512,128]{1,0:T(8,128)(2,1)S(1)}, bf16[512,128]{1,0:T(8,128)(2,1)S(1)}, u32[]{:S(2)}, u32[]{:S(2)}) collective-permute-start(bf16[512,128]{1,0:T(8,128)(2,1)S(1)} %get-tuple-element.27), channel_id=1, source_target_pairs={{0,64},{16,80},{32,96},{48,112},{64,0},{80,16},{96,32},{112,48},{1... | collective-permute-start | bytes 393224 | tf_op jit(solution)/shard_map/ppermute | solution.py:345
  112.8 6.4 %collective-permute-start.6 = (bf16[512,128]{1,0:T(8,128)(2,1)S(1)}, bf16[512,128]{1,0:T(8,128)(2,1)S(1)}, u32[]{:S(2)}, u32[]{:S(2)}) collective-permute-start(bf16[512,128]{1,0:T(8,128)(2,1)S(1)} %get-tuple-element.27), channel_id=1, source_target_pairs={{0,96},{16,112},{32,0},{48,16},{64,32},{80,48},{96,64},{112,80},{1... | collective-permute-start | bytes 393224 | tf_op jit(solution)/shard_map/ppermute | solution.py:345
  119.3 12.8 %collective-permute-start.8 = (bf16[16,128,128]{2,1,0:T(8,128)(2,1)S(1)}, bf16[16,128,128]{2,1,0:T(8,128)(2,1)S(1)}, u32[]{:S(2)}, u32[]{:S(2)}) collective-permute-start(bf16[16,128,128]{2,1,0:T(8,128)(2,1)S(1)} %all-to-all-done.1.own_ref), channel_id=1, source_target_pairs={{0,8},{1,9},{2,10},{3,11},{4,12},{5,13},{6,14},{7,15},{8,0},{9,1},... | collective-permute-start | bytes 1572872 | tf_op jit(solution)/shard_map/ppermute | solution.py:349
  120.8 11.2 %collective-permute-start.9 = (bf16[2048,128]{1,0:T(8,128)(2,1)S(1)}, bf16[2048,128]{1,0:T(8,128)(2,1)S(1)}, u32[]{:S(2)}, u32[]{:S(2)}) collective-permute-start(bf16[2048,128]{1,0:T(8,128)(2,1)S(1)} %constant_dynamic-update-slice_fusion.2.near_ref), channel_id=1, source_target_pairs={{0,16},{16,0},{32,48},{48,32},{64,80},{80,64},{96,112},{112,96},{1... | collective-permute-start | bytes 1572872 | tf_op jit(solution)/shard_map/ppermute | solution.py:350

commit v4 on v3

v4 whole, which is shorter than its diff:
```python
import functools
import math

import jax
import jax.numpy as jnp
import ml_dtypes
import numpy as np
from jax import lax
from jax.experimental import pallas as pl
from jax.experimental.pallas import tpu as pltpu
from jax.sharding import PartitionSpec as P

GRID = 96
BOX = 24
NG = 4096
NV = 2
NC = 32
COLS = 768
ROWS = 256
HALF = 128
YCHUNK = 32
ZROW = 104
PICK = 256


def dft_tables():
    turns = np.mod((np.arange(BOX) - BOX // 2)[:, None] * np.arange(GRID)[None, :], GRID)
    angle = turns.astype(np.float32) * np.float32(2.0 * math.pi / GRID)
    return np.cos(angle), np.sin(angle)


def z_table():
    cosine, sine = dft_tables()
    out = np.zeros((BOX, 2, 2, GRID), np.float32)
    out[:, 0, 0], out[:, 0, 1] = cosine, sine
    out[:, 1, 0], out[:, 1, 1] = -sine, cosine
    return out.reshape(2 * BOX, 2 * GRID).astype(ml_dtypes.bfloat16)


def y_table():
    cosine, sine = dft_tables()
    out = np.zeros((2, 32, 2, GRID), np.float32)
    out[0, :BOX, 0], out[0, :BOX, 1] = cosine, sine
    out[1, :BOX, 0], out[1, :BOX, 1] = -sine, cosine
    return out.reshape(64, 2 * GRID).astype(ml_dtypes.bfloat16)


def val_spread():
    out = np.zeros((NV, 2, 2, 2, 2, NV, NC), np.float32)
    for v in range(NV):
        for p in range(2):
            for i in range(2):
                out[v, p, i, i, p, v, :] = 1.0
    return out.reshape(8, 256).astype(ml_dtypes.bfloat16)


def cond_spread():
    out = np.zeros((2, 2, NC, 2, 2, NV, NC), np.float32)
    for p in range(2):
        for i in range(2):
            for c in range(NC):
                out[p, i, c, i, p, :, c] = 1.0
    return out.reshape(128, 256).astype(ml_dtypes.bfloat16)


def dot(left, right):
    return jnp.dot(left, right, preferred_element_type=jnp.float32)


def tables():
    out = np.zeros((128, 256), ml_dtypes.bfloat16)
    out[:64, : 2 * GRID] = y_table()
    out[64:112, : 2 * GRID] = z_table()
    out[112:120] = val_spread()
    return out


def spread_kernel(cond_ref, cs_ref, out_ref):
    out_ref[0] = dot(cond_ref[0, 0], cs_ref[...]).astype(jnp.bfloat16)


def spread_cond(cond):
    planes, points = cond.shape[1:3]
    chunk = points // 3
    return pl.pallas_call(
        spread_kernel,
        grid=(planes, 3),
        in_specs=[
            pl.BlockSpec((1, 1, chunk, 128), lambda a, g: (0, a, g, 0)),
            pl.BlockSpec((128, 256), lambda a, g: (0, 0)),
        ],
        out_specs=pl.BlockSpec((1, chunk, 256), lambda a, g: (a, g, 0)),
        out_shape=jax.ShapeDtypeStruct((planes, points, 256), jnp.bfloat16),
        compiler_params=pltpu.CompilerParams(vmem_limit_bytes=20 * 2**20),
        cost_estimate=pl.CostEstimate(
            flops=2_000_000_000, bytes_accessed=20_000_000, transcendentals=0
        ),
    )(cond, cond_spread())


def field_kernel(val_ref, cond_ref, table_ref, out_ref, zs_ref, pair_ref, y_ref):
    points = YCHUNK * GRID
    steps = GRID // YCHUNK
    ty = table_ref[:64, : 2 * GRID]
    tz = table_ref[64:112, : 2 * GRID]
    vs = table_ref[112:120, :]

    def pairs(slot):
        val = jnp.concatenate(
            [val_ref[v].astype(jnp.float32) for v in range(NV)], axis=0
        ).astype(jnp.bfloat16)
        spread = lax.dot_general(
            val, vs, (((0,), (0,)), ((), ())), preferred_element_type=jnp.float32
        )
        cond = cond_ref[0].astype(jnp.float32)
        val_re, val_im = spread[:, :128], spread[:, 128:]
        cond_re, cond_im = cond[:, :128], cond[:, 128:]
        pair_ref[slot, 0] = (val_re * cond_re + val_im * cond_im).astype(jnp.bfloat16)
        pair_ref[slot, 1] = (val_re * cond_im - val_im * cond_re).astype(jnp.bfloat16)

    def z_pass(step, slot):
        for y in range(0, YCHUNK, 2):
            rhs = jnp.concatenate(
                [
                    jnp.concatenate(
                        [pair_ref[slot, i, (y + u) * GRID : (y + u + 1) * GRID] for u in range(2)],
                        axis=1,
                    )
                    for i in range(2)
                ],
                axis=0,
            )
            z_out = dot(tz, rhs)
            for u in range(2):
                zs_ref[pl.ds(step * YCHUNK + y + u, 2 * BOX, stride=ZROW), :] = z_out[
                    :, u * 128 : (u + 1) * 128
                ]

    def y_pass():
        for fz in range(0, BOX, 2):
            rhs = jnp.concatenate(
                [
                    jnp.concatenate(
                        [
                            zs_ref[pl.ds(((fz + u) * 2 + i) * ZROW, GRID), :].astype(jnp.bfloat16)
                            for i in range(2)
                        ],
                        axis=0,
                    )
                    for u in range(2)
                ],
                axis=1,
            )
            y_out = dot(ty, rhs).astype(jnp.bfloat16)
            for u in range(2):
                for i in range(2):
                    y_ref[(fz + u) * 32 : (fz + u + 1) * 32, i * 128 : (i + 1) * 128] = y_out[
                        i * 32 : (i + 1) * 32, u * 128 : (u + 1) * 128
                    ]
        out_ref[0] = y_ref[...].T

    step = pl.program_id(1)

    @pl.when(step == 0)
    def _():
        pairs(0)

    @pl.when(step > 0)
    def _():
        z_pass(step - 1, (step - 1) % 2)
        pairs(step % 2)

    @pl.when(step == steps - 1)
    def _():
        z_pass(step, step % 2)
        y_pass()


def fields(val, cond, first):
    planes = val.shape[2] // (GRID * GRID)
    chunks = GRID // YCHUNK
    return pl.pallas_call(
        field_kernel,
        grid=(planes, chunks),
        in_specs=[
            pl.BlockSpec((NV, 4, YCHUNK * GRID), lambda a, g: (0, 0, a * chunks + g)),
            pl.BlockSpec((1, YCHUNK * GRID, 256), lambda a, g: (first + a, g, 0)),
            pl.BlockSpec((128, 256), lambda a, g: (0, 0)),
        ],
        out_specs=pl.BlockSpec((1, 256, COLS), lambda a, g: (a, 0, 0)),
        out_shape=jax.ShapeDtypeStruct((planes, 256, COLS), jnp.bfloat16),
        scratch_shapes=[
            pltpu.VMEM((2 * BOX * ZROW, 128), jnp.float32),
            pltpu.VMEM((2, 2, YCHUNK * GRID, 128), jnp.bfloat16),
            pltpu.VMEM((COLS, 256), jnp.bfloat16),
        ],
        compiler_params=pltpu.CompilerParams(vmem_limit_bytes=24 * 2**20),
        cost_estimate=pl.CostEstimate(
            flops=2_000_000_000, bytes_accessed=3_000_000, transcendentals=0
        ),
    )(val, cond, tables())


def x_phases(planes):
    angle = np.mod(
        np.arange(-BOX // 2 - 2, 32 - BOX // 2 - 2)[None, :] * np.arange(GRID)[:, None], GRID
    ).astype(np.float32) * np.float32(2.0 * math.pi / GRID)
    out = np.zeros((GRID // (2 * planes), 2, 8, 32), np.float32)
    out[:, 0, : 2 * planes] = np.cos(angle).reshape(-1, 2 * planes, 32)
    out[:, 1, : 2 * planes] = np.sin(angle).reshape(-1, 2 * planes, 32)
    return out.reshape(-1, 16, 32).astype(ml_dtypes.bfloat16)


def whole_div(value, by):
    return ((value.astype(jnp.float32) + 0.5) * (1.0 / by)).astype(jnp.int32)


def pick_kernel(first, away, umklapp_ref, sphere_ref, xt_ref, *refs):
    y_refs, out_ref = refs[:-1], refs[-1]
    place = lax.axis_index("fft")
    offset = umklapp_ref[lax.rem(lax.axis_index("ka") + 12, 16)]
    part = lax.rem(place // 8 + (1 if away else 0), 2)
    table = xt_ref[place]

    def tile(step, carry):
        index = jnp.concatenate(
            [
                sphere_ref[pl.ds((first + step * (PICK // HALF) + u) * 2 + part, 1), :]
                for u in range(PICK // HALF)
            ],
            axis=1,
        )
        x_freq = whole_div(index, BOX * BOX)
        plane = index - x_freq * (BOX * BOX)
        y_freq = whole_div(plane, BOX)
        column = (plane - y_freq * BOX) * 32 + y_freq
        spot = lax.broadcasted_iota(jnp.int32, (COLS, PICK), 0)
        chosen = jnp.where(column == spot, 1.0, 0.0).astype(jnp.bfloat16)
        freq = jnp.where(x_freq - offset + 2 == spot[:32], 1.0, 0.0).astype(jnp.bfloat16)
        phase = dot(table, freq)
        real = jnp.zeros((64, PICK), jnp.float32)
        imag = jnp.zeros((64, PICK), jnp.float32)
        a = 0
        for y_ref in y_refs:
            for plane_at in range(y_ref.shape[0]):
                got = dot(y_ref[plane_at], chosen)
                for p in range(2):
                    cosine = phase[a * 2 + p : a * 2 + p + 1]
                    sine = phase[8 + a * 2 + p : 9 + a * 2 + p]
                    got_re = got[p * 64 : (p + 1) * 64]
                    got_im = got[128 + p * 64 : 128 + (p + 1) * 64]
                    real = real + cosine * got_re + sine * got_im
                    imag = imag + cosine * got_im - sine * got_re
                a += 1
        scale = 1.0 / (GRID * math.sqrt(GRID))
        both = (jnp.concatenate([real, imag], axis=0) * scale).astype(jnp.bfloat16)
        out_ref[pl.ds(pl.multiple_of(step * PICK, PICK), PICK), :] = both.T
        return carry

    lax.fori_loop(0, out_ref.shape[0] // PICK, tile, 0)


def pick(first, count, away, umklapp, sphere, planes):
    vmem = pl.BlockSpec(memory_space=pltpu.VMEM)
    return pl.pallas_call(
        functools.partial(pick_kernel, first, away),
        in_specs=[pl.BlockSpec(memory_space=pltpu.SMEM)] + [vmem] * (2 + len(planes)),
        out_specs=vmem,
        out_shape=jax.ShapeDtypeStruct((count * HALF, 128), jnp.bfloat16),
        compiler_params=pltpu.CompilerParams(vmem_limit_bytes=24 * 2**20),
        cost_estimate=pl.CostEstimate(
            flops=100_000_000, bytes_accessed=500_000, transcendentals=0
        ),
    )(umklapp, sphere, x_phases(3), *planes)


def chi_kernel(
    e_val_ref, occ_val_ref, e_cond_ref, occ_cond_ref, own_ref, other_ref, near_ref, far_ref,
    out_ref, wa_ref,
):
    lane = lax.broadcasted_iota(jnp.int32, (1, 128), 1)
    sign = jnp.where(lane < 64, 1.0, -1.0)
    band = (lane // NC) % NV == 0
    e_cond = jnp.concatenate([e_cond_ref[...]] * 4, axis=1)
    occ_cond = jnp.concatenate([occ_cond_ref[...].astype(jnp.float32)] * 4, axis=1)
    for row in range(own_ref.shape[0]):
        k = (row + 12) % 16
        e_val = jnp.where(band, e_val_ref[0, k], e_val_ref[1, k])
        occ_val = jnp.where(band, occ_val_ref[0, k], occ_val_ref[1, k]).astype(jnp.float32)
        weight = (occ_val - occ_cond[row : row + 1]) / (
            (e_val - e_cond[row : row + 1]) * (16 * NV)
        )
        for h, ref in enumerate((own_ref, other_ref)):
            weighted = ref[row].astype(jnp.float32) * weight
            weighted = weighted.astype(jnp.bfloat16).astype(jnp.float32)
            wa_ref[row, (2 * h) * HALF : (2 * h + 1) * HALF] = weighted.astype(jnp.bfloat16)
            wa_ref[row, (2 * h + 1) * HALF : (2 * h + 2) * HALF] = (
                pltpu.roll(weighted, 64, 1) * sign
            ).astype(jnp.bfloat16)
    at = lax.axis_index("ka")
    y, x, c = at // 8, lax.rem(at // 2, 4), lax.rem(at, 2)
    total = jnp.zeros((4 * HALF, ROWS), jnp.float32)
    for dc, ref in enumerate((near_ref, far_ref)):
        for s in range(4):
            rows = [
                lax.rem(y + dy, 2) * 8 + lax.rem(x + 4 - s, 4) * 2 + lax.rem(c + dc, 2)
                for dy in range(2)
            ]
            left = jnp.concatenate([wa_ref[r] for r in rows], axis=1)
            right = jnp.concatenate(
                [ref[(2 * s + u) * ROWS : (2 * s + u + 1) * ROWS, :] for u in range(2)], axis=1
            )
            total = total + lax.dot_general(
                left, right, (((1,), (1,)), ((), ())), preferred_element_type=jnp.float32
            )
    half = lax.axis_index("fft") // 8
    for h in range(2):
        start = pl.multiple_of(lax.rem(half + h, 2) * HALF, HALF)
        for i in range(2):
            out_ref[pl.ds(start, HALF), i, :] = total[(2 * h + i) * HALF : (2 * h + i + 1) * HALF]


def contract(e_val, occ_val, e_cond, occ_cond, own, other, near, far):
    smem = pl.BlockSpec(memory_space=pltpu.SMEM)
    vmem = pl.BlockSpec(memory_space=pltpu.VMEM)
    return pl.pallas_call(
        chi_kernel,
        in_specs=[smem, smem] + [vmem] * 6,
        out_specs=vmem,
        out_shape=jax.ShapeDtypeStruct((ROWS, 2, ROWS), jnp.float32),
        scratch_shapes=[pltpu.VMEM((16, 4 * HALF, 128), jnp.bfloat16)],
        compiler_params=pltpu.CompilerParams(vmem_limit_bytes=24 * 2**20),
        cost_estimate=pl.CostEstimate(
            flops=600_000_000, bytes_accessed=4_000_000, transcendentals=0
        ),
    )(e_val.T, occ_val.T, e_cond, occ_cond, own, other, near, far)


def ka_route(move):
    route = []
    for i in range(16):
        y, x, c = move(i // 8, (i // 2) % 4, i % 2)
        route.append((i, (y % 2) * 8 + (x % 4) * 2 + c % 2))
    return route


def fft_route(move):
    route = []
    for i in range(16):
        y, z = move(i // 8, i % 8)
        route.append((i, (y % 2) * 8 + z % 8))
    return route


def mesh_route(move):
    route = []
    for k in range(16):
        for f in range(16):
            to_k, to_f = move(k, f)
            route.append((k * 16 + f, to_k * 16 + to_f))
    return route


def shards(psi_val, psi_cond, e_val, e_cond, occ_val, occ_cond, umklapp, sphere):
    count_k = 16
    step_q = 4
    planes = psi_cond.shape[1]
    shift = [(i, (i + step_q) % count_k) for i in range(count_k)]
    val = lax.ppermute(psi_val, "ka", shift)[0]
    field = [fields(val, spread_cond(psi_cond), 0)]
    sphere = sphere.reshape(NG // HALF, HALF)
    swap = fft_route(lambda y, z: (y + 1, z))
    came = []
    for at in (0, 8):
        sent = pick(at, 8, True, umklapp, sphere, field)
        sent, *field = lax.optimization_barrier((sent, *field))
        came.append(lax.ppermute(sent, "fft", swap))
    kept = pick(0, 16, False, umklapp, sphere, field)
    came = jnp.concatenate(came)
    share = (kept.astype(jnp.float32) + came.astype(jnp.float32)).astype(jnp.bfloat16)
    spread = lax.all_to_all(share.reshape(16, HALF, 128), "fft", 0, 0)
    rho = spread.reshape(2, 8, HALF, 128).astype(jnp.float32).sum(1).astype(jnp.bfloat16)
    rho = rho.reshape(ROWS, 128)
    own = lax.ppermute(rho, ("ka", "fft"), mesh_route(lambda k, f: (f, k)))
    copies = jnp.broadcast_to(own.reshape(2, 1, HALF, 128), (2, 8, HALF, 128))
    copies, rho = lax.optimization_barrier((copies, rho))
    mine = lax.all_to_all(copies.reshape(16, HALF, 128), "fft", 0, 0)
    across = lax.ppermute(rho, "ka", ka_route(lambda y, x, c: (y + 1, x, c)))
    block = jnp.concatenate([rho, across])
    ring = [
        lax.ppermute(block, "ka", ka_route(lambda y, x, c, s=s: (y, x + s, c))) for s in (1, 2, 3)
    ]
    near = jnp.concatenate([block] + ring)
    near, mine = lax.optimization_barrier((near, mine))
    other = lax.ppermute(mine, "fft", swap)
    far = lax.ppermute(near, "ka", ka_route(lambda y, x, c: (y, x, c + 1)))
    return contract(e_val, occ_val, e_cond, occ_cond, mine, other, near, far)


def solution(mesh):
    placed = (P("ka", None, None, "fft"), P("ka", "fft", None, None), P(), P(), P(), P(), P(), P())
    return jax.shard_map(
        shards, mesh=mesh, in_specs=placed, out_specs=P("ka", None, "fft"), check_vma=False
    )
```

time: 137 us -> 115 us (0.84)
  waiting for transfers between devices: 47.8 us -> 34.6 us
  starting transfers between devices: 25.4 us -> 21.3 us
  other arithmetic: 3.81 us -> 0.21 us
  local copies, waits for them, and re-layouts: 6.78 us -> 4.87 us
  Pallas kernels: 27.7 us -> 29.3 us
    ppermute x6, waiting for transfers between devices: 41.5 us -> 28.7 us  [the longest x1 8.68 us: shards(): own = lax.ppermute(rho, ('ka', 'fft'), mesh_route(lambda k, f: (f, k)))]
    ppermute x6, starting transfers between devices: 13.8 us -> 9.51 us  [the longest x2 2.11 us: shards(): came.append(lax.ppermute(sent, 'fft', swap))]
    ppermute x3, starting transfers between devices: 3.76 us -> 5.7 us  [shards(): lax.ppermute(block, 'ka', ka_route(lambda y, x, c, s=s: (y, x + s, c)))]
    unnamed x9 -> x23, local copies, waits for them, and re-layouts: 2.08 us -> 3.93 us
    all_to_all x1, starting transfers between devices: 7.85 us -> 6.07 us  [shards(): mine = lax.all_to_all(copies.reshape(16, HALF, 128), 'fft', 0, 0)]
    pallas_call x4 -> x6, Pallas kernels: 27.7 us -> 29.3 us  [the longest x3 11.2 us: pick(): pl.pallas_call(functools.partial(pick_kernel, first, away), in_specs=[pl....]
    concatenate x4 -> x0, other arithmetic: 1.59 us -> none  [the longest x1 0.75 us: shards(): val_occ = jnp.roll(occ_val, step_q, 0)[:, :, None]]
    slice x2 -> x0, local copies, waits for them, and re-layouts: 1.5 us -> none  [the longest x1 0.75 us: shards(): val_energy = jnp.roll(e_val, step_q, 0)[:, :, None]]
  transfers between devices with their start and end apart: 11 -> 11, of which waited for: 9 -> 9; matrix products, arithmetic and copies ran while one was open for 6% -> 0% of each run, Pallas kernels for 4% -> 9%
where the time goes in v4:
time: 115 us; the launch traced here: 113 us
  waiting for transfers between devices  34.6 us (30%)
  Pallas kernels  29.3 us (25%)
  blocking collectives  22.9 us (20%)
  starting transfers between devices  21.3 us (19%)
  local copies, waits for them, and re-layouts  4.87 us (4%)
    all_to_all x1, blocking collectives, shards(): spread = lax.all_to_all(share.reshape(16, HALF, 128), 'fft', 0, 0)  22.9 us
    pallas_call x3, Pallas kernels, pick(): pl.pallas_call(functools.partial(pick_kernel, first, away), in_specs=[pl....  11.2 us
    pallas_call x1, Pallas kernels, fields(): pl.pallas_call(field_kernel, grid=(planes, chunks), in_specs=[pl.BlockSpe...  10.6 us
    ppermute x1, waiting for transfers between devices, shards(): own = lax.ppermute(rho, ('ka', 'fft'), mesh_route(lambda k, f: (f, k)))  8.68 us
    ppermute x1, waiting for transfers between devices, shards(): other = lax.ppermute(mine, 'fft', swap)  7.61 us
    all_to_all x1, starting transfers between devices, shards(): mine = lax.all_to_all(copies.reshape(16, HALF, 128), 'fft', 0, 0)  6.07 us
    ppermute x3, waiting for transfers between devices, shards(): lax.ppermute(block, 'ka', ka_route(lambda y, x, c, s=s: (y, x + s, c)))  5.88 us
    ppermute x3, starting transfers between devices, shards(): lax.ppermute(block, 'ka', ka_route(lambda y, x, c, s=s: (y, x + s, c)))  5.7 us
  transfers between devices with their start and end apart: 11, of which 9 were waited for; matrix products, arithmetic and copies ran while one was open for 0% of the time, Pallas kernels for 9%

profile of v4, /device:TPU:62, one launch (start us, length us, event | category | flops | bytes accessed | tf_op | source)
XLA Modules:
  0.0 113.3 jit_solution(4078417111139597519)
XLA Ops:
  0.0 2.1 %collective-permute-start = (bf16[1,2,4,27648]{3,2,1,0:T(4,128)(2,1)}, bf16[1,2,4,27648]{3,2,1,0:T(4,128)(2,1)S(1)}, u32[]{:S(2)}, u32[]{:S(2)}) collective-permute-start(bf16[1,2,4,27648]{3,2,1,0:T(4,128)(2,1)} %param.13), channel_id=1, source_target_pairs={{0,64},{16,80},{32,96},{48,112},{64,128},{80,144},{96,160},{112,17... | collective-permute-start | bytes 1327112 | tf_op jit(solution)/shard_map/ppermute | solution.py:369
  2.1 3.0 %copy-done = bf16[1,3,9216,128]{3,2,1,0:T(8,128)(2,1)S(1)} copy-done((bf16[1,3,9216,128]{3,2,1,0:T(8,128)(2,1)S(1)}, bf16[1,3,9216,128]{3,2,1,0:T(8,128)(2,1)}, u32[]{:S(2)}) %copy-start) | copy-done | bytes 7077912
  5.9 5.0 %shard_map.127.cond_ref = bf16[3,9216,256]{2,1,0:T(8,128)(2,1)S(1)} custom-call(bf16[1,3,9216,128]{3,2,1,0:T(8,128)(2,1)S(1)} %copy-done, bf16[128,256]{1,0:T(8,128)(2,1)S(1)} %copy-done.3), custom_call_target="tpu_custom_call" | custom-call | flops 2000000000 | bytes 20000000 | tf_op jit(solution)/shard_map/pallas_call | solution.py:85
  10.9 2.7 %collective-permute-done = bf16[1,2,4,27648]{3,2,1,0:T(4,128)(2,1)S(1)} collective-permute-done((bf16[1,2,4,27648]{3,2,1,0:T(4,128)(2,1)}, bf16[1,2,4,27648]{3,2,1,0:T(4,128)(2,1)S(1)}, u32[]{:S(2)}, u32[]{:S(2)}) %collective-permute-start) | collective-permute-done | bytes 442400 | tf_op jit(solution)/shard_map/ppermute | solution.py:369
  13.6 10.6 %shard_map.128.refs_0_ = bf16[3,256,768]{2,1,0:T(8,128)(2,1)S(1)} custom-call(bf16[2,4,27648]{2,1,0:T(4,128)(2,1)S(1)} %bitcast.10, bf16[3,9216,256]{2,1,0:T(8,128)(2,1)S(1)} %shard_map.127.cond_ref, bf16[128,256]{1,0:T(8,128)(2,1)S(1)} %copy-done.4), custom_call_target="tpu_custom_call" | custom-call | flops 2000000000 | bytes 3000000 | tf_op jit(solution)/shard_map/pallas_call | solution.py:182
  24.3 2.9 %shard_map.129 = bf16[1024,128]{1,0:T(8,128)(2,1)S(1)} custom-call(s32[16]{0:T(128)S(1)} %copy-done.7, s32[32,128]{1,0:T(8,128)S(1)} %bitcast.11, bf16[16,16,32]{2,1,0:T(8,128)(2,1)S(1)} %copy-done.1, bf16[3,256,768]{2,1,0:T(8,128)(2,1)S(1)} %shard_map.128.refs_0_), custom_call_target="tpu_custom_call" | custom-call | flops 100000000 | bytes 500000 | tf_op jit(solution)/shard_map/pallas_call | solution.py:265
  27.2 2.9 %shard_map.130 = bf16[1024,128]{1,0:T(8,128)(2,1)S(1)} custom-call(s32[16]{0:T(128)S(1)} %copy-done.7, s32[32,128]{1,0:T(8,128)S(1)} %bitcast.12, bf16[16,16,32]{2,1,0:T(8,128)(2,1)S(1)} %copy-done.1, bf16[3,256,768]{2,1,0:T(8,128)(2,1)S(1)} %shard_map.128.refs_0_), custom_call_target="tpu_custom_call" | custom-call | flops 100000000 | bytes 500000 | tf_op jit(solution)/shard_map/pallas_call | solution.py:265
  31.0 1.3 %collective-permute-start.1 = (bf16[1024,128]{1,0:T(8,128)(2,1)S(1)}, bf16[1024,128]{1,0:T(8,128)(2,1)S(1)}, u32[]{:S(2)}, u32[]{:S(2)}) collective-permute-start(bf16[1024,128]{1,0:T(8,128)(2,1)S(1)} %shard_map.129), channel_id=1, source_target_pairs={{0,8},{1,9},{2,10},{3,11},{4,12},{5,13},{6,14},{7,15},{8,0},{9,1},... | collective-permute-start | bytes 786440 | tf_op jit(solution)/shard_map/ppermute | solution.py:377
  32.3 5.3 %shard_map.131 = bf16[2048,128]{1,0:T(8,128)(2,1)S(1)} custom-call(s32[16]{0:T(128)S(1)} %copy-done.7, s32[32,128]{1,0:T(8,128)S(1)} %bitcast.13, bf16[16,16,32]{2,1,0:T(8,128)(2,1)S(1)} %copy-done.1, bf16[3,256,768]{2,1,0:T(8,128)(2,1)S(1)} %shard_map.128.refs_0_), custom_call_target="tpu_custom_call" | custom-call | flops 100000000 | bytes 500000 | tf_op jit(solution)/shard_map/pallas_call | solution.py:265
  37.6 1.9 %collective-permute-done.2 = bf16[1024,128]{1,0:T(8,128)(2,1)S(1)} collective-permute-done((bf16[1024,128]{1,0:T(8,128)(2,1)S(1)}, bf16[1024,128]{1,0:T(8,128)(2,1)S(1)}, u32[]{:S(2)}, u32[]{:S(2)}) %collective-permute-start.2) | collective-permute-done | bytes 262176 | tf_op jit(solution)/shard_map/ppermute | solution.py:377
  39.5 3.5 %collective-permute-done.1 = bf16[1024,128]{1,0:T(8,128)(2,1)S(1)} collective-permute-done((bf16[1024,128]{1,0:T(8,128)(2,1)S(1)}, bf16[1024,128]{1,0:T(8,128)(2,1)S(1)}, u32[]{:S(2)}, u32[]{:S(2)}) %collective-permute-start.1) | collective-permute-done | bytes 262176 | tf_op jit(solution)/shard_map/ppermute | solution.py:377
  43.2 22.9 %all_to_all.10 = bf16[16,128,128]{2,1,0:T(8,128)(2,1)S(1)} all-to-all(bf16[16,128,128]{2,1,0:T(8,128)(2,1)S(1)} %bitcast.16), channel_id=1, replica_groups=mesh['ka'=16,'fft'=16] {'fft'}, dimensions={0} | all-to-all | bytes 1048576 | tf_op jit(solution)/shard_map/all_to_all | solution.py:381
  66.1 2.0 %collective-permute-start.3 = (bf16[256,128]{1,0:T(8,128)(2,1)S(1)}, bf16[256,128]{1,0:T(8,128)(2,1)S(1)}, u32[]{:S(2)}, u32[]{:S(2)}) collective-permute-start(bf16[256,128]{1,0:T(8,128)(2,1)S(1)} %bitcast.17), channel_id=1, source_target_pairs={{0,0},{1,16},{2,32},{3,48},{4,64},{5,80},{6,96},{7,112},{8,128},{9... | collective-permute-start | bytes 196616 | tf_op jit(solution)/shard_map/ppermute | solution.py:384
  68.2 8.7 %collective-permute-done.3 = bf16[256,128]{1,0:T(8,128)(2,1)S(1)} collective-permute-done((bf16[256,128]{1,0:T(8,128)(2,1)S(1)}, bf16[256,128]{1,0:T(8,128)(2,1)S(1)}, u32[]{:S(2)}, u32[]{:S(2)}) %collective-permute-start.3) | collective-permute-done | bytes 65568 | tf_op jit(solution)/shard_map/ppermute | solution.py:384
  77.7 6.1 %all-to-all-start.1 = ((bf16[16,128,128]{2,1,0:T(8,128)(2,1)}), bf16[16,128,128]{2,1,0:T(8,128)(2,1)S(1)}, u32[]{:S(2)}, u32[]{:S(2)}) async-start(bf16[16,128,128]{2,1,0:T(8,128)(2,1)} %bitcast.8), calls=%async_computation.1 | async-start | bytes 1048576 | tf_op jit(solution)/shard_map/all_to_all | solution.py:387
  83.8 1.6 %collective-permute-start.4 = (bf16[256,128]{1,0:T(8,128)(2,1)S(1)}, bf16[256,128]{1,0:T(8,128)(2,1)S(1)}, u32[]{:S(2)}, u32[]{:S(2)}) collective-permute-start(bf16[256,128]{1,0:T(8,128)(2,1)S(1)} %bitcast.18), channel_id=1, source_target_pairs={{0,128},{16,144},{32,160},{48,176},{64,192},{80,208},{96,224},{112... | collective-permute-start | bytes 196616 | tf_op jit(solution)/shard_map/ppermute | solution.py:388
  85.5 4.3 %collective-permute-done.4 = bf16[256,128]{1,0:T(8,128)(2,1)S(1)} collective-permute-done((bf16[256,128]{1,0:T(8,128)(2,1)S(1)}, bf16[256,128]{1,0:T(8,128)(2,1)S(1)}, u32[]{:S(2)}, u32[]{:S(2)}) %collective-permute-start.4) | collective-permute-done | bytes 65568 | tf_op jit(solution)/shard_map/ppermute | solution.py:388
  89.8 3.7 %collective-permute-start.5 = (bf16[512,128]{1,0:T(8,128)(2,1)S(1)}, bf16[512,128]{1,0:T(8,128)(2,1)S(1)}, u32[]{:S(2)}, u32[]{:S(2)}) collective-permute-start(bf16[512,128]{1,0:T(8,128)(2,1)S(1)} %get-tuple-element.21), channel_id=1, source_target_pairs={{0,32},{16,48},{32,64},{48,80},{64,96},{80,112},{96,0},{112,16},{1... | collective-permute-start | bytes 393224 | tf_op jit(solution)/shard_map/ppermute | solution.py:391
  94.2 1.3 %collective-permute-start.7 = (bf16[512,128]{1,0:T(8,128)(2,1)S(1)}, bf16[512,128]{1,0:T(8,128)(2,1)S(1)}, u32[]{:S(2)}, u32[]{:S(2)}) collective-permute-start(bf16[512,128]{1,0:T(8,128)(2,1)S(1)} %get-tuple-element.21), channel_id=1, source_target_pairs={{0,96},{16,112},{32,0},{48,16},{64,32},{80,48},{96,64},{112,80},{1... | collective-permute-start | bytes 393224 | tf_op jit(solution)/shard_map/ppermute | solution.py:391
  96.1 4.0 %collective-permute-done.6 = bf16[512,128]{1,0:T(8,128)(2,1)S(1)} collective-permute-done((bf16[512,128]{1,0:T(8,128)(2,1)S(1)}, bf16[512,128]{1,0:T(8,128)(2,1)S(1)}, u32[]{:S(2)}, u32[]{:S(2)}) %collective-permute-start.6) | collective-permute-done | bytes 131104 | tf_op jit(solution)/shard_map/ppermute | solution.py:391
  100.1 1.3 %collective-permute-done.7 = bf16[512,128]{1,0:T(8,128)(2,1)S(1)} collective-permute-done((bf16[512,128]{1,0:T(8,128)(2,1)S(1)}, bf16[512,128]{1,0:T(8,128)(2,1)S(1)}, u32[]{:S(2)}, u32[]{:S(2)}) %collective-permute-start.7) | collective-permute-done | bytes 131104 | tf_op jit(solution)/shard_map/ppermute | solution.py:391
  101.4 1.7 %collective-permute-start.8 = (bf16[16,128,128]{2,1,0:T(8,128)(2,1)S(1)}, bf16[16,128,128]{2,1,0:T(8,128)(2,1)S(1)}, u32[]{:S(2)}, u32[]{:S(2)}) collective-permute-start(bf16[16,128,128]{2,1,0:T(8,128)(2,1)S(1)} %all-to-all-done.1.own_ref), channel_id=1, source_target_pairs={{0,8},{1,9},{2,10},{3,11},{4,12},{5,13},{6,14},{7,15},{8,0},{9,1},... | collective-permute-start | bytes 1572872 | tf_op jit(solution)/shard_map/ppermute | solution.py:395
  103.1 7.6 %collective-permute-done.8.other_ref = bf16[16,128,128]{2,1,0:T(8,128)(2,1)S(1)} collective-permute-done((bf16[16,128,128]{2,1,0:T(8,128)(2,1)S(1)}, bf16[16,128,128]{2,1,0:T(8,128)(2,1)S(1)}, u32[]{:S(2)}, u32[]{:S(2)}) %collective-permute-start.8) | collective-permute-done | bytes 524320 | tf_op jit(solution)/shard_map/ppermute | solution.py:395
  110.7 2.6 %shard_map.132 = f32[256,2,256]{2,1,0:T(2,128)} custom-call(f32[2,16]{1,0:T(2,128)S(1)} %bitcast.14, s32[2,16]{1,0:T(2,128)S(1)} %bitcast.15, f32[16,32]{1,0:T(8,128)S(1)} %copy-done.5, s32[16,32]{1,0:T(8,128)S(1)} %copy-done.6, bf16[16,128,128]{2,1,0:T(8,128)(2,1)S(1)} %all-to-all-done.1.own_ref, ...), custom_call_target="tpu_custom_call" | custom-call | flops 600000000 | bytes 4000000 | tf_op jit(solution)/shard_map/pallas_call | solution.py:326
  (33 shorter events, 4.1 us)
Async XLA Ops:
  0.0 13.6 %collective-permute-start = (bf16[1,2,4,27648]{3,2,1,0:T(4,128)(2,1)}, bf16[1,2,4,27648]{3,2,1,0:T(4,128)(2,1)S(1)}, u32[]{:S(2)}, u32[]{:S(2)}) collective-permute-start(bf16[1,2,4,27648]{3,2,1,0:T(4,128)(2,1)} %param.13), channel_id=1, source_target_pairs={{0,64},{16,80},{32,96},{48,112},{64,128},{80,144},{96,160},{112,17... | collective-permute-start | bytes 1327112 | tf_op jit(solution)/shard_map/ppermute | solution.py:369
  2.1 3.0 %copy-start = (bf16[1,3,9216,128]{3,2,1,0:T(8,128)(2,1)S(1)}, bf16[1,3,9216,128]{3,2,1,0:T(8,128)(2,1)}, u32[]{:S(2)}) copy-start(bf16[1,3,9216,128]{3,2,1,0:T(8,128)(2,1)} %cond_ref.1) | copy-start | bytes 21233668
  5.1 0.8 copy-start.3
  5.9 7.7 %copy-start.4 = (bf16[128,256]{1,0:T(8,128)(2,1)S(1)}, bf16[128,256]{1,0:T(8,128)(2,1)}, u32[]{:S(2)}) copy-start(bf16[128,256]{1,0:T(8,128)(2,1)} %constant.10.clone.table_ref) | copy-start | bytes 196612
  13.6 10.6 %copy-start.1 = (bf16[16,16,32]{2,1,0:T(8,128)(2,1)S(1)}, bf16[16,16,32]{2,1,0:T(8,128)(2,1)}, u32[]{:S(2)}) copy-start(bf16[16,16,32]{2,1,0:T(8,128)(2,1)} %constant.11.clone.xt_ref) | copy-start | bytes 49156
  13.6 10.7 %copy-start.2 = (s32[4096]{0:T(1024)S(1)}, s32[4096]{0:T(1024)}, u32[]{:S(2)}) copy-start(s32[4096]{0:T(1024)} %param.20) | copy-start | bytes 49156
  13.6 10.7 %copy-start.7 = (s32[16]{0:T(128)S(1)}, s32[16]{0:T(128)}, u32[]{:S(2)}) copy-start(s32[16]{0:T(128)} %umklapp_ref.5) | copy-start | bytes 196
  24.2 86.5 %copy-start.5 = (f32[16,32]{1,0:T(8,128)S(1)}, f32[16,32]{1,0:T(8,128)}, u32[]{:S(2)}) copy-start(f32[16,32]{1,0:T(8,128)} %e_cond_ref.1) | copy-start | bytes 6148
  24.2 86.5 %copy-start.6 = (s32[16,32]{1,0:T(8,128)S(1)}, s32[16,32]{1,0:T(8,128)}, u32[]{:S(2)}) copy-start(s32[16,32]{1,0:T(8,128)} %occ_cond_ref.1) | copy-start | bytes 6148
  24.2 86.5 %copy-start.8 = (f32[16,2]{0,1:T(2,128)S(1)}, f32[16,2]{0,1:T(2,128)}, u32[]{:S(2)}) copy-start(f32[16,2]{0,1:T(2,128)} %param.15) | copy-start | bytes 388
  24.3 86.5 %copy-start.9 = (s32[16,2]{0,1:T(2,128)S(1)}, s32[16,2]{0,1:T(2,128)}, u32[]{:S(2)}) copy-start(s32[16,2]{0,1:T(2,128)} %param.17) | copy-start | bytes 388
  30.2 9.3 %collective-permute-start.2 = (bf16[1024,128]{1,0:T(8,128)(2,1)S(1)}, bf16[1024,128]{1,0:T(8,128)(2,1)S(1)}, u32[]{:S(2)}, u32[]{:S(2)}) collective-permute-start(bf16[1024,128]{1,0:T(8,128)(2,1)S(1)} %shard_map.130), channel_id=1, source_target_pairs={{0,8},{1,9},{2,10},{3,11},{4,12},{5,13},{6,14},{7,15},{8,0},{9,1},... | collective-permute-start | bytes 786440 | tf_op jit(solution)/shard_map/ppermute | solution.py:377
  31.0 12.0 %collective-permute-start.1 = (bf16[1024,128]{1,0:T(8,128)(2,1)S(1)}, bf16[1024,128]{1,0:T(8,128)(2,1)S(1)}, u32[]{:S(2)}, u32[]{:S(2)}) collective-permute-start(bf16[1024,128]{1,0:T(8,128)(2,1)S(1)} %shard_map.129), channel_id=1, source_target_pairs={{0,8},{1,9},{2,10},{3,11},{4,12},{5,13},{6,14},{7,15},{8,0},{9,1},... | collective-permute-start | bytes 786440 | tf_op jit(solution)/shard_map/ppermute | solution.py:377
  66.1 10.7 %collective-permute-start.3 = (bf16[256,128]{1,0:T(8,128)(2,1)S(1)}, bf16[256,128]{1,0:T(8,128)(2,1)S(1)}, u32[]{:S(2)}, u32[]{:S(2)}) collective-permute-start(bf16[256,128]{1,0:T(8,128)(2,1)S(1)} %bitcast.17), channel_id=1, source_target_pairs={{0,0},{1,16},{2,32},{3,48},{4,64},{5,80},{6,96},{7,112},{8,128},{9... | collective-permute-start | bytes 196616 | tf_op jit(solution)/shard_map/ppermute | solution.py:384
  77.7 23.7 %all-to-all-start.1 = ((bf16[16,128,128]{2,1,0:T(8,128)(2,1)}), bf16[16,128,128]{2,1,0:T(8,128)(2,1)S(1)}, u32[]{:S(2)}, u32[]{:S(2)}) async-start(bf16[16,128,128]{2,1,0:T(8,128)(2,1)} %bitcast.8), calls=%async_computation.1 | async-start | bytes 1048576 | tf_op jit(solution)/shard_map/all_to_all | solution.py:387
  83.8 6.0 %collective-permute-start.4 = (bf16[256,128]{1,0:T(8,128)(2,1)S(1)}, bf16[256,128]{1,0:T(8,128)(2,1)S(1)}, u32[]{:S(2)}, u32[]{:S(2)}) collective-permute-start(bf16[256,128]{1,0:T(8,128)(2,1)S(1)} %bitcast.18), channel_id=1, source_target_pairs={{0,128},{16,144},{32,160},{48,176},{64,192},{80,208},{96,224},{112... | collective-permute-start | bytes 196616 | tf_op jit(solution)/shard_map/ppermute | solution.py:388
  89.8 6.3 %collective-permute-start.5 = (bf16[512,128]{1,0:T(8,128)(2,1)S(1)}, bf16[512,128]{1,0:T(8,128)(2,1)S(1)}, u32[]{:S(2)}, u32[]{:S(2)}) collective-permute-start(bf16[512,128]{1,0:T(8,128)(2,1)S(1)} %get-tuple-element.21), channel_id=1, source_target_pairs={{0,32},{16,48},{32,64},{48,80},{64,96},{80,112},{96,0},{112,16},{1... | collective-permute-start | bytes 393224 | tf_op jit(solution)/shard_map/ppermute | solution.py:391
  93.5 6.6 %collective-permute-start.6 = (bf16[512,128]{1,0:T(8,128)(2,1)S(1)}, bf16[512,128]{1,0:T(8,128)(2,1)S(1)}, u32[]{:S(2)}, u32[]{:S(2)}) collective-permute-start(bf16[512,128]{1,0:T(8,128)(2,1)S(1)} %get-tuple-element.21), channel_id=1, source_target_pairs={{0,64},{16,80},{32,96},{48,112},{64,0},{80,16},{96,32},{112,48},{1... | collective-permute-start | bytes 393224 | tf_op jit(solution)/shard_map/ppermute | solution.py:391
  94.2 7.2 %collective-permute-start.7 = (bf16[512,128]{1,0:T(8,128)(2,1)S(1)}, bf16[512,128]{1,0:T(8,128)(2,1)S(1)}, u32[]{:S(2)}, u32[]{:S(2)}) collective-permute-start(bf16[512,128]{1,0:T(8,128)(2,1)S(1)} %get-tuple-element.21), channel_id=1, source_target_pairs={{0,96},{16,112},{32,0},{48,16},{64,32},{80,48},{96,64},{112,80},{1... | collective-permute-start | bytes 393224 | tf_op jit(solution)/shard_map/ppermute | solution.py:391
  101.4 9.3 %collective-permute-start.8 = (bf16[16,128,128]{2,1,0:T(8,128)(2,1)S(1)}, bf16[16,128,128]{2,1,0:T(8,128)(2,1)S(1)}, u32[]{:S(2)}, u32[]{:S(2)}) collective-permute-start(bf16[16,128,128]{2,1,0:T(8,128)(2,1)S(1)} %all-to-all-done.1.own_ref), channel_id=1, source_target_pairs={{0,8},{1,9},{2,10},{3,11},{4,12},{5,13},{6,14},{7,15},{8,0},{9,1},... | collective-permute-start | bytes 1572872 | tf_op jit(solution)/shard_map/ppermute | solution.py:395
  103.1 7.6 %collective-permute-start.9 = (bf16[2048,128]{1,0:T(8,128)(2,1)S(1)}, bf16[2048,128]{1,0:T(8,128)(2,1)S(1)}, u32[]{:S(2)}, u32[]{:S(2)}) collective-permute-start(bf16[2048,128]{1,0:T(8,128)(2,1)S(1)} %constant_dynamic-update-slice_fusion.2.near_ref), channel_id=1, source_target_pairs={{0,16},{16,0},{32,48},{48,32},{64,80},{80,64},{96,112},{112,96},{1... | collective-permute-start | bytes 1572872 | tf_op jit(solution)/shard_map/ppermute | solution.py:396

commit v5 on v4

--- a/solution.py
+++ b/solution.py
@@ -257,7 +257,7 @@
         out_ref[pl.ds(pl.multiple_of(step * PICK, PICK), PICK), :] = both.T
         return carry
 
-    lax.fori_loop(0, out_ref.shape[0] // PICK, tile, 0)
+    lax.fori_loop(0, out_ref.shape[0] // PICK, tile, 0, unroll=2)
 
 
 def pick(first, count, away, umklapp, sphere, planes):
@@ -370,14 +370,17 @@
     field = [fields(val, spread_cond(psi_cond), 0)]
     sphere = sphere.reshape(NG // HALF, HALF)
     swap = fft_route(lambda y, z: (y + 1, z))
-    came = []
-    for at in (0, 8):
-        sent = pick(at, 8, True, umklapp, sphere, field)
-        sent, *field = lax.optimization_barrier((sent, *field))
-        came.append(lax.ppermute(sent, "fft", swap))
-    kept = pick(0, 16, False, umklapp, sphere, field)
-    came = jnp.concatenate(came)
-    share = (kept.astype(jnp.float32) + came.astype(jnp.float32)).astype(jnp.bfloat16)
+    shares = []
+    sent = [None, None]
+    for i, at in enumerate((0, 8)):
+        sent[i] = pick(at, 8, True, umklapp, sphere, field)
+        sent[i], *field = lax.optimization_barrier((sent[i], *field))
+    came = [lax.ppermute(part, "fft", swap) for part in sent]
+    for i, at in enumerate((0, 8)):
+        kept = pick(at, 8, False, umklapp, sphere, field)
+        shares.append((kept.astype(jnp.float32) + came[i].astype(jnp.float32)).astype(jnp.bfloat16))
+        shares[i], *field = lax.optimization_barrier((shares[i], *field))
+    share = jnp.concatenate(shares)
     spread = lax.all_to_all(share.reshape(16, HALF, 128), "fft", 0, 0)
     rho = spread.reshape(2, 8, HALF, 128).astype(jnp.float32).sum(1).astype(jnp.bfloat16)
     rho = rho.reshape(ROWS, 128)

time: 115 us -> 112 us (0.974)
  waiting for transfers between devices: 34.6 us -> 32.5 us
  Pallas kernels: 29.3 us -> 27.8 us
    ppermute x2, waiting for transfers between devices: 5.45 us -> 3.31 us  [shards(): came = [lax.ppermute(part, 'fft', swap) for part in sent]]
    pallas_call x3 -> x4, Pallas kernels: 11.2 us -> 9.7 us  [pick(): pl.pallas_call(functools.partial(pick_kernel, first, away), in_specs=[pl....]
  transfers between devices with their start and end apart: 11 -> 11, of which waited for: 9 -> 9; matrix products, arithmetic and copies ran while one was open for 0% -> 0% of each run, Pallas kernels for 9% -> 11%
where the time goes in v5:
time: 112 us; the launch traced here: 110 us
  waiting for transfers between devices  32.5 us (29%)
  Pallas kernels  27.8 us (25%)
  blocking collectives  22.9 us (20%)
  starting transfers between devices  21.3 us (19%)
  local copies, waits for them, and re-layouts  4.87 us (4%)
    all_to_all x1, blocking collectives, shards(): spread = lax.all_to_all(share.reshape(16, HALF, 128), 'fft', 0, 0)  22.9 us
    pallas_call x1, Pallas kernels, fields(): pl.pallas_call(field_kernel, grid=(planes, chunks), in_specs=[pl.BlockSpe...  10.6 us
    pallas_call x4, Pallas kernels, pick(): pl.pallas_call(functools.partial(pick_kernel, first, away), in_specs=[pl....  9.7 us
    ppermute x1, waiting for transfers between devices, shards(): own = lax.ppermute(rho, ('ka', 'fft'), mesh_route(lambda k, f: (f, k)))  8.68 us
    ppermute x1, waiting for transfers between devices, shards(): other = lax.ppermute(mine, 'fft', swap)  7.61 us
    all_to_all x1, starting transfers between devices, shards(): mine = lax.all_to_all(copies.reshape(16, HALF, 128), 'fft', 0, 0)  6.07 us
    ppermute x3, waiting for transfers between devices, shards(): lax.ppermute(block, 'ka', ka_route(lambda y, x, c, s=s: (y, x + s, c)))  5.88 us
    ppermute x3, starting transfers between devices, shards(): lax.ppermute(block, 'ka', ka_route(lambda y, x, c, s=s: (y, x + s, c)))  5.68 us
  transfers between devices with their start and end apart: 11, of which 9 were waited for; matrix products, arithmetic and copies ran while one was open for 0% of the time, Pallas kernels for 11%

profile of v5, /device:TPU:62, one launch (start us, length us, event | category | flops | bytes accessed | tf_op | source)
XLA Modules:
  0.0 109.8 jit_solution(11051086498071442479)
XLA Ops:
  0.0 2.1 %collective-permute-start = (bf16[1,2,4,27648]{3,2,1,0:T(4,128)(2,1)}, bf16[1,2,4,27648]{3,2,1,0:T(4,128)(2,1)S(1)}, u32[]{:S(2)}, u32[]{:S(2)}) collective-permute-start(bf16[1,2,4,27648]{3,2,1,0:T(4,128)(2,1)} %param.14), channel_id=1, source_target_pairs={{0,64},{16,80},{32,96},{48,112},{64,128},{80,144},{96,160},{112,17... | collective-permute-start | bytes 1327112 | tf_op jit(solution)/shard_map/ppermute | solution.py:369
  2.1 3.0 %copy-done = bf16[1,3,9216,128]{3,2,1,0:T(8,128)(2,1)S(1)} copy-done((bf16[1,3,9216,128]{3,2,1,0:T(8,128)(2,1)S(1)}, bf16[1,3,9216,128]{3,2,1,0:T(8,128)(2,1)}, u32[]{:S(2)}) %copy-start) | copy-done | bytes 7077912
  5.9 5.0 %shard_map.136.cond_ref = bf16[3,9216,256]{2,1,0:T(8,128)(2,1)S(1)} custom-call(bf16[1,3,9216,128]{3,2,1,0:T(8,128)(2,1)S(1)} %copy-done, bf16[128,256]{1,0:T(8,128)(2,1)S(1)} %copy-done.3), custom_call_target="tpu_custom_call" | custom-call | flops 2000000000 | bytes 20000000 | tf_op jit(solution)/shard_map/pallas_call | solution.py:85
  10.9 2.7 %collective-permute-done = bf16[1,2,4,27648]{3,2,1,0:T(4,128)(2,1)S(1)} collective-permute-done((bf16[1,2,4,27648]{3,2,1,0:T(4,128)(2,1)}, bf16[1,2,4,27648]{3,2,1,0:T(4,128)(2,1)S(1)}, u32[]{:S(2)}, u32[]{:S(2)}) %collective-permute-start) | collective-permute-done | bytes 442400 | tf_op jit(solution)/shard_map/ppermute | solution.py:369
  13.6 10.6 %shard_map.137.refs_0_ = bf16[3,256,768]{2,1,0:T(8,128)(2,1)S(1)} custom-call(bf16[2,4,27648]{2,1,0:T(4,128)(2,1)S(1)} %bitcast.10, bf16[3,9216,256]{2,1,0:T(8,128)(2,1)S(1)} %shard_map.136.cond_ref, bf16[128,256]{1,0:T(8,128)(2,1)S(1)} %copy-done.4), custom_call_target="tpu_custom_call" | custom-call | flops 2000000000 | bytes 3000000 | tf_op jit(solution)/shard_map/pallas_call | solution.py:182
  24.3 2.4 %shard_map.138 = bf16[1024,128]{1,0:T(8,128)(2,1)S(1)} custom-call(s32[16]{0:T(128)S(1)} %copy-done.7, s32[32,128]{1,0:T(8,128)S(1)} %bitcast.11, bf16[16,16,32]{2,1,0:T(8,128)(2,1)S(1)} %copy-done.1, bf16[3,256,768]{2,1,0:T(8,128)(2,1)S(1)} %shard_map.137.refs_0_), custom_call_target="tpu_custom_call" | custom-call | flops 100000000 | bytes 500000 | tf_op jit(solution)/shard_map/pallas_call | solution.py:265
  27.6 2.4 %shard_map.139 = bf16[1024,128]{1,0:T(8,128)(2,1)S(1)} custom-call(s32[16]{0:T(128)S(1)} %copy-done.7, s32[32,128]{1,0:T(8,128)S(1)} %bitcast.12, bf16[16,16,32]{2,1,0:T(8,128)(2,1)S(1)} %copy-done.1, bf16[3,256,768]{2,1,0:T(8,128)(2,1)S(1)} %shard_map.137.refs_0_), custom_call_target="tpu_custom_call" | custom-call | flops 100000000 | bytes 500000 | tf_op jit(solution)/shard_map/pallas_call | solution.py:265
  30.0 1.4 %collective-permute-start.2 = (bf16[1024,128]{1,0:T(8,128)(2,1)S(1)}, bf16[1024,128]{1,0:T(8,128)(2,1)S(1)}, u32[]{:S(2)}, u32[]{:S(2)}) collective-permute-start(bf16[1024,128]{1,0:T(8,128)(2,1)S(1)} %shard_map.139), channel_id=1, source_target_pairs={{0,8},{1,9},{2,10},{3,11},{4,12},{5,13},{6,14},{7,15},{8,0},{9,1},... | collective-permute-start | bytes 786440 | tf_op jit(solution)/shard_map/ppermute | solution.py:378
  31.4 2.4 %shard_map.140 = bf16[1024,128]{1,0:T(8,128)(2,1)S(1)} custom-call(s32[16]{0:T(128)S(1)} %copy-done.7, s32[32,128]{1,0:T(8,128)S(1)} %bitcast.13, bf16[16,16,32]{2,1,0:T(8,128)(2,1)S(1)} %copy-done.1, bf16[3,256,768]{2,1,0:T(8,128)(2,1)S(1)} %shard_map.137.refs_0_), custom_call_target="tpu_custom_call" | custom-call | flops 100000000 | bytes 500000 | tf_op jit(solution)/shard_map/pallas_call | solution.py:265
  33.8 2.3 %collective-permute-done.1 = bf16[1024,128]{1,0:T(8,128)(2,1)S(1)} collective-permute-done((bf16[1024,128]{1,0:T(8,128)(2,1)S(1)}, bf16[1024,128]{1,0:T(8,128)(2,1)S(1)}, u32[]{:S(2)}, u32[]{:S(2)}) %collective-permute-start.1) | collective-permute-done | bytes 262176 | tf_op jit(solution)/shard_map/ppermute | solution.py:378
  36.1 2.4 %shard_map.141 = bf16[1024,128]{1,0:T(8,128)(2,1)S(1)} custom-call(s32[16]{0:T(128)S(1)} %copy-done.7, s32[32,128]{1,0:T(8,128)S(1)} %bitcast.14, bf16[16,16,32]{2,1,0:T(8,128)(2,1)S(1)} %copy-done.1, bf16[3,256,768]{2,1,0:T(8,128)(2,1)S(1)} %shard_map.137.refs_0_), custom_call_target="tpu_custom_call" | custom-call | flops 100000000 | bytes 500000 | tf_op jit(solution)/shard_map/pallas_call | solution.py:265
  39.7 22.9 %all_to_all.10 = bf16[16,128,128]{2,1,0:T(8,128)(2,1)S(1)} all-to-all(bf16[16,128,128]{2,1,0:T(8,128)(2,1)S(1)} %bitcast.17), channel_id=1, replica_groups=mesh['ka'=16,'fft'=16] {'fft'}, dimensions={0} | all-to-all | bytes 1048576 | tf_op jit(solution)/shard_map/all_to_all | solution.py:384
  62.7 2.0 %collective-permute-start.3 = (bf16[256,128]{1,0:T(8,128)(2,1)S(1)}, bf16[256,128]{1,0:T(8,128)(2,1)S(1)}, u32[]{:S(2)}, u32[]{:S(2)}) collective-permute-start(bf16[256,128]{1,0:T(8,128)(2,1)S(1)} %bitcast.18), channel_id=1, source_target_pairs={{0,0},{1,16},{2,32},{3,48},{4,64},{5,80},{6,96},{7,112},{8,128},{9... | collective-permute-start | bytes 196616 | tf_op jit(solution)/shard_map/ppermute | solution.py:387
  64.7 8.7 %collective-permute-done.3 = bf16[256,128]{1,0:T(8,128)(2,1)S(1)} collective-permute-done((bf16[256,128]{1,0:T(8,128)(2,1)S(1)}, bf16[256,128]{1,0:T(8,128)(2,1)S(1)}, u32[]{:S(2)}, u32[]{:S(2)}) %collective-permute-start.3) | collective-permute-done | bytes 65568 | tf_op jit(solution)/shard_map/ppermute | solution.py:387
  74.3 6.1 %all-to-all-start.1 = ((bf16[16,128,128]{2,1,0:T(8,128)(2,1)}), bf16[16,128,128]{2,1,0:T(8,128)(2,1)S(1)}, u32[]{:S(2)}, u32[]{:S(2)}) async-start(bf16[16,128,128]{2,1,0:T(8,128)(2,1)} %bitcast.8), calls=%async_computation.1 | async-start | bytes 1048576 | tf_op jit(solution)/shard_map/all_to_all | solution.py:390
  80.3 1.6 %collective-permute-start.4 = (bf16[256,128]{1,0:T(8,128)(2,1)S(1)}, bf16[256,128]{1,0:T(8,128)(2,1)S(1)}, u32[]{:S(2)}, u32[]{:S(2)}) collective-permute-start(bf16[256,128]{1,0:T(8,128)(2,1)S(1)} %bitcast.19), channel_id=1, source_target_pairs={{0,128},{16,144},{32,160},{48,176},{64,192},{80,208},{96,224},{112... | collective-permute-start | bytes 196616 | tf_op jit(solution)/shard_map/ppermute | solution.py:391
  82.0 4.3 %collective-permute-done.4 = bf16[256,128]{1,0:T(8,128)(2,1)S(1)} collective-permute-done((bf16[256,128]{1,0:T(8,128)(2,1)S(1)}, bf16[256,128]{1,0:T(8,128)(2,1)S(1)}, u32[]{:S(2)}, u32[]{:S(2)}) %collective-permute-start.4) | collective-permute-done | bytes 65568 | tf_op jit(solution)/shard_map/ppermute | solution.py:391
  86.3 3.7 %collective-permute-start.5 = (bf16[512,128]{1,0:T(8,128)(2,1)S(1)}, bf16[512,128]{1,0:T(8,128)(2,1)S(1)}, u32[]{:S(2)}, u32[]{:S(2)}) collective-permute-start(bf16[512,128]{1,0:T(8,128)(2,1)S(1)} %get-tuple-element.27), channel_id=1, source_target_pairs={{0,32},{16,48},{32,64},{48,80},{64,96},{80,112},{96,0},{112,16},{1... | collective-permute-start | bytes 393224 | tf_op jit(solution)/shard_map/ppermute | solution.py:394
  90.7 1.3 %collective-permute-start.7 = (bf16[512,128]{1,0:T(8,128)(2,1)S(1)}, bf16[512,128]{1,0:T(8,128)(2,1)S(1)}, u32[]{:S(2)}, u32[]{:S(2)}) collective-permute-start(bf16[512,128]{1,0:T(8,128)(2,1)S(1)} %get-tuple-element.27), channel_id=1, source_target_pairs={{0,96},{16,112},{32,0},{48,16},{64,32},{80,48},{96,64},{112,80},{1... | collective-permute-start | bytes 393224 | tf_op jit(solution)/shard_map/ppermute | solution.py:394
  92.6 4.0 %collective-permute-done.6 = bf16[512,128]{1,0:T(8,128)(2,1)S(1)} collective-permute-done((bf16[512,128]{1,0:T(8,128)(2,1)S(1)}, bf16[512,128]{1,0:T(8,128)(2,1)S(1)}, u32[]{:S(2)}, u32[]{:S(2)}) %collective-permute-start.6) | collective-permute-done | bytes 131104 | tf_op jit(solution)/shard_map/ppermute | solution.py:394
  96.7 1.3 %collective-permute-done.7 = bf16[512,128]{1,0:T(8,128)(2,1)S(1)} collective-permute-done((bf16[512,128]{1,0:T(8,128)(2,1)S(1)}, bf16[512,128]{1,0:T(8,128)(2,1)S(1)}, u32[]{:S(2)}, u32[]{:S(2)}) %collective-permute-start.7) | collective-permute-done | bytes 131104 | tf_op jit(solution)/shard_map/ppermute | solution.py:394
  98.0 1.7 %collective-permute-start.8 = (bf16[16,128,128]{2,1,0:T(8,128)(2,1)S(1)}, bf16[16,128,128]{2,1,0:T(8,128)(2,1)S(1)}, u32[]{:S(2)}, u32[]{:S(2)}) collective-permute-start(bf16[16,128,128]{2,1,0:T(8,128)(2,1)S(1)} %all-to-all-done.1.own_ref), channel_id=1, source_target_pairs={{0,8},{1,9},{2,10},{3,11},{4,12},{5,13},{6,14},{7,15},{8,0},{9,1},... | collective-permute-start | bytes 1572872 | tf_op jit(solution)/shard_map/ppermute | solution.py:398
  99.6 7.6 %collective-permute-done.8.other_ref = bf16[16,128,128]{2,1,0:T(8,128)(2,1)S(1)} collective-permute-done((bf16[16,128,128]{2,1,0:T(8,128)(2,1)S(1)}, bf16[16,128,128]{2,1,0:T(8,128)(2,1)S(1)}, u32[]{:S(2)}, u32[]{:S(2)}) %collective-permute-start.8) | collective-permute-done | bytes 524320 | tf_op jit(solution)/shard_map/ppermute | solution.py:398
  107.3 2.6 %shard_map.142 = f32[256,2,256]{2,1,0:T(2,128)} custom-call(f32[2,16]{1,0:T(2,128)S(1)} %bitcast.15, s32[2,16]{1,0:T(2,128)S(1)} %bitcast.16, f32[16,32]{1,0:T(8,128)S(1)} %copy-done.5, s32[16,32]{1,0:T(8,128)S(1)} %copy-done.6, bf16[16,128,128]{2,1,0:T(8,128)(2,1)S(1)} %all-to-all-done.1.own_ref, ...), custom_call_target="tpu_custom_call" | custom-call | flops 600000000 | bytes 4000000 | tf_op jit(solution)/shard_map/pallas_call | solution.py:326
  (36 shorter events, 5.2 us)
Async XLA Ops:
  0.0 13.6 %collective-permute-start = (bf16[1,2,4,27648]{3,2,1,0:T(4,128)(2,1)}, bf16[1,2,4,27648]{3,2,1,0:T(4,128)(2,1)S(1)}, u32[]{:S(2)}, u32[]{:S(2)}) collective-permute-start(bf16[1,2,4,27648]{3,2,1,0:T(4,128)(2,1)} %param.14), channel_id=1, source_target_pairs={{0,64},{16,80},{32,96},{48,112},{64,128},{80,144},{96,160},{112,17... | collective-permute-start | bytes 1327112 | tf_op jit(solution)/shard_map/ppermute | solution.py:369
  2.1 3.0 %copy-start = (bf16[1,3,9216,128]{3,2,1,0:T(8,128)(2,1)S(1)}, bf16[1,3,9216,128]{3,2,1,0:T(8,128)(2,1)}, u32[]{:S(2)}) copy-start(bf16[1,3,9216,128]{3,2,1,0:T(8,128)(2,1)} %cond_ref.1) | copy-start | bytes 21233668
  5.1 0.8 copy-start.3
  5.9 7.7 %copy-start.4 = (bf16[128,256]{1,0:T(8,128)(2,1)S(1)}, bf16[128,256]{1,0:T(8,128)(2,1)}, u32[]{:S(2)}) copy-start(bf16[128,256]{1,0:T(8,128)(2,1)} %constant.10.clone.table_ref) | copy-start | bytes 196612
  13.6 10.6 %copy-start.1 = (bf16[16,16,32]{2,1,0:T(8,128)(2,1)S(1)}, bf16[16,16,32]{2,1,0:T(8,128)(2,1)}, u32[]{:S(2)}) copy-start(bf16[16,16,32]{2,1,0:T(8,128)(2,1)} %constant.11.clone.xt_ref) | copy-start | bytes 49156
  13.6 10.7 %copy-start.2 = (s32[4096]{0:T(1024)S(1)}, s32[4096]{0:T(1024)}, u32[]{:S(2)}) copy-start(s32[4096]{0:T(1024)} %param.21) | copy-start | bytes 49156
  13.6 10.7 %copy-start.7 = (s32[16]{0:T(128)S(1)}, s32[16]{0:T(128)}, u32[]{:S(2)}) copy-start(s32[16]{0:T(128)} %umklapp_ref.7) | copy-start | bytes 196
  24.2 83.0 %copy-start.5 = (f32[16,32]{1,0:T(8,128)S(1)}, f32[16,32]{1,0:T(8,128)}, u32[]{:S(2)}) copy-start(f32[16,32]{1,0:T(8,128)} %e_cond_ref.1) | copy-start | bytes 6148
  24.2 83.0 %copy-start.6 = (s32[16,32]{1,0:T(8,128)S(1)}, s32[16,32]{1,0:T(8,128)}, u32[]{:S(2)}) copy-start(s32[16,32]{1,0:T(8,128)} %occ_cond_ref.1) | copy-start | bytes 6148
  24.2 83.0 %copy-start.8 = (f32[16,2]{0,1:T(2,128)S(1)}, f32[16,2]{0,1:T(2,128)}, u32[]{:S(2)}) copy-start(f32[16,2]{0,1:T(2,128)} %param.16) | copy-start | bytes 388
  24.3 83.0 %copy-start.9 = (s32[16,2]{0,1:T(2,128)S(1)}, s32[16,2]{0,1:T(2,128)}, u32[]{:S(2)}) copy-start(s32[16,2]{0,1:T(2,128)} %param.18) | copy-start | bytes 388
  26.7 9.3 %collective-permute-start.1 = (bf16[1024,128]{1,0:T(8,128)(2,1)S(1)}, bf16[1024,128]{1,0:T(8,128)(2,1)S(1)}, u32[]{:S(2)}, u32[]{:S(2)}) collective-permute-start(bf16[1024,128]{1,0:T(8,128)(2,1)S(1)} %shard_map.138), channel_id=1, source_target_pairs={{0,8},{1,9},{2,10},{3,11},{4,12},{5,13},{6,14},{7,15},{8,0},{9,1},... | collective-permute-start | bytes 786440 | tf_op jit(solution)/shard_map/ppermute | solution.py:378
  30.0 9.6 %collective-permute-start.2 = (bf16[1024,128]{1,0:T(8,128)(2,1)S(1)}, bf16[1024,128]{1,0:T(8,128)(2,1)S(1)}, u32[]{:S(2)}, u32[]{:S(2)}) collective-permute-start(bf16[1024,128]{1,0:T(8,128)(2,1)S(1)} %shard_map.139), channel_id=1, source_target_pairs={{0,8},{1,9},{2,10},{3,11},{4,12},{5,13},{6,14},{7,15},{8,0},{9,1},... | collective-permute-start | bytes 786440 | tf_op jit(solution)/shard_map/ppermute | solution.py:378
  62.7 10.7 %collective-permute-start.3 = (bf16[256,128]{1,0:T(8,128)(2,1)S(1)}, bf16[256,128]{1,0:T(8,128)(2,1)S(1)}, u32[]{:S(2)}, u32[]{:S(2)}) collective-permute-start(bf16[256,128]{1,0:T(8,128)(2,1)S(1)} %bitcast.18), channel_id=1, source_target_pairs={{0,0},{1,16},{2,32},{3,48},{4,64},{5,80},{6,96},{7,112},{8,128},{9... | collective-permute-start | bytes 196616 | tf_op jit(solution)/shard_map/ppermute | solution.py:387
  74.3 23.7 %all-to-all-start.1 = ((bf16[16,128,128]{2,1,0:T(8,128)(2,1)}), bf16[16,128,128]{2,1,0:T(8,128)(2,1)S(1)}, u32[]{:S(2)}, u32[]{:S(2)}) async-start(bf16[16,128,128]{2,1,0:T(8,128)(2,1)} %bitcast.8), calls=%async_computation.1 | async-start | bytes 1048576 | tf_op jit(solution)/shard_map/all_to_all | solution.py:390
  80.3 6.0 %collective-permute-start.4 = (bf16[256,128]{1,0:T(8,128)(2,1)S(1)}, bf16[256,128]{1,0:T(8,128)(2,1)S(1)}, u32[]{:S(2)}, u32[]{:S(2)}) collective-permute-start(bf16[256,128]{1,0:T(8,128)(2,1)S(1)} %bitcast.19), channel_id=1, source_target_pairs={{0,128},{16,144},{32,160},{48,176},{64,192},{80,208},{96,224},{112... | collective-permute-start | bytes 196616 | tf_op jit(solution)/shard_map/ppermute | solution.py:391
  86.3 6.3 %collective-permute-start.5 = (bf16[512,128]{1,0:T(8,128)(2,1)S(1)}, bf16[512,128]{1,0:T(8,128)(2,1)S(1)}, u32[]{:S(2)}, u32[]{:S(2)}) collective-permute-start(bf16[512,128]{1,0:T(8,128)(2,1)S(1)} %get-tuple-element.27), channel_id=1, source_target_pairs={{0,32},{16,48},{32,64},{48,80},{64,96},{80,112},{96,0},{112,16},{1... | collective-permute-start | bytes 393224 | tf_op jit(solution)/shard_map/ppermute | solution.py:394
  90.1 6.6 %collective-permute-start.6 = (bf16[512,128]{1,0:T(8,128)(2,1)S(1)}, bf16[512,128]{1,0:T(8,128)(2,1)S(1)}, u32[]{:S(2)}, u32[]{:S(2)}) collective-permute-start(bf16[512,128]{1,0:T(8,128)(2,1)S(1)} %get-tuple-element.27), channel_id=1, source_target_pairs={{0,64},{16,80},{32,96},{48,112},{64,0},{80,16},{96,32},{112,48},{1... | collective-permute-start | bytes 393224 | tf_op jit(solution)/shard_map/ppermute | solution.py:394
  90.7 7.2 %collective-permute-start.7 = (bf16[512,128]{1,0:T(8,128)(2,1)S(1)}, bf16[512,128]{1,0:T(8,128)(2,1)S(1)}, u32[]{:S(2)}, u32[]{:S(2)}) collective-permute-start(bf16[512,128]{1,0:T(8,128)(2,1)S(1)} %get-tuple-element.27), channel_id=1, source_target_pairs={{0,96},{16,112},{32,0},{48,16},{64,32},{80,48},{96,64},{112,80},{1... | collective-permute-start | bytes 393224 | tf_op jit(solution)/shard_map/ppermute | solution.py:394
  98.0 9.3 %collective-permute-start.8 = (bf16[16,128,128]{2,1,0:T(8,128)(2,1)S(1)}, bf16[16,128,128]{2,1,0:T(8,128)(2,1)S(1)}, u32[]{:S(2)}, u32[]{:S(2)}) collective-permute-start(bf16[16,128,128]{2,1,0:T(8,128)(2,1)S(1)} %all-to-all-done.1.own_ref), channel_id=1, source_target_pairs={{0,8},{1,9},{2,10},{3,11},{4,12},{5,13},{6,14},{7,15},{8,0},{9,1},... | collective-permute-start | bytes 1572872 | tf_op jit(solution)/shard_map/ppermute | solution.py:398
  99.6 7.6 %collective-permute-start.9 = (bf16[2048,128]{1,0:T(8,128)(2,1)S(1)}, bf16[2048,128]{1,0:T(8,128)(2,1)S(1)}, u32[]{:S(2)}, u32[]{:S(2)}) collective-permute-start(bf16[2048,128]{1,0:T(8,128)(2,1)S(1)} %constant_dynamic-update-slice_fusion.2.near_ref), channel_id=1, source_target_pairs={{0,16},{16,0},{32,48},{48,32},{64,80},{80,64},{96,112},{112,96},{1... | collective-permute-start | bytes 1572872 | tf_op jit(solution)/shard_map/ppermute | solution.py:399

commit v6 on v5

--- a/solution.py
+++ b/solution.py
@@ -18,7 +18,7 @@
 COLS = 768
 ROWS = 256
 HALF = 128
-YCHUNK = 32
+YCHUNK = 48
 ZROW = 104
 PICK = 256
 
@@ -257,7 +257,7 @@
         out_ref[pl.ds(pl.multiple_of(step * PICK, PICK), PICK), :] = both.T
         return carry
 
-    lax.fori_loop(0, out_ref.shape[0] // PICK, tile, 0, unroll=2)
+    lax.fori_loop(0, out_ref.shape[0] // PICK, tile, 0, unroll=4)
 
 
 def pick(first, count, away, umklapp, sphere, planes):
@@ -385,14 +385,14 @@
     rho = spread.reshape(2, 8, HALF, 128).astype(jnp.float32).sum(1).astype(jnp.bfloat16)
     rho = rho.reshape(ROWS, 128)
     own = lax.ppermute(rho, ("ka", "fft"), mesh_route(lambda k, f: (f, k)))
-    copies = jnp.broadcast_to(own.reshape(2, 1, HALF, 128), (2, 8, HALF, 128))
-    copies, rho = lax.optimization_barrier((copies, rho))
-    mine = lax.all_to_all(copies.reshape(16, HALF, 128), "fft", 0, 0)
     across = lax.ppermute(rho, "ka", ka_route(lambda y, x, c: (y + 1, x, c)))
     block = jnp.concatenate([rho, across])
+    own, block = lax.optimization_barrier((own, block))
     ring = [
         lax.ppermute(block, "ka", ka_route(lambda y, x, c, s=s: (y, x + s, c))) for s in (1, 2, 3)
     ]
+    copies = jnp.broadcast_to(own.reshape(2, 1, HALF, 128), (2, 8, HALF, 128))
+    mine = lax.all_to_all(copies.reshape(16, HALF, 128), "fft", 0, 0)
     near = jnp.concatenate([block] + ring)
     near, mine = lax.optimization_barrier((near, mine))
     other = lax.ppermute(mine, "fft", swap)

time: 112 us -> 111 us (level); the launches traced: 110 us -> 111 us
  waiting for transfers between devices: 32.5 us -> 35.4 us
  Pallas kernels: 27.8 us -> 26.4 us
    all_to_all x1, waiting for transfers between devices: 0.01 us -> 5 us  [shards(): mine = lax.all_to_all(copies.reshape(16, HALF, 128), 'fft', 0, 0)]
    ppermute x1, waiting for transfers between devices: 7.61 us -> 12.1 us  [shards(): other = lax.ppermute(mine, 'fft', swap)]
    ppermute x3, waiting for transfers between devices: 5.88 us -> 2.87 us  [shards(): lax.ppermute(block, 'ka', ka_route(lambda y, x, c, s=s: (y, x + s, c)))]
    ppermute x1, waiting for transfers between devices: 8.68 us -> 6.14 us  [shards(): own = lax.ppermute(rho, ('ka', 'fft'), mesh_route(lambda k, f: (f, k)))]
    ppermute x3, starting transfers between devices: 5.68 us -> 7.5 us  [shards(): lax.ppermute(block, 'ka', ka_route(lambda y, x, c, s=s: (y, x + s, c)))]
    ppermute x1, waiting for transfers between devices: 4.3 us -> 2.63 us  [shards(): across = lax.ppermute(rho, 'ka', ka_route(lambda y, x, c: (y + 1, x, c)))]
    ppermute x1, starting transfers between devices: 1.66 us -> 0.31 us  [shards(): other = lax.ppermute(mine, 'fft', swap)]
    unnamed x23 -> x20, local copies, waits for them, and re-layouts: 3.93 us -> 3.89 us
  transfers between devices with their start and end apart: 11 -> 11, of which waited for: 9 -> 9; matrix products, arithmetic and copies ran while one was open for 0% -> 0% of each run, Pallas kernels for 11% -> 10%
where the time goes in v6:
time: 111 us
  waiting for transfers between devices  35.4 us (32%)
  Pallas kernels  26.4 us (24%)
  blocking collectives  22.9 us (21%)
  starting transfers between devices  21.1 us (19%)
  local copies, waits for them, and re-layouts  4.78 us (4%)
    all_to_all x1, blocking collectives, shards(): spread = lax.all_to_all(share.reshape(16, HALF, 128), 'fft', 0, 0)  22.9 us
    ppermute x1, waiting for transfers between devices, shards(): other = lax.ppermute(mine, 'fft', swap)  12.1 us
    pallas_call x1, Pallas kernels, fields(): pl.pallas_call(field_kernel, grid=(planes, chunks), in_specs=[pl.BlockSpe...  9.97 us
    pallas_call x4, Pallas kernels, pick(): pl.pallas_call(functools.partial(pick_kernel, first, away), in_specs=[pl....  8.88 us
    ppermute x3, starting transfers between devices, shards(): lax.ppermute(block, 'ka', ka_route(lambda y, x, c, s=s: (y, x + s, c)))  7.5 us
    ppermute x1, waiting for transfers between devices, shards(): own = lax.ppermute(rho, ('ka', 'fft'), mesh_route(lambda k, f: (f, k)))  6.14 us
    all_to_all x1, starting transfers between devices, shards(): mine = lax.all_to_all(copies.reshape(16, HALF, 128), 'fft', 0, 0)  5.59 us
    all_to_all x1, waiting for transfers between devices, shards(): mine = lax.all_to_all(copies.reshape(16, HALF, 128), 'fft', 0, 0)  5 us
  transfers between devices with their start and end apart: 11, of which 9 were waited for; matrix products, arithmetic and copies ran while one was open for 0% of the time, Pallas kernels for 10%

profile of v6, /device:TPU:62, one launch (start us, length us, event | category | flops | bytes accessed | tf_op | source)
XLA Modules:
  0.0 111.0 jit_solution(4814778282973922526)
XLA Ops:
  0.0 2.1 %collective-permute-start = (bf16[1,2,4,27648]{3,2,1,0:T(4,128)(2,1)}, bf16[1,2,4,27648]{3,2,1,0:T(4,128)(2,1)S(1)}, u32[]{:S(2)}, u32[]{:S(2)}) collective-permute-start(bf16[1,2,4,27648]{3,2,1,0:T(4,128)(2,1)} %param.14), channel_id=1, source_target_pairs={{0,64},{16,80},{32,96},{48,112},{64,128},{80,144},{96,160},{112,17... | collective-permute-start | bytes 1327112 | tf_op jit(solution)/shard_map/ppermute | solution.py:369
  2.1 3.0 %copy-done = bf16[1,3,9216,128]{3,2,1,0:T(8,128)(2,1)S(1)} copy-done((bf16[1,3,9216,128]{3,2,1,0:T(8,128)(2,1)S(1)}, bf16[1,3,9216,128]{3,2,1,0:T(8,128)(2,1)}, u32[]{:S(2)}) %copy-start) | copy-done | bytes 7077912
  5.9 5.0 %shard_map.136.cond_ref = bf16[3,9216,256]{2,1,0:T(8,128)(2,1)S(1)} custom-call(bf16[1,3,9216,128]{3,2,1,0:T(8,128)(2,1)S(1)} %copy-done, bf16[128,256]{1,0:T(8,128)(2,1)S(1)} %copy-done.3), custom_call_target="tpu_custom_call" | custom-call | flops 2000000000 | bytes 20000000 | tf_op jit(solution)/shard_map/pallas_call | solution.py:85
  10.9 2.7 %collective-permute-done = bf16[1,2,4,27648]{3,2,1,0:T(4,128)(2,1)S(1)} collective-permute-done((bf16[1,2,4,27648]{3,2,1,0:T(4,128)(2,1)}, bf16[1,2,4,27648]{3,2,1,0:T(4,128)(2,1)S(1)}, u32[]{:S(2)}, u32[]{:S(2)}) %collective-permute-start) | collective-permute-done | bytes 442400 | tf_op jit(solution)/shard_map/ppermute | solution.py:369
  13.6 10.0 %shard_map.137.refs_0_ = bf16[3,256,768]{2,1,0:T(8,128)(2,1)S(1)} custom-call(bf16[2,4,27648]{2,1,0:T(4,128)(2,1)S(1)} %bitcast.10, bf16[3,9216,256]{2,1,0:T(8,128)(2,1)S(1)} %shard_map.136.cond_ref, bf16[128,256]{1,0:T(8,128)(2,1)S(1)} %copy-done.4), custom_call_target="tpu_custom_call" | custom-call | flops 2000000000 | bytes 3000000 | tf_op jit(solution)/shard_map/pallas_call | solution.py:182
  23.7 2.2 %shard_map.138 = bf16[1024,128]{1,0:T(8,128)(2,1)S(1)} custom-call(s32[16]{0:T(128)S(1)} %copy-done.7, s32[32,128]{1,0:T(8,128)S(1)} %bitcast.11, bf16[16,16,32]{2,1,0:T(8,128)(2,1)S(1)} %copy-done.1, bf16[3,256,768]{2,1,0:T(8,128)(2,1)S(1)} %shard_map.137.refs_0_), custom_call_target="tpu_custom_call" | custom-call | flops 100000000 | bytes 500000 | tf_op jit(solution)/shard_map/pallas_call | solution.py:265
  26.8 2.2 %shard_map.139 = bf16[1024,128]{1,0:T(8,128)(2,1)S(1)} custom-call(s32[16]{0:T(128)S(1)} %copy-done.7, s32[32,128]{1,0:T(8,128)S(1)} %bitcast.12, bf16[16,16,32]{2,1,0:T(8,128)(2,1)S(1)} %copy-done.1, bf16[3,256,768]{2,1,0:T(8,128)(2,1)S(1)} %shard_map.137.refs_0_), custom_call_target="tpu_custom_call" | custom-call | flops 100000000 | bytes 500000 | tf_op jit(solution)/shard_map/pallas_call | solution.py:265
  29.0 1.4 %collective-permute-start.2 = (bf16[1024,128]{1,0:T(8,128)(2,1)S(1)}, bf16[1024,128]{1,0:T(8,128)(2,1)S(1)}, u32[]{:S(2)}, u32[]{:S(2)}) collective-permute-start(bf16[1024,128]{1,0:T(8,128)(2,1)S(1)} %shard_map.139), channel_id=1, source_target_pairs={{0,8},{1,9},{2,10},{3,11},{4,12},{5,13},{6,14},{7,15},{8,0},{9,1},... | collective-permute-start | bytes 786440 | tf_op jit(solution)/shard_map/ppermute | solution.py:378
  30.4 2.2 %shard_map.140 = bf16[1024,128]{1,0:T(8,128)(2,1)S(1)} custom-call(s32[16]{0:T(128)S(1)} %copy-done.7, s32[32,128]{1,0:T(8,128)S(1)} %bitcast.13, bf16[16,16,32]{2,1,0:T(8,128)(2,1)S(1)} %copy-done.1, bf16[3,256,768]{2,1,0:T(8,128)(2,1)S(1)} %shard_map.137.refs_0_), custom_call_target="tpu_custom_call" | custom-call | flops 100000000 | bytes 500000 | tf_op jit(solution)/shard_map/pallas_call | solution.py:265
  32.6 2.7 %collective-permute-done.1 = bf16[1024,128]{1,0:T(8,128)(2,1)S(1)} collective-permute-done((bf16[1024,128]{1,0:T(8,128)(2,1)S(1)}, bf16[1024,128]{1,0:T(8,128)(2,1)S(1)}, u32[]{:S(2)}, u32[]{:S(2)}) %collective-permute-start.1) | collective-permute-done | bytes 262176 | tf_op jit(solution)/shard_map/ppermute | solution.py:378
  35.3 2.2 %shard_map.141 = bf16[1024,128]{1,0:T(8,128)(2,1)S(1)} custom-call(s32[16]{0:T(128)S(1)} %copy-done.7, s32[32,128]{1,0:T(8,128)S(1)} %bitcast.14, bf16[16,16,32]{2,1,0:T(8,128)(2,1)S(1)} %copy-done.1, bf16[3,256,768]{2,1,0:T(8,128)(2,1)S(1)} %shard_map.137.refs_0_), custom_call_target="tpu_custom_call" | custom-call | flops 100000000 | bytes 500000 | tf_op jit(solution)/shard_map/pallas_call | solution.py:265
  37.6 1.2 %collective-permute-done.2 = bf16[1024,128]{1,0:T(8,128)(2,1)S(1)} collective-permute-done((bf16[1024,128]{1,0:T(8,128)(2,1)S(1)}, bf16[1024,128]{1,0:T(8,128)(2,1)S(1)}, u32[]{:S(2)}, u32[]{:S(2)}) %collective-permute-start.2) | collective-permute-done | bytes 262176 | tf_op jit(solution)/shard_map/ppermute | solution.py:378
  38.9 22.9 %all_to_all.10 = bf16[16,128,128]{2,1,0:T(8,128)(2,1)S(1)} all-to-all(bf16[16,128,128]{2,1,0:T(8,128)(2,1)S(1)} %bitcast.17), channel_id=1, replica_groups=mesh['ka'=16,'fft'=16] {'fft'}, dimensions={0} | all-to-all | bytes 1048576 | tf_op jit(solution)/shard_map/all_to_all | solution.py:384
  61.9 1.5 %collective-permute-start.4 = (bf16[256,128]{1,0:T(8,128)(2,1)S(1)}, bf16[256,128]{1,0:T(8,128)(2,1)S(1)}, u32[]{:S(2)}, u32[]{:S(2)}) collective-permute-start(bf16[256,128]{1,0:T(8,128)(2,1)S(1)} %bitcast.18), channel_id=1, source_target_pairs={{0,128},{16,144},{32,160},{48,176},{64,192},{80,208},{96,224},{112... | collective-permute-start | bytes 196616 | tf_op jit(solution)/shard_map/ppermute | solution.py:388
  63.4 1.9 %collective-permute-start.3 = (bf16[256,128]{1,0:T(8,128)(2,1)S(1)}, bf16[256,128]{1,0:T(8,128)(2,1)S(1)}, u32[]{:S(2)}, u32[]{:S(2)}) collective-permute-start(bf16[256,128]{1,0:T(8,128)(2,1)S(1)} %bitcast.19), channel_id=1, source_target_pairs={{0,0},{1,16},{2,32},{3,48},{4,64},{5,80},{6,96},{7,112},{8,128},{9... | collective-permute-start | bytes 196616 | tf_op jit(solution)/shard_map/ppermute | solution.py:387
  65.3 2.6 %collective-permute-done.4 = bf16[256,128]{1,0:T(8,128)(2,1)S(1)} collective-permute-done((bf16[256,128]{1,0:T(8,128)(2,1)S(1)}, bf16[256,128]{1,0:T(8,128)(2,1)S(1)}, u32[]{:S(2)}, u32[]{:S(2)}) %collective-permute-start.4) | collective-permute-done | bytes 65568 | tf_op jit(solution)/shard_map/ppermute | solution.py:388
  67.9 6.1 %collective-permute-done.3 = bf16[256,128]{1,0:T(8,128)(2,1)S(1)} collective-permute-done((bf16[256,128]{1,0:T(8,128)(2,1)S(1)}, bf16[256,128]{1,0:T(8,128)(2,1)S(1)}, u32[]{:S(2)}, u32[]{:S(2)}) %collective-permute-start.3) | collective-permute-done | bytes 65568 | tf_op jit(solution)/shard_map/ppermute | solution.py:387
  75.0 5.6 %all-to-all-start.1 = ((bf16[16,128,128]{2,1,0:T(8,128)(2,1)}), bf16[16,128,128]{2,1,0:T(8,128)(2,1)S(1)}, u32[]{:S(2)}, u32[]{:S(2)}) async-start(bf16[16,128,128]{2,1,0:T(8,128)(2,1)} %bitcast.8), calls=%async_computation.1 | async-start | bytes 1048576 | tf_op jit(solution)/shard_map/all_to_all | solution.py:395
  81.1 4.9 %collective-permute-start.6 = (bf16[512,128]{1,0:T(8,128)(2,1)S(1)}, bf16[512,128]{1,0:T(8,128)(2,1)S(1)}, u32[]{:S(2)}, u32[]{:S(2)}) collective-permute-start(bf16[512,128]{1,0:T(8,128)(2,1)S(1)} %pad_maximum_fusion.2), channel_id=1, source_target_pairs={{0,64},{16,80},{32,96},{48,112},{64,0},{80,16},{96,32},{112,48},{1... | collective-permute-start | bytes 393224 | tf_op jit(solution)/shard_map/ppermute | solution.py:392
  85.9 2.1 %collective-permute-start.5 = (bf16[512,128]{1,0:T(8,128)(2,1)S(1)}, bf16[512,128]{1,0:T(8,128)(2,1)S(1)}, u32[]{:S(2)}, u32[]{:S(2)}) collective-permute-start(bf16[512,128]{1,0:T(8,128)(2,1)S(1)} %pad_maximum_fusion.2), channel_id=1, source_target_pairs={{0,32},{16,48},{32,64},{48,80},{64,96},{80,112},{96,0},{112,16},{1... | collective-permute-start | bytes 393224 | tf_op jit(solution)/shard_map/ppermute | solution.py:392
  88.0 2.2 %collective-permute-done.6 = bf16[512,128]{1,0:T(8,128)(2,1)S(1)} collective-permute-done((bf16[512,128]{1,0:T(8,128)(2,1)S(1)}, bf16[512,128]{1,0:T(8,128)(2,1)S(1)}, u32[]{:S(2)}, u32[]{:S(2)}) %collective-permute-start.6) | collective-permute-done | bytes 131104 | tf_op jit(solution)/shard_map/ppermute | solution.py:392
  90.9 5.0 %all-to-all-done.1.own_ref = bf16[16,128,128]{2,1,0:T(8,128)(2,1)S(1)} async-done(((bf16[16,128,128]{2,1,0:T(8,128)(2,1)}), bf16[16,128,128]{2,1,0:T(8,128)(2,1)S(1)}, u32[]{:S(2)}, u32[]{:S(2)}) %all-to-all-start.1) | async-done | bytes 524320 | tf_op jit(solution)/shard_map/all_to_all | solution.py:395
  96.3 12.1 %collective-permute-done.8.other_ref = bf16[16,128,128]{2,1,0:T(8,128)(2,1)S(1)} collective-permute-done((bf16[16,128,128]{2,1,0:T(8,128)(2,1)S(1)}, bf16[16,128,128]{2,1,0:T(8,128)(2,1)S(1)}, u32[]{:S(2)}, u32[]{:S(2)}) %collective-permute-start.8) | collective-permute-done | bytes 524320 | tf_op jit(solution)/shard_map/ppermute | solution.py:398
  108.4 2.6 %shard_map.142 = f32[256,2,256]{2,1,0:T(2,128)} custom-call(f32[2,16]{1,0:T(2,128)S(1)} %bitcast.15, s32[2,16]{1,0:T(2,128)S(1)} %bitcast.16, f32[16,32]{1,0:T(8,128)S(1)} %copy-done.5, s32[16,32]{1,0:T(8,128)S(1)} %copy-done.6, bf16[16,128,128]{2,1,0:T(8,128)(2,1)S(1)} %all-to-all-done.1.own_ref, ...), custom_call_target="tpu_custom_call" | custom-call | flops 600000000 | bytes 4000000 | tf_op jit(solution)/shard_map/pallas_call | solution.py:326
  (33 shorter events, 4.4 us)
Async XLA Ops:
  0.0 13.6 %collective-permute-start = (bf16[1,2,4,27648]{3,2,1,0:T(4,128)(2,1)}, bf16[1,2,4,27648]{3,2,1,0:T(4,128)(2,1)S(1)}, u32[]{:S(2)}, u32[]{:S(2)}) collective-permute-start(bf16[1,2,4,27648]{3,2,1,0:T(4,128)(2,1)} %param.14), channel_id=1, source_target_pairs={{0,64},{16,80},{32,96},{48,112},{64,128},{80,144},{96,160},{112,17... | collective-permute-start | bytes 1327112 | tf_op jit(solution)/shard_map/ppermute | solution.py:369
  2.1 3.0 %copy-start = (bf16[1,3,9216,128]{3,2,1,0:T(8,128)(2,1)S(1)}, bf16[1,3,9216,128]{3,2,1,0:T(8,128)(2,1)}, u32[]{:S(2)}) copy-start(bf16[1,3,9216,128]{3,2,1,0:T(8,128)(2,1)} %cond_ref.1) | copy-start | bytes 21233668
  5.1 0.8 copy-start.3
  5.9 7.7 %copy-start.4 = (bf16[128,256]{1,0:T(8,128)(2,1)S(1)}, bf16[128,256]{1,0:T(8,128)(2,1)}, u32[]{:S(2)}) copy-start(bf16[128,256]{1,0:T(8,128)(2,1)} %constant.10.clone.table_ref) | copy-start | bytes 196612
  13.6 10.0 %copy-start.1 = (bf16[16,16,32]{2,1,0:T(8,128)(2,1)S(1)}, bf16[16,16,32]{2,1,0:T(8,128)(2,1)}, u32[]{:S(2)}) copy-start(bf16[16,16,32]{2,1,0:T(8,128)(2,1)} %constant.11.clone.xt_ref) | copy-start | bytes 49156
  13.6 10.1 %copy-start.2 = (s32[4096]{0:T(1024)S(1)}, s32[4096]{0:T(1024)}, u32[]{:S(2)}) copy-start(s32[4096]{0:T(1024)} %param.21) | copy-start | bytes 49156
  13.6 10.1 %copy-start.7 = (s32[16]{0:T(128)S(1)}, s32[16]{0:T(128)}, u32[]{:S(2)}) copy-start(s32[16]{0:T(128)} %umklapp_ref.7) | copy-start | bytes 196
  23.6 84.8 %copy-start.5 = (f32[16,32]{1,0:T(8,128)S(1)}, f32[16,32]{1,0:T(8,128)}, u32[]{:S(2)}) copy-start(f32[16,32]{1,0:T(8,128)} %e_cond_ref.1) | copy-start | bytes 6148
  23.6 84.7 %copy-start.6 = (s32[16,32]{1,0:T(8,128)S(1)}, s32[16,32]{1,0:T(8,128)}, u32[]{:S(2)}) copy-start(s32[16,32]{1,0:T(8,128)} %occ_cond_ref.1) | copy-start | bytes 6148
  23.6 84.7 %copy-start.8 = (f32[16,2]{0,1:T(2,128)S(1)}, f32[16,2]{0,1:T(2,128)}, u32[]{:S(2)}) copy-start(f32[16,2]{0,1:T(2,128)} %param.16) | copy-start | bytes 388
  23.7 84.7 %copy-start.9 = (s32[16,2]{0,1:T(2,128)S(1)}, s32[16,2]{0,1:T(2,128)}, u32[]{:S(2)}) copy-start(s32[16,2]{0,1:T(2,128)} %param.18) | copy-start | bytes 388
  25.9 9.3 %collective-permute-start.1 = (bf16[1024,128]{1,0:T(8,128)(2,1)S(1)}, bf16[1024,128]{1,0:T(8,128)(2,1)S(1)}, u32[]{:S(2)}, u32[]{:S(2)}) collective-permute-start(bf16[1024,128]{1,0:T(8,128)(2,1)S(1)} %shard_map.138), channel_id=1, source_target_pairs={{0,8},{1,9},{2,10},{3,11},{4,12},{5,13},{6,14},{7,15},{8,0},{9,1},... | collective-permute-start | bytes 786440 | tf_op jit(solution)/shard_map/ppermute | solution.py:378
  29.0 9.8 %collective-permute-start.2 = (bf16[1024,128]{1,0:T(8,128)(2,1)S(1)}, bf16[1024,128]{1,0:T(8,128)(2,1)S(1)}, u32[]{:S(2)}, u32[]{:S(2)}) collective-permute-start(bf16[1024,128]{1,0:T(8,128)(2,1)S(1)} %shard_map.139), channel_id=1, source_target_pairs={{0,8},{1,9},{2,10},{3,11},{4,12},{5,13},{6,14},{7,15},{8,0},{9,1},... | collective-permute-start | bytes 786440 | tf_op jit(solution)/shard_map/ppermute | solution.py:378
  61.9 6.0 %collective-permute-start.4 = (bf16[256,128]{1,0:T(8,128)(2,1)S(1)}, bf16[256,128]{1,0:T(8,128)(2,1)S(1)}, u32[]{:S(2)}, u32[]{:S(2)}) collective-permute-start(bf16[256,128]{1,0:T(8,128)(2,1)S(1)} %bitcast.18), channel_id=1, source_target_pairs={{0,128},{16,144},{32,160},{48,176},{64,192},{80,208},{96,224},{112... | collective-permute-start | bytes 196616 | tf_op jit(solution)/shard_map/ppermute | solution.py:388
  63.4 10.7 %collective-permute-start.3 = (bf16[256,128]{1,0:T(8,128)(2,1)S(1)}, bf16[256,128]{1,0:T(8,128)(2,1)S(1)}, u32[]{:S(2)}, u32[]{:S(2)}) collective-permute-start(bf16[256,128]{1,0:T(8,128)(2,1)S(1)} %bitcast.19), channel_id=1, source_target_pairs={{0,0},{1,16},{2,32},{3,48},{4,64},{5,80},{6,96},{7,112},{8,128},{9... | collective-permute-start | bytes 196616 | tf_op jit(solution)/shard_map/ppermute | solution.py:387
  75.0 21.0 %all-to-all-start.1 = ((bf16[16,128,128]{2,1,0:T(8,128)(2,1)}), bf16[16,128,128]{2,1,0:T(8,128)(2,1)S(1)}, u32[]{:S(2)}, u32[]{:S(2)}) async-start(bf16[16,128,128]{2,1,0:T(8,128)(2,1)} %bitcast.8), calls=%async_computation.1 | async-start | bytes 1048576 | tf_op jit(solution)/shard_map/all_to_all | solution.py:395
  80.5 7.5 %collective-permute-start.7 = (bf16[512,128]{1,0:T(8,128)(2,1)S(1)}, bf16[512,128]{1,0:T(8,128)(2,1)S(1)}, u32[]{:S(2)}, u32[]{:S(2)}) collective-permute-start(bf16[512,128]{1,0:T(8,128)(2,1)S(1)} %pad_maximum_fusion.2), channel_id=1, source_target_pairs={{0,96},{16,112},{32,0},{48,16},{64,32},{80,48},{96,64},{112,80},{1... | collective-permute-start | bytes 393224 | tf_op jit(solution)/shard_map/ppermute | solution.py:392
  81.1 9.2 %collective-permute-start.6 = (bf16[512,128]{1,0:T(8,128)(2,1)S(1)}, bf16[512,128]{1,0:T(8,128)(2,1)S(1)}, u32[]{:S(2)}, u32[]{:S(2)}) collective-permute-start(bf16[512,128]{1,0:T(8,128)(2,1)S(1)} %pad_maximum_fusion.2), channel_id=1, source_target_pairs={{0,64},{16,80},{32,96},{48,112},{64,0},{80,16},{96,32},{112,48},{1... | collective-permute-start | bytes 393224 | tf_op jit(solution)/shard_map/ppermute | solution.py:392
  85.9 5.0 %collective-permute-start.5 = (bf16[512,128]{1,0:T(8,128)(2,1)S(1)}, bf16[512,128]{1,0:T(8,128)(2,1)S(1)}, u32[]{:S(2)}, u32[]{:S(2)}) collective-permute-start(bf16[512,128]{1,0:T(8,128)(2,1)S(1)} %pad_maximum_fusion.2), channel_id=1, source_target_pairs={{0,32},{16,48},{32,64},{48,80},{64,96},{80,112},{96,0},{112,16},{1... | collective-permute-start | bytes 393224 | tf_op jit(solution)/shard_map/ppermute | solution.py:392
  95.9 12.4 %collective-permute-start.8 = (bf16[16,128,128]{2,1,0:T(8,128)(2,1)S(1)}, bf16[16,128,128]{2,1,0:T(8,128)(2,1)S(1)}, u32[]{:S(2)}, u32[]{:S(2)}) collective-permute-start(bf16[16,128,128]{2,1,0:T(8,128)(2,1)S(1)} %all-to-all-done.1.own_ref), channel_id=1, source_target_pairs={{0,8},{1,9},{2,10},{3,11},{4,12},{5,13},{6,14},{7,15},{8,0},{9,1},... | collective-permute-start | bytes 1572872 | tf_op jit(solution)/shard_map/ppermute | solution.py:398
  96.3 12.1 %collective-permute-start.9 = (bf16[2048,128]{1,0:T(8,128)(2,1)S(1)}, bf16[2048,128]{1,0:T(8,128)(2,1)S(1)}, u32[]{:S(2)}, u32[]{:S(2)}) collective-permute-start(bf16[2048,128]{1,0:T(8,128)(2,1)S(1)} %pad_maximum_fusion.1.near_ref), channel_id=1, source_target_pairs={{0,16},{16,0},{32,48},{48,32},{64,80},{80,64},{96,112},{112,96},{1... | collective-permute-start | bytes 1572872 | tf_op jit(solution)/shard_map/ppermute | solution.py:399

commit v7 on v6

--- a/solution.py
+++ b/solution.py
@@ -103,11 +103,13 @@
     steps = GRID // YCHUNK
     ty = table_ref[:64, : 2 * GRID]
     tz = table_ref[64:112, : 2 * GRID]
-    vs = table_ref[112:120, :]
+    vs = table_ref[112:128, :]
 
     def pairs(slot):
         val = jnp.concatenate(
-            [val_ref[v].astype(jnp.float32) for v in range(NV)], axis=0
+            [val_ref[v].astype(jnp.float32) for v in range(NV)]
+            + [jnp.zeros((8, points), jnp.float32)],
+            axis=0,
         ).astype(jnp.bfloat16)
         spread = lax.dot_general(
             val, vs, (((0,), (0,)), ((), ())), preferred_element_type=jnp.float32

time: 111 us -> 111 us (level)
  no operation moved by 1% of the time
where the time goes in v7:
time: 111 us
  waiting for transfers between devices  35.3 us (32%)
  Pallas kernels  26.4 us (24%)
  blocking collectives  22.9 us (21%)
  starting transfers between devices  21.1 us (19%)
  local copies, waits for them, and re-layouts  4.78 us (4%)
    all_to_all x1, blocking collectives, shards(): spread = lax.all_to_all(share.reshape(16, HALF, 128), 'fft', 0, 0)  22.9 us
    ppermute x1, waiting for transfers between devices, shards(): other = lax.ppermute(mine, 'fft', swap)  12.1 us
    pallas_call x1, Pallas kernels, fields(): pl.pallas_call(field_kernel, grid=(planes, chunks), in_specs=[pl.BlockSpe...  9.97 us
    pallas_call x4, Pallas kernels, pick(): pl.pallas_call(functools.partial(pick_kernel, first, away), in_specs=[pl....  8.88 us
    ppermute x3, starting transfers between devices, shards(): lax.ppermute(block, 'ka', ka_route(lambda y, x, c, s=s: (y, x + s, c)))  7.51 us
    ppermute x1, waiting for transfers between devices, shards(): own = lax.ppermute(rho, ('ka', 'fft'), mesh_route(lambda k, f: (f, k)))  6.15 us
    all_to_all x1, starting transfers between devices, shards(): mine = lax.all_to_all(copies.reshape(16, HALF, 128), 'fft', 0, 0)  5.59 us
    pallas_call x1, Pallas kernels, spread_cond(): pl.pallas_call(spread_kernel, grid=(planes, 3), in_specs=[pl.BlockSpec((1...  4.98 us
  transfers between devices with their start and end apart: 11, of which 9 were waited for; matrix products, arithmetic and copies ran while one was open for 0% of the time, Pallas kernels for 10%

profile of v7, /device:TPU:62, one launch (start us, length us, event | category | flops | bytes accessed | tf_op | source)
XLA Modules:
  0.0 110.9 jit_solution(695892689423214849)
XLA Ops:
  0.0 2.1 %collective-permute-start = (bf16[1,2,4,27648]{3,2,1,0:T(4,128)(2,1)}, bf16[1,2,4,27648]{3,2,1,0:T(4,128)(2,1)S(1)}, u32[]{:S(2)}, u32[]{:S(2)}) collective-permute-start(bf16[1,2,4,27648]{3,2,1,0:T(4,128)(2,1)} %param.14), channel_id=1, source_target_pairs={{0,64},{16,80},{32,96},{48,112},{64,128},{80,144},{96,160},{112,17... | collective-permute-start | bytes 1327112 | tf_op jit(solution)/shard_map/ppermute | solution.py:371
  2.1 3.0 %copy-done = bf16[1,3,9216,128]{3,2,1,0:T(8,128)(2,1)S(1)} copy-done((bf16[1,3,9216,128]{3,2,1,0:T(8,128)(2,1)S(1)}, bf16[1,3,9216,128]{3,2,1,0:T(8,128)(2,1)}, u32[]{:S(2)}) %copy-start) | copy-done | bytes 7077912
  5.9 5.0 %shard_map.136.cond_ref = bf16[3,9216,256]{2,1,0:T(8,128)(2,1)S(1)} custom-call(bf16[1,3,9216,128]{3,2,1,0:T(8,128)(2,1)S(1)} %copy-done, bf16[128,256]{1,0:T(8,128)(2,1)S(1)} %copy-done.3), custom_call_target="tpu_custom_call" | custom-call | flops 2000000000 | bytes 20000000 | tf_op jit(solution)/shard_map/pallas_call | solution.py:85
  10.9 2.7 %collective-permute-done = bf16[1,2,4,27648]{3,2,1,0:T(4,128)(2,1)S(1)} collective-permute-done((bf16[1,2,4,27648]{3,2,1,0:T(4,128)(2,1)}, bf16[1,2,4,27648]{3,2,1,0:T(4,128)(2,1)S(1)}, u32[]{:S(2)}, u32[]{:S(2)}) %collective-permute-start) | collective-permute-done | bytes 442400 | tf_op jit(solution)/shard_map/ppermute | solution.py:371
  13.6 10.0 %shard_map.137.refs_0_ = bf16[3,256,768]{2,1,0:T(8,128)(2,1)S(1)} custom-call(bf16[2,4,27648]{2,1,0:T(4,128)(2,1)S(1)} %bitcast.10, bf16[3,9216,256]{2,1,0:T(8,128)(2,1)S(1)} %shard_map.136.cond_ref, bf16[128,256]{1,0:T(8,128)(2,1)S(1)} %copy-done.4), custom_call_target="tpu_custom_call" | custom-call | flops 2000000000 | bytes 3000000 | tf_op jit(solution)/shard_map/pallas_call | solution.py:184
  23.7 2.2 %shard_map.138 = bf16[1024,128]{1,0:T(8,128)(2,1)S(1)} custom-call(s32[16]{0:T(128)S(1)} %copy-done.7, s32[32,128]{1,0:T(8,128)S(1)} %bitcast.11, bf16[16,16,32]{2,1,0:T(8,128)(2,1)S(1)} %copy-done.1, bf16[3,256,768]{2,1,0:T(8,128)(2,1)S(1)} %shard_map.137.refs_0_), custom_call_target="tpu_custom_call" | custom-call | flops 100000000 | bytes 500000 | tf_op jit(solution)/shard_map/pallas_call | solution.py:267
  26.8 2.2 %shard_map.139 = bf16[1024,128]{1,0:T(8,128)(2,1)S(1)} custom-call(s32[16]{0:T(128)S(1)} %copy-done.7, s32[32,128]{1,0:T(8,128)S(1)} %bitcast.12, bf16[16,16,32]{2,1,0:T(8,128)(2,1)S(1)} %copy-done.1, bf16[3,256,768]{2,1,0:T(8,128)(2,1)S(1)} %shard_map.137.refs_0_), custom_call_target="tpu_custom_call" | custom-call | flops 100000000 | bytes 500000 | tf_op jit(solution)/shard_map/pallas_call | solution.py:267
  29.0 1.4 %collective-permute-start.2 = (bf16[1024,128]{1,0:T(8,128)(2,1)S(1)}, bf16[1024,128]{1,0:T(8,128)(2,1)S(1)}, u32[]{:S(2)}, u32[]{:S(2)}) collective-permute-start(bf16[1024,128]{1,0:T(8,128)(2,1)S(1)} %shard_map.139), channel_id=1, source_target_pairs={{0,8},{1,9},{2,10},{3,11},{4,12},{5,13},{6,14},{7,15},{8,0},{9,1},... | collective-permute-start | bytes 786440 | tf_op jit(solution)/shard_map/ppermute | solution.py:380
  30.3 2.2 %shard_map.140 = bf16[1024,128]{1,0:T(8,128)(2,1)S(1)} custom-call(s32[16]{0:T(128)S(1)} %copy-done.7, s32[32,128]{1,0:T(8,128)S(1)} %bitcast.13, bf16[16,16,32]{2,1,0:T(8,128)(2,1)S(1)} %copy-done.1, bf16[3,256,768]{2,1,0:T(8,128)(2,1)S(1)} %shard_map.137.refs_0_), custom_call_target="tpu_custom_call" | custom-call | flops 100000000 | bytes 500000 | tf_op jit(solution)/shard_map/pallas_call | solution.py:267
  32.6 2.7 %collective-permute-done.1 = bf16[1024,128]{1,0:T(8,128)(2,1)S(1)} collective-permute-done((bf16[1024,128]{1,0:T(8,128)(2,1)S(1)}, bf16[1024,128]{1,0:T(8,128)(2,1)S(1)}, u32[]{:S(2)}, u32[]{:S(2)}) %collective-permute-start.1) | collective-permute-done | bytes 262176 | tf_op jit(solution)/shard_map/ppermute | solution.py:380
  35.3 2.2 %shard_map.141 = bf16[1024,128]{1,0:T(8,128)(2,1)S(1)} custom-call(s32[16]{0:T(128)S(1)} %copy-done.7, s32[32,128]{1,0:T(8,128)S(1)} %bitcast.14, bf16[16,16,32]{2,1,0:T(8,128)(2,1)S(1)} %copy-done.1, bf16[3,256,768]{2,1,0:T(8,128)(2,1)S(1)} %shard_map.137.refs_0_), custom_call_target="tpu_custom_call" | custom-call | flops 100000000 | bytes 500000 | tf_op jit(solution)/shard_map/pallas_call | solution.py:267
  37.6 1.2 %collective-permute-done.2 = bf16[1024,128]{1,0:T(8,128)(2,1)S(1)} collective-permute-done((bf16[1024,128]{1,0:T(8,128)(2,1)S(1)}, bf16[1024,128]{1,0:T(8,128)(2,1)S(1)}, u32[]{:S(2)}, u32[]{:S(2)}) %collective-permute-start.2) | collective-permute-done | bytes 262176 | tf_op jit(solution)/shard_map/ppermute | solution.py:380
  38.9 22.9 %all_to_all.10 = bf16[16,128,128]{2,1,0:T(8,128)(2,1)S(1)} all-to-all(bf16[16,128,128]{2,1,0:T(8,128)(2,1)S(1)} %bitcast.17), channel_id=1, replica_groups=mesh['ka'=16,'fft'=16] {'fft'}, dimensions={0} | all-to-all | bytes 1048576 | tf_op jit(solution)/shard_map/all_to_all | solution.py:386
  61.8 1.5 %collective-permute-start.4 = (bf16[256,128]{1,0:T(8,128)(2,1)S(1)}, bf16[256,128]{1,0:T(8,128)(2,1)S(1)}, u32[]{:S(2)}, u32[]{:S(2)}) collective-permute-start(bf16[256,128]{1,0:T(8,128)(2,1)S(1)} %bitcast.18), channel_id=1, source_target_pairs={{0,128},{16,144},{32,160},{48,176},{64,192},{80,208},{96,224},{112... | collective-permute-start | bytes 196616 | tf_op jit(solution)/shard_map/ppermute | solution.py:390
  63.4 1.9 %collective-permute-start.3 = (bf16[256,128]{1,0:T(8,128)(2,1)S(1)}, bf16[256,128]{1,0:T(8,128)(2,1)S(1)}, u32[]{:S(2)}, u32[]{:S(2)}) collective-permute-start(bf16[256,128]{1,0:T(8,128)(2,1)S(1)} %bitcast.19), channel_id=1, source_target_pairs={{0,0},{1,16},{2,32},{3,48},{4,64},{5,80},{6,96},{7,112},{8,128},{9... | collective-permute-start | bytes 196616 | tf_op jit(solution)/shard_map/ppermute | solution.py:389
  65.3 2.6 %collective-permute-done.4 = bf16[256,128]{1,0:T(8,128)(2,1)S(1)} collective-permute-done((bf16[256,128]{1,0:T(8,128)(2,1)S(1)}, bf16[256,128]{1,0:T(8,128)(2,1)S(1)}, u32[]{:S(2)}, u32[]{:S(2)}) %collective-permute-start.4) | collective-permute-done | bytes 65568 | tf_op jit(solution)/shard_map/ppermute | solution.py:390
  67.9 6.2 %collective-permute-done.3 = bf16[256,128]{1,0:T(8,128)(2,1)S(1)} collective-permute-done((bf16[256,128]{1,0:T(8,128)(2,1)S(1)}, bf16[256,128]{1,0:T(8,128)(2,1)S(1)}, u32[]{:S(2)}, u32[]{:S(2)}) %collective-permute-start.3) | collective-permute-done | bytes 65568 | tf_op jit(solution)/shard_map/ppermute | solution.py:389
  74.9 5.6 %all-to-all-start.1 = ((bf16[16,128,128]{2,1,0:T(8,128)(2,1)}), bf16[16,128,128]{2,1,0:T(8,128)(2,1)S(1)}, u32[]{:S(2)}, u32[]{:S(2)}) async-start(bf16[16,128,128]{2,1,0:T(8,128)(2,1)} %bitcast.8), calls=%async_computation.1 | async-start | bytes 1048576 | tf_op jit(solution)/shard_map/all_to_all | solution.py:397
  81.1 4.9 %collective-permute-start.6 = (bf16[512,128]{1,0:T(8,128)(2,1)S(1)}, bf16[512,128]{1,0:T(8,128)(2,1)S(1)}, u32[]{:S(2)}, u32[]{:S(2)}) collective-permute-start(bf16[512,128]{1,0:T(8,128)(2,1)S(1)} %pad_maximum_fusion.2), channel_id=1, source_target_pairs={{0,64},{16,80},{32,96},{48,112},{64,0},{80,16},{96,32},{112,48},{1... | collective-permute-start | bytes 393224 | tf_op jit(solution)/shard_map/ppermute | solution.py:394
  85.9 2.1 %collective-permute-start.5 = (bf16[512,128]{1,0:T(8,128)(2,1)S(1)}, bf16[512,128]{1,0:T(8,128)(2,1)S(1)}, u32[]{:S(2)}, u32[]{:S(2)}) collective-permute-start(bf16[512,128]{1,0:T(8,128)(2,1)S(1)} %pad_maximum_fusion.2), channel_id=1, source_target_pairs={{0,32},{16,48},{32,64},{48,80},{64,96},{80,112},{96,0},{112,16},{1... | collective-permute-start | bytes 393224 | tf_op jit(solution)/shard_map/ppermute | solution.py:394
  88.0 2.2 %collective-permute-done.6 = bf16[512,128]{1,0:T(8,128)(2,1)S(1)} collective-permute-done((bf16[512,128]{1,0:T(8,128)(2,1)S(1)}, bf16[512,128]{1,0:T(8,128)(2,1)S(1)}, u32[]{:S(2)}, u32[]{:S(2)}) %collective-permute-start.6) | collective-permute-done | bytes 131104 | tf_op jit(solution)/shard_map/ppermute | solution.py:394
  90.9 4.9 %all-to-all-done.1.own_ref = bf16[16,128,128]{2,1,0:T(8,128)(2,1)S(1)} async-done(((bf16[16,128,128]{2,1,0:T(8,128)(2,1)}), bf16[16,128,128]{2,1,0:T(8,128)(2,1)S(1)}, u32[]{:S(2)}, u32[]{:S(2)}) %all-to-all-start.1) | async-done | bytes 524320 | tf_op jit(solution)/shard_map/all_to_all | solution.py:397
  96.2 12.1 %collective-permute-done.8.other_ref = bf16[16,128,128]{2,1,0:T(8,128)(2,1)S(1)} collective-permute-done((bf16[16,128,128]{2,1,0:T(8,128)(2,1)S(1)}, bf16[16,128,128]{2,1,0:T(8,128)(2,1)S(1)}, u32[]{:S(2)}, u32[]{:S(2)}) %collective-permute-start.8) | collective-permute-done | bytes 524320 | tf_op jit(solution)/shard_map/ppermute | solution.py:400
  108.4 2.6 %shard_map.142 = f32[256,2,256]{2,1,0:T(2,128)} custom-call(f32[2,16]{1,0:T(2,128)S(1)} %bitcast.15, s32[2,16]{1,0:T(2,128)S(1)} %bitcast.16, f32[16,32]{1,0:T(8,128)S(1)} %copy-done.5, s32[16,32]{1,0:T(8,128)S(1)} %copy-done.6, bf16[16,128,128]{2,1,0:T(8,128)(2,1)S(1)} %all-to-all-done.1.own_ref, ...), custom_call_target="tpu_custom_call" | custom-call | flops 600000000 | bytes 4000000 | tf_op jit(solution)/shard_map/pallas_call | solution.py:328
  (33 shorter events, 4.4 us)
Async XLA Ops:
  0.0 13.6 %collective-permute-start = (bf16[1,2,4,27648]{3,2,1,0:T(4,128)(2,1)}, bf16[1,2,4,27648]{3,2,1,0:T(4,128)(2,1)S(1)}, u32[]{:S(2)}, u32[]{:S(2)}) collective-permute-start(bf16[1,2,4,27648]{3,2,1,0:T(4,128)(2,1)} %param.14), channel_id=1, source_target_pairs={{0,64},{16,80},{32,96},{48,112},{64,128},{80,144},{96,160},{112,17... | collective-permute-start | bytes 1327112 | tf_op jit(solution)/shard_map/ppermute | solution.py:371
  2.1 3.0 %copy-start = (bf16[1,3,9216,128]{3,2,1,0:T(8,128)(2,1)S(1)}, bf16[1,3,9216,128]{3,2,1,0:T(8,128)(2,1)}, u32[]{:S(2)}) copy-start(bf16[1,3,9216,128]{3,2,1,0:T(8,128)(2,1)} %cond_ref.1) | copy-start | bytes 21233668
  5.1 0.8 copy-start.3
  5.9 7.7 %copy-start.4 = (bf16[128,256]{1,0:T(8,128)(2,1)S(1)}, bf16[128,256]{1,0:T(8,128)(2,1)}, u32[]{:S(2)}) copy-start(bf16[128,256]{1,0:T(8,128)(2,1)} %constant.10.clone.table_ref) | copy-start | bytes 196612
  13.6 10.0 %copy-start.1 = (bf16[16,16,32]{2,1,0:T(8,128)(2,1)S(1)}, bf16[16,16,32]{2,1,0:T(8,128)(2,1)}, u32[]{:S(2)}) copy-start(bf16[16,16,32]{2,1,0:T(8,128)(2,1)} %constant.11.clone.xt_ref) | copy-start | bytes 49156
  13.6 10.0 %copy-start.2 = (s32[4096]{0:T(1024)S(1)}, s32[4096]{0:T(1024)}, u32[]{:S(2)}) copy-start(s32[4096]{0:T(1024)} %param.21) | copy-start | bytes 49156
  13.6 10.1 %copy-start.7 = (s32[16]{0:T(128)S(1)}, s32[16]{0:T(128)}, u32[]{:S(2)}) copy-start(s32[16]{0:T(128)} %umklapp_ref.7) | copy-start | bytes 196
  23.6 84.7 %copy-start.5 = (f32[16,32]{1,0:T(8,128)S(1)}, f32[16,32]{1,0:T(8,128)}, u32[]{:S(2)}) copy-start(f32[16,32]{1,0:T(8,128)} %e_cond_ref.1) | copy-start | bytes 6148
  23.6 84.7 %copy-start.6 = (s32[16,32]{1,0:T(8,128)S(1)}, s32[16,32]{1,0:T(8,128)}, u32[]{:S(2)}) copy-start(s32[16,32]{1,0:T(8,128)} %occ_cond_ref.1) | copy-start | bytes 6148
  23.6 84.7 %copy-start.8 = (f32[16,2]{0,1:T(2,128)S(1)}, f32[16,2]{0,1:T(2,128)}, u32[]{:S(2)}) copy-start(f32[16,2]{0,1:T(2,128)} %param.16) | copy-start | bytes 388
  23.7 84.7 %copy-start.9 = (s32[16,2]{0,1:T(2,128)S(1)}, s32[16,2]{0,1:T(2,128)}, u32[]{:S(2)}) copy-start(s32[16,2]{0,1:T(2,128)} %param.18) | copy-start | bytes 388
  25.9 9.3 %collective-permute-start.1 = (bf16[1024,128]{1,0:T(8,128)(2,1)S(1)}, bf16[1024,128]{1,0:T(8,128)(2,1)S(1)}, u32[]{:S(2)}, u32[]{:S(2)}) collective-permute-start(bf16[1024,128]{1,0:T(8,128)(2,1)S(1)} %shard_map.138), channel_id=1, source_target_pairs={{0,8},{1,9},{2,10},{3,11},{4,12},{5,13},{6,14},{7,15},{8,0},{9,1},... | collective-permute-start | bytes 786440 | tf_op jit(solution)/shard_map/ppermute | solution.py:380
  29.0 9.8 %collective-permute-start.2 = (bf16[1024,128]{1,0:T(8,128)(2,1)S(1)}, bf16[1024,128]{1,0:T(8,128)(2,1)S(1)}, u32[]{:S(2)}, u32[]{:S(2)}) collective-permute-start(bf16[1024,128]{1,0:T(8,128)(2,1)S(1)} %shard_map.139), channel_id=1, source_target_pairs={{0,8},{1,9},{2,10},{3,11},{4,12},{5,13},{6,14},{7,15},{8,0},{9,1},... | collective-permute-start | bytes 786440 | tf_op jit(solution)/shard_map/ppermute | solution.py:380
  61.8 6.0 %collective-permute-start.4 = (bf16[256,128]{1,0:T(8,128)(2,1)S(1)}, bf16[256,128]{1,0:T(8,128)(2,1)S(1)}, u32[]{:S(2)}, u32[]{:S(2)}) collective-permute-start(bf16[256,128]{1,0:T(8,128)(2,1)S(1)} %bitcast.18), channel_id=1, source_target_pairs={{0,128},{16,144},{32,160},{48,176},{64,192},{80,208},{96,224},{112... | collective-permute-start | bytes 196616 | tf_op jit(solution)/shard_map/ppermute | solution.py:390
  63.4 10.7 %collective-permute-start.3 = (bf16[256,128]{1,0:T(8,128)(2,1)S(1)}, bf16[256,128]{1,0:T(8,128)(2,1)S(1)}, u32[]{:S(2)}, u32[]{:S(2)}) collective-permute-start(bf16[256,128]{1,0:T(8,128)(2,1)S(1)} %bitcast.19), channel_id=1, source_target_pairs={{0,0},{1,16},{2,32},{3,48},{4,64},{5,80},{6,96},{7,112},{8,128},{9... | collective-permute-start | bytes 196616 | tf_op jit(solution)/shard_map/ppermute | solution.py:389
  74.9 20.9 %all-to-all-start.1 = ((bf16[16,128,128]{2,1,0:T(8,128)(2,1)}), bf16[16,128,128]{2,1,0:T(8,128)(2,1)S(1)}, u32[]{:S(2)}, u32[]{:S(2)}) async-start(bf16[16,128,128]{2,1,0:T(8,128)(2,1)} %bitcast.8), calls=%async_computation.1 | async-start | bytes 1048576 | tf_op jit(solution)/shard_map/all_to_all | solution.py:397
  80.5 7.5 %collective-permute-start.7 = (bf16[512,128]{1,0:T(8,128)(2,1)S(1)}, bf16[512,128]{1,0:T(8,128)(2,1)S(1)}, u32[]{:S(2)}, u32[]{:S(2)}) collective-permute-start(bf16[512,128]{1,0:T(8,128)(2,1)S(1)} %pad_maximum_fusion.2), channel_id=1, source_target_pairs={{0,96},{16,112},{32,0},{48,16},{64,32},{80,48},{96,64},{112,80},{1... | collective-permute-start | bytes 393224 | tf_op jit(solution)/shard_map/ppermute | solution.py:394
  81.1 9.2 %collective-permute-start.6 = (bf16[512,128]{1,0:T(8,128)(2,1)S(1)}, bf16[512,128]{1,0:T(8,128)(2,1)S(1)}, u32[]{:S(2)}, u32[]{:S(2)}) collective-permute-start(bf16[512,128]{1,0:T(8,128)(2,1)S(1)} %pad_maximum_fusion.2), channel_id=1, source_target_pairs={{0,64},{16,80},{32,96},{48,112},{64,0},{80,16},{96,32},{112,48},{1... | collective-permute-start | bytes 393224 | tf_op jit(solution)/shard_map/ppermute | solution.py:394
  85.9 5.0 %collective-permute-start.5 = (bf16[512,128]{1,0:T(8,128)(2,1)S(1)}, bf16[512,128]{1,0:T(8,128)(2,1)S(1)}, u32[]{:S(2)}, u32[]{:S(2)}) collective-permute-start(bf16[512,128]{1,0:T(8,128)(2,1)S(1)} %pad_maximum_fusion.2), channel_id=1, source_target_pairs={{0,32},{16,48},{32,64},{48,80},{64,96},{80,112},{96,0},{112,16},{1... | collective-permute-start | bytes 393224 | tf_op jit(solution)/shard_map/ppermute | solution.py:394
  95.9 12.4 %collective-permute-start.8 = (bf16[16,128,128]{2,1,0:T(8,128)(2,1)S(1)}, bf16[16,128,128]{2,1,0:T(8,128)(2,1)S(1)}, u32[]{:S(2)}, u32[]{:S(2)}) collective-permute-start(bf16[16,128,128]{2,1,0:T(8,128)(2,1)S(1)} %all-to-all-done.1.own_ref), channel_id=1, source_target_pairs={{0,8},{1,9},{2,10},{3,11},{4,12},{5,13},{6,14},{7,15},{8,0},{9,1},... | collective-permute-start | bytes 1572872 | tf_op jit(solution)/shard_map/ppermute | solution.py:400
  96.2 12.2 %collective-permute-start.9 = (bf16[2048,128]{1,0:T(8,128)(2,1)S(1)}, bf16[2048,128]{1,0:T(8,128)(2,1)S(1)}, u32[]{:S(2)}, u32[]{:S(2)}) collective-permute-start(bf16[2048,128]{1,0:T(8,128)(2,1)S(1)} %pad_maximum_fusion.1.near_ref), channel_id=1, source_target_pairs={{0,16},{16,0},{32,48},{48,32},{64,80},{80,64},{96,112},{112,96},{1... | collective-permute-start | bytes 1572872 | tf_op jit(solution)/shard_map/ppermute | solution.py:401
